TPU v7x, 256 devices: a whole 4x4x8 slice. The times are simulated.
256 devices in a mesh: gz: 64 (over x, z, core), gy: 4 (over y).
Axes of the slice: x: 4, y: 4, z: 8, core: 2. Of those that a mesh axis runs over, the one named last changes fastest.
Arguments:
- labels: int32 [256, 512, 512], P('gz', 'gy'), may hold values from 0 to 3
- phase_table: float32 [4], replicated, may hold values from 0.2 to 5
- collector_mask: int32 [2, 256, 512], P(None, 'gz', 'gy'), may hold values 0 or 1
- collector_value: float32 [2], replicated, may hold values from -1 to 1
- source: float32 [256, 512, 512], P('gz', 'gy'), may hold values from -6 to 6
Outputs:
- potential: float32 [256, 512, 512], P('gz', 'gy')
- residual: float32 [256, 512, 512], P('gz', 'gy')
All inputs are finite; a program needn't handle non-finite values. No bound on the sum of `collector_mask` on one device may be relied on, other than what follows from the above.
Results may differ from a plain program's by a relative error of at most 0.0003.
Values sent between devices are 32-bit elements; how exact they have to be, the bound alone decides.
No kernel may reach another device: no remote copies, remote signals or barrier semaphores. Data moves between devices by JAX's collectives and lax.ppermute only.
A program may use at most 64 MiB of HBM per device.

v0:
```python
import math

import jax
import jax.numpy as jnp
from jax import lax
from jax.sharding import PartitionSpec as P

ITERS = 2


HIGHEST = lax.Precision.HIGHEST
line_shift = 0.0016


def with_halo(shard, sides, width):
    for axis, dim in sides:
        devices, length = (lax.axis_size(axis), shard.shape[dim])
        up = [(i, (i + 1) % devices) for i in range(devices - 1)]
        down = [(j, i) for i, j in up]
        last = lax.slice_in_dim(shard, length - width, length, axis=dim)
        leading = lax.slice_in_dim(shard, 0, width, axis=dim)
        before = lax.ppermute(last, axis, up)
        after = lax.ppermute(leading, axis, down)
        shard = jnp.concatenate([before, shard, after], axis=dim)
    return shard


def harmonic(lower, upper):
    return 2.0 * lower * upper / (lower + upper)


def coefficients(padded):
    face_z = harmonic(padded[:-1, 1:-1, 1:-1], padded[1:, 1:-1, 1:-1])
    face_y = harmonic(padded[1:-1, :-1, 1:-1], padded[1:-1, 1:, 1:-1])
    face_x = harmonic(padded[1:-1, 1:-1, :-1], padded[1:-1, 1:-1, 1:])
    return (face_z, face_y, face_x)


def neighbours(padded, face_z, face_y, face_x):
    beside = face_z[:-1] * padded[:-2, 1:-1, 1:-1] + face_z[1:] * padded[2:, 1:-1, 1:-1]
    beside = (
        beside + face_y[:, :-1] * padded[1:-1, :-2, 1:-1] + face_y[:, 1:] * padded[1:-1, 2:, 1:-1]
    )
    beside = (
        beside
        + face_x[:, :, :-1] * padded[1:-1, 1:-1, :-2]
        + face_x[:, :, 1:] * padded[1:-1, 1:-1, 2:]
    )
    return beside


def basis_rows(rows, count):
    cols = jnp.arange(count).astype(rows.dtype)
    angle = jnp.pi * (rows[:, None] + 0.5) * cols[None, :] / count
    weight = jnp.where(cols == 0, math.sqrt(1.0 / count), math.sqrt(2.0 / count))
    return jnp.cos(angle) * weight[None, :]


def inverse_values(count, dtype):
    cols = jnp.arange(count).astype(dtype)
    return 1.0 / (line_shift + 2.0 - 2.0 * jnp.cos(jnp.pi * cols / count))


def with_rims(field):
    padded = with_halo(field, (("gz", 0), ("gy", 1)), 1)
    return jnp.pad(padded, ((0, 0), (0, 0), (1, 1)))


def residual_dot(residual, pre):
    return lax.psum(jnp.sum(residual * pre), ("gz", "gy"))


def local(labels, phase_table, collector_mask, collector_value, source):
    conductivity = jnp.zeros(labels.shape, jnp.float32)
    for phase in range(phase_table.shape[0]):
        conductivity = conductivity + jnp.where(labels == phase, phase_table[phase], 0.0)
    padded_rim = with_halo(conductivity, (("gz", 0), ("gy", 1)), 1)
    face_z, face_y, face_x = coefficients(jnp.pad(padded_rim, ((0, 0), (0, 0), (1, 1))))
    width = conductivity.shape[2]
    local_rows = conductivity.shape[1]
    total_rows = local_rows * lax.axis_size("gy")
    column = lax.broadcasted_iota(jnp.int32, conductivity.shape, 2)
    masks = collector_mask.astype(jnp.float32)
    low_edge = jnp.where(column == 0, 2.0 * conductivity * masks[0][:, :, None], 0.0)
    high_edge = jnp.where(column == width - 1, 2.0 * conductivity * masks[1][:, :, None], 0.0)
    diagonal = (
        face_z[:-1]
        + face_z[1:]
        + (face_y[:, :-1] + face_y[:, 1:])
        + (face_x[:, :, :-1] + face_x[:, :, 1:])
    )
    diagonal = diagonal + low_edge + high_edge
    right_side = source + low_edge * collector_value[0] + high_edge * collector_value[1]
    scale = lax.rsqrt(diagonal)
    inverse = inverse_values(total_rows, jnp.float32)
    basis = basis_rows(jnp.arange(total_rows).astype(jnp.float32), total_rows)

    def line_solve(lines):
        spectrum = (
            jnp.einsum("yj,zyx->zjx", basis, lines, precision=HIGHEST) * inverse[None, :, None]
        )
        result = jnp.einsum("yj,zjx->zyx", basis, spectrum, precision=HIGHEST)
        return lax.all_to_all(result, "gy", split_axis=1, concat_axis=2, tiled=True)

    def precondition(values):
        solved = line_solve(
            lax.all_to_all(values * scale, "gy", split_axis=2, concat_axis=1, tiled=True)
        )
        return scale * solved

    potential = jnp.zeros_like(source)
    residual = right_side
    pre = precondition(residual)
    direction = pre
    product = residual_dot(residual, pre)
    for iteration in range(ITERS):
        image = diagonal * direction - neighbours(with_rims(direction), face_z, face_y, face_x)
        curvature_sum = lax.psum(jnp.sum(direction * image), ("gz", "gy"))
        step_length = product / curvature_sum
        potential = potential + step_length * direction
        residual = residual - step_length * image
        if iteration + 1 < ITERS:
            pre = precondition(residual)
            product_next = residual_dot(residual, pre)
            direction = pre + product_next / product * direction
            product = product_next
    return (potential, residual)


def solution(mesh):
    return jax.shard_map(
        local,
        mesh=mesh,
        in_specs=(P("gz", "gy", None), P(), P(None, "gz", "gy"), P(), P("gz", "gy", None)),
        out_specs=(P("gz", "gy", None), P("gz", "gy", None)),
        check_vma=False,
    )
```

profile of v0, /device:TPU:1, one launch (start us, length us, event | category | flops | bytes accessed | tf_op | source)
XLA Modules:
  0.0 462.8 jit_solution(9160019207568913131)
XLA Ops:
  2.1 4.1 select_add_fusion
  6.3 4.9 %collective-permute-start = (f32[1,128,512]{2,1,0:T(8,128)S(1)}, f32[1,128,512]{2,1,0:T(8,128)S(1)}, u32[]{:S(2)}, u32[]{:S(2)}) collective-permute-start(f32[1,128,512]{2,1,0:T(8,128)S(1)} %get-tuple-element.28), channel_id=1, source_target_pairs={{0,4},{4,8},{8,12},{12,16},{16,20},{20,24},{24,28},{28,32},{32,36}... | collective-permute-start | bytes 786440 | tf_op jit(solution)/shard_map/ppermute | solution.py:22
  14.5 4.4 collective-permute-done.1
  18.9 3.2 collective-permute-start.2
  23.7 2.9 collective-permute-done.3
  29.9 6.3 %fusion.55 = (f32[4,128,512]{2,1,0:T(8,128)S(1)}, f32[4,128,512]{2,1,0:T(8,128)}, f32[4,128,512]{2,1,0:T(8,128)}) fusion(f32[]{:T(128)} %bitcast.7, f32[4,128]{1,0:T(4,128)S(1)} %get-tuple-element.31, pred[512]{0:T(512)(128)(4,1)S(1)} %get-tuple-element.38, f32[4,128,512]{2,1,0:T(8,128)S(1)} %copy-done.10, f32[]{:T(128)} %bitcast.5, ...), kind=kLoop, calls=%fused_computation.134 | loop fusion | flops 7077888 | bytes 11539480 | tf_op jit(solution)/shard_map/mul | solution.py:107
  37.5 4.3 all-to-all-start
  41.9 13.2 %all-to-all-done = f32[4,128,512]{1,0,2:T(4,128)S(1)} async-done(((f32[4,128,512]{1,0,2:T(4,128)}), f32[4,128,512]{1,0,2:T(4,128)S(1)}, u32[]{:S(2)}, u32[]{:S(2)}) %all-to-all-start) | async-done | bytes 1048608 | tf_op jit(solution)/shard_map/all_to_all | solution.py:107
  57.6 5.7 %fusion.2 = f32[4,512,128]{1,2,0:T(8,128)S(1)} fusion(f32[4,512,128]{2,1,0:T(8,128)S(1)} %bitcast.47, f32[512]{0:T(512)S(1)} %get-tuple-element.40, f32[512]{0:T(512)S(1)} %fusion.47, f32[512]{0:T(512)S(1)} %iota_convert_fusion, f32[512]{0:T(512)S(1)} %get-tuple-element.41), kind=kOutput, calls=%fused_computation.20 | convolution fusion | flops 1611661312 | bytes 2105344 | tf_op jit(solution)/shard_map/yj,zyx->zjx/dot_general | solution.py:100
  63.3 5.5 %convolution_bitcast_fusion.1 = f32[4,512,128]{1,2,0:T(8,128)S(1)} fusion(f32[4,512,128]{1,2,0:T(8,128)S(1)} %fusion.2, f32[512]{0:T(512)S(1)} %fusion.47, f32[512]{0:T(512)S(1)} %iota_convert_fusion, f32[512]{0:T(512)S(1)} %get-tuple-element.41), kind=kOutput, calls=%fused_computation.18 | convolution fusion | flops 1611399168 | bytes 2103296 | tf_op jit(solution)/shard_map/yj,zjx->zyx/dot_general | solution.py:102
  70.2 29.2 %all_to_all.72 = f32[4,512,128]{2,0,1:T(4,128)S(1)} all-to-all(f32[4,512,128]{2,0,1:T(4,128)} %copy.28), channel_id=1, replica_groups=mesh['gz'=64,'gy'=4] {'gy'}, dimensions={1} | all-to-all | bytes 2097152 | tf_op jit(solution)/shard_map/all_to_all | solution.py:103
  103.2 7.1 %collective-permute-start.4 = (f32[1,128,512]{2,1,0:T(8,128)S(1)}, f32[1,128,512]{2,1,0:T(8,128)S(1)}, u32[]{:S(2)}, u32[]{:S(2)}) collective-permute-start(f32[1,128,512]{2,1,0:T(8,128)S(1)} %get-tuple-element.26), channel_id=1, source_target_pairs={{0,4},{4,8},{8,12},{12,16},{16,20},{20,24},{24,28},{28,32},{32,36}... | collective-permute-start | bytes 786440 | tf_op jit(solution)/shard_map/ppermute | solution.py:22
  113.6 4.4 collective-permute-done.5
  121.8 3.1 collective-permute-done.7
  125.7 6.7 %multiply_reduce_fusion.2 = (f32[]{:T(128)}, f32[]{:T(128)}, f32[4,128,512]{2,1,0:T(8,128)}) fusion(f32[4,128,512]{2,1,0:T(8,128)S(1)} %mul.299, f32[4,128,512]{2,1,0:T(8,128)S(1)} %copy-done.7, f32[6,130,514]{2,1,0:T(8,128)S(1)} %select_maximum_fusion.4, f32[6,1,512]{2,1,0:T(1,128)S(1)} %collective-permute-done.7, ...), kind=kLoop, calls=%fused_computation.84 | loop fusion | flops 12320766 | bytes 13136920 | tf_op jit(solution)/shard_map/reduce_sum | solution.py:118
  132.4 77.4 %all-reduce.3 = (f32[]{:T(128)}, f32[]{:T(128)}) all-reduce(f32[]{:T(128)} %get-tuple-element.5, f32[]{:T(128)} %get-tuple-element.4), channel_id=1, replica_groups=mesh['gz'=64,'gy'=4] {'gz','gy'}, use_global_device_ids=true, to_apply=%region_1.2 | all-reduce | flops 2 | bytes 16 | tf_op jit(solution)/shard_map/psum | solution.py:70
  211.2 3.6 fusion.53
  214.8 2.5 copy.30
  217.4 17.5 %all_to_all.73 = f32[4,128,512]{1,0,2:T(4,128)S(1)} all-to-all(f32[4,128,512]{1,0,2:T(4,128)} %copy.30), channel_id=1, replica_groups=mesh['gz'=64,'gy'=4] {'gy'}, dimensions={2} | all-to-all | bytes 2097152 | tf_op jit(solution)/shard_map/all_to_all | solution.py:107
  235.9 2.5 copy.32
  238.4 6.9 %fusion.1 = f32[4,512,128]{1,2,0:T(8,128)S(1)} fusion(f32[4,512,128]{2,1,0:T(8,128)} %bitcast.48, f32[512]{0:T(512)S(1)} %get-tuple-element.40, f32[512]{0:T(512)S(1)} %fusion.47, f32[512]{0:T(512)S(1)} %iota_convert_fusion, f32[512]{0:T(512)S(1)} %get-tuple-element.41), kind=kOutput, calls=%fused_computation.17 | convolution fusion | flops 1611661312 | bytes 2105344 | tf_op jit(solution)/shard_map/yj,zyx->zjx/dot_general | solution.py:100
  245.3 6.6 %convolution_bitcast_fusion = f32[4,512,128]{1,2,0:T(8,128)} fusion(f32[4,512,128]{1,2,0:T(8,128)S(1)} %fusion.1, f32[512]{0:T(512)S(1)} %fusion.47, f32[512]{0:T(512)S(1)} %iota_convert_fusion, f32[512]{0:T(512)S(1)} %get-tuple-element.41), kind=kOutput, calls=%fused_computation.15 | convolution fusion | flops 1611399168 | bytes 2103296 | tf_op jit(solution)/shard_map/yj,zjx->zyx/dot_general | solution.py:102
  254.4 16.3 %all_to_all.74 = f32[4,512,128]{2,0,1:T(4,128)S(1)} all-to-all(f32[4,512,128]{2,0,1:T(4,128)} %copy.34), channel_id=1, replica_groups=mesh['gz'=64,'gy'=4] {'gy'}, dimensions={1} | all-to-all | bytes 2097152 | tf_op jit(solution)/shard_map/all_to_all | solution.py:103
  272.4 2.6 all_to_all.67
  275.0 3.7 multiply_reduce_fusion.1
  278.7 75.0 %psum.30 = f32[]{:T(128)} all-reduce(f32[]{:T(128)} %get-tuple-element.10), channel_id=1, replica_groups=mesh['gz'=64,'gy'=4] {'gz','gy'}, use_global_device_ids=true, to_apply=%region_5.6 | all-reduce | flops 1 | bytes 8 | tf_op jit(solution)/shard_map/psum | solution.py:70
  356.5 3.8 collective-permute-start.8
  363.6 4.4 collective-permute-done.9
  368.0 2.6 collective-permute-start.10
  372.0 3.1 collective-permute-done.11
  375.9 6.5 %multiply_reduce_fusion = (f32[]{:T(128)}, f32[4,128,512]{2,1,0:T(8,128)}) fusion(f32[4,128,512]{2,1,0:T(8,128)S(1)} %multiply_add_fusion.1, f32[6,130,514]{2,1,0:T(8,128)S(1)} %select_maximum_fusion, f32[6,1,512]{2,1,0:T(1,128)S(1)} %collective-permute-done.11, f32[1,128,512]{2,1,0:T(8,128)S(1)} %collective-permute-done.9, ...), kind=kLoop, calls=%fused_computation.80 | loop fusion | flops 11796479 | bytes 12088340 | tf_op jit(solution)/shard_map/reduce_sum | solution.py:118
  382.4 75.2 %psum.31 = f32[]{:T(128)} all-reduce(f32[]{:T(128)} %get-tuple-element.8), channel_id=1, replica_groups=mesh['gz'=64,'gy'=4] {'gz','gy'}, use_global_device_ids=true, to_apply=%region_7.8 | all-reduce | flops 1 | bytes 8 | tf_op jit(solution)/shard_map/psum | solution.py:118
  (72 shorter events, 42.3 us)
Async XLA Ops:
  0.6 12.5 %copy-start.12 = (f32[2]{0:T(128)S(1)}, f32[2]{0:T(128)}, u32[]{:S(2)}) copy-start(f32[2]{0:T(128)} %param.8) | copy-start | bytes 28
  0.6 13.2 %copy-start.11 = (s32[2,4,128]{2,1,0:T(4,128)S(1)}, s32[2,4,128]{2,1,0:T(4,128)}, u32[]{:S(2)}) copy-start(s32[2,4,128]{2,1,0:T(4,128)} %param.7) | copy-start | bytes 12292
  6.3 8.2 %collective-permute-start = (f32[1,128,512]{2,1,0:T(8,128)S(1)}, f32[1,128,512]{2,1,0:T(8,128)S(1)}, u32[]{:S(2)}, u32[]{:S(2)}) collective-permute-start(f32[1,128,512]{2,1,0:T(8,128)S(1)} %get-tuple-element.28), channel_id=1, source_target_pairs={{0,4},{4,8},{8,12},{12,16},{16,20},{20,24},{24,28},{28,32},{32,36}... | collective-permute-start | bytes 786440 | tf_op jit(solution)/shard_map/ppermute | solution.py:22
  11.2 7.7 %collective-permute-start.1 = (f32[1,128,512]{2,1,0:T(8,128)S(1)}, f32[1,128,512]{2,1,0:T(8,128)S(1)}, u32[]{:S(2)}, u32[]{:S(2)}) collective-permute-start(f32[1,128,512]{2,1,0:T(8,128)S(1)} %get-tuple-element.29), channel_id=1, source_target_pairs={{4,0},{8,4},{12,8},{16,12},{20,16},{24,20},{28,24},{32,28},{36,32}... | collective-permute-start | bytes 786440 | tf_op jit(solution)/shard_map/ppermute | solution.py:23
  18.9 4.7 %collective-permute-start.2 = (f32[6,1,512]{2,1,0:T(1,128)S(1)}, f32[6,1,512]{2,1,0:T(1,128)S(1)}, u32[]{:S(2)}, u32[]{:S(2)}) collective-permute-start(f32[6,1,512]{2,1,0:T(1,128)S(1)} %get-tuple-element.22), channel_id=1, source_target_pairs={{0,1},{1,2},{2,3},{4,5},{5,6},{6,7},{8,9},{9,10},{10,11},{12,13},{... | collective-permute-start | bytes 36872 | tf_op jit(solution)/shard_map/ppermute | solution.py:22
  22.1 4.4 collective-permute-start.3
  27.9 8.3 %copy-start = (f32[4,128,513]{2,1,0:T(8,128)}, f32[4,128,513]{2,1,0:T(8,128)S(1)}, u32[]{:S(2)}) copy-start(f32[4,128,513]{2,1,0:T(8,128)S(1)} %add_divide_fusion) | copy-start | bytes 3151876
  27.9 1.7 copy-start.4
  27.9 2.0 copy-start.10
  37.5 17.5 %all-to-all-start = ((f32[4,128,512]{1,0,2:T(4,128)}), f32[4,128,512]{1,0,2:T(4,128)S(1)}, u32[]{:S(2)}, u32[]{:S(2)}) async-start(f32[4,128,512]{1,0,2:T(4,128)} %copy.24), calls=%async_computation | async-start | bytes 2097152 | tf_op jit(solution)/shard_map/all_to_all | solution.py:107
  103.2 10.4 %collective-permute-start.4 = (f32[1,128,512]{2,1,0:T(8,128)S(1)}, f32[1,128,512]{2,1,0:T(8,128)S(1)}, u32[]{:S(2)}, u32[]{:S(2)}) collective-permute-start(f32[1,128,512]{2,1,0:T(8,128)S(1)} %get-tuple-element.26), channel_id=1, source_target_pairs={{0,4},{4,8},{8,12},{12,16},{16,20},{20,24},{24,28},{28,32},{32,36}... | collective-permute-start | bytes 786440 | tf_op jit(solution)/shard_map/ppermute | solution.py:22
  110.3 7.7 %collective-permute-start.5 = (f32[1,128,512]{2,1,0:T(8,128)S(1)}, f32[1,128,512]{2,1,0:T(8,128)S(1)}, u32[]{:S(2)}, u32[]{:S(2)}) collective-permute-start(f32[1,128,512]{2,1,0:T(8,128)S(1)} %get-tuple-element.27), channel_id=1, source_target_pairs={{4,0},{8,4},{12,8},{16,12},{20,16},{24,20},{28,24},{32,28},{36,32}... | collective-permute-start | bytes 786440 | tf_op jit(solution)/shard_map/ppermute | solution.py:23
  118.0 7.7 %copy-start.1 = (f32[4,128,513]{2,1,0:T(8,128)S(1)}, f32[4,128,513]{2,1,0:T(8,128)}, u32[]{:S(2)}) copy-start(f32[4,128,513]{2,1,0:T(8,128)} %copy-done) | copy-start | bytes 3151876
  118.0 7.7 %copy-start.5 = (s32[4,128,512]{2,1,0:T(8,128)S(1)}, s32[4,128,512]{2,1,0:T(8,128)}, u32[]{:S(2)}) copy-start(s32[4,128,512]{2,1,0:T(8,128)} %param.5) | copy-start | bytes 3145732
  118.0 7.7 %copy-start.7 = (f32[4,128,512]{2,1,0:T(8,128)S(1)}, f32[4,128,512]{2,1,0:T(8,128)}, u32[]{:S(2)}) copy-start(f32[4,128,512]{2,1,0:T(8,128)} %get-tuple-element.16) | copy-start | bytes 3145732
  118.1 3.8 collective-permute-start.6
  120.5 4.4 collective-permute-start.7
  356.4 19.4 %copy-start.3 = (f32[4,128,512]{2,1,0:T(8,128)}, f32[4,128,512]{2,1,0:T(8,128)S(1)}, u32[]{:S(2)}) copy-start(f32[4,128,512]{2,1,0:T(8,128)S(1)} %multiply_add_fusion.1) | copy-start | bytes 3145732
  356.5 7.1 %collective-permute-start.8 = (f32[1,128,512]{2,1,0:T(8,128)S(1)}, f32[1,128,512]{2,1,0:T(8,128)S(1)}, u32[]{:S(2)}, u32[]{:S(2)}) collective-permute-start(f32[1,128,512]{2,1,0:T(8,128)S(1)} %get-tuple-element.24), channel_id=1, source_target_pairs={{0,4},{4,8},{8,12},{12,16},{16,20},{20,24},{24,28},{28,32},{32,36}... | collective-permute-start | bytes 786440 | tf_op jit(solution)/shard_map/ppermute | solution.py:22
  360.3 7.7 %collective-permute-start.9 = (f32[1,128,512]{2,1,0:T(8,128)S(1)}, f32[1,128,512]{2,1,0:T(8,128)S(1)}, u32[]{:S(2)}, u32[]{:S(2)}) collective-permute-start(f32[1,128,512]{2,1,0:T(8,128)S(1)} %get-tuple-element.25), channel_id=1, source_target_pairs={{4,0},{8,4},{12,8},{16,12},{20,16},{24,20},{28,24},{32,28},{36,32}... | collective-permute-start | bytes 786440 | tf_op jit(solution)/shard_map/ppermute | solution.py:23
  368.0 7.9 %copy-start.2 = (f32[4,128,513]{2,1,0:T(8,128)S(1)}, f32[4,128,513]{2,1,0:T(8,128)}, u32[]{:S(2)}) copy-start(f32[4,128,513]{2,1,0:T(8,128)} %copy-done) | copy-start | bytes 3151876
  368.0 7.9 %copy-start.6 = (s32[4,128,512]{2,1,0:T(8,128)S(1)}, s32[4,128,512]{2,1,0:T(8,128)}, u32[]{:S(2)}) copy-start(s32[4,128,512]{2,1,0:T(8,128)} %param.5) | copy-start | bytes 3145732
  368.0 4.0 collective-permute-start.10
  370.7 4.4 collective-permute-start.11
  382.4 79.0 %copy-start.8 = (f32[4,128,512]{2,1,0:T(8,128)S(1)}, f32[4,128,512]{2,1,0:T(8,128)}, u32[]{:S(2)}) copy-start(f32[4,128,512]{2,1,0:T(8,128)} %get-tuple-element.13) | copy-start | bytes 3145732
  382.4 79.0 %copy-start.9 = (f32[4,128,512]{2,1,0:T(8,128)S(1)}, f32[4,128,512]{2,1,0:T(8,128)}, u32[]{:S(2)}) copy-start(f32[4,128,512]{2,1,0:T(8,128)} %get-tuple-element.9) | copy-start | bytes 3145732
where the time goes:
time: 468 us; the launch traced here: 463 us
  blocking collectives  291 us (62%)
  other arithmetic  41 us (9%)
  waiting for transfers between devices  39 us (8%)
  starting transfers between devices  38 us (8%)
  matrix products  24.7 us (5%)
  local copies, waits for them, and re-layouts  24.2 us (5%)
  between operations  5.29 us (1%)
    psum x2, blocking collectives, residual_dot(): return lax.psum(jnp.sum(residual * pre), ('gz', 'gy'))  152 us
    psum x1, blocking collectives, local(): curvature_sum = lax.psum(jnp.sum(direction * image), ('gz', 'gy'))  75.2 us
    all_to_all x2, blocking collectives, line_solve(): return lax.all_to_all(result, 'gy', split_axis=1, concat_axis=2, tiled=True)  45.4 us
    ppermute x6, starting transfers between devices, with_halo(): before = lax.ppermute(last, axis, up)  24.1 us
    ppermute x6, waiting for transfers between devices, with_halo(): after = lax.ppermute(leading, axis, down)  22.3 us
    all_to_all x1, blocking collectives, precondition(): lax.all_to_all(values * scale, 'gy', split_axis=2, concat_axis=1, tiled=T...  17.5 us
    all_to_all x1, waiting for transfers between devices, precondition(): lax.all_to_all(values * scale, 'gy', split_axis=2, concat_axis=1, tiled=T...  13.2 us
    reduce_sum x2, other arithmetic, local(): curvature_sum = lax.psum(jnp.sum(direction * image), ('gz', 'gy'))  13.2 us
  transfers between devices with their start and end apart: 13, of which 10 were waited for; matrix products, arithmetic and copies ran while one was open for 0% of the time, Pallas kernels for 0%

commit v1 on v0

v1 whole, which is shorter than its diff:
```python
import math

import jax
import jax.numpy as jnp
import ml_dtypes
import numpy as np
from jax import lax
from jax.experimental import pallas as pl
from jax.experimental.pallas import tpu as pltpu
from jax.sharding import PartitionSpec as P

F32 = jnp.float32
SHIFT = 0.0016
VMEM = pl.BlockSpec(memory_space=pltpu.VMEM)
SMEM = pl.BlockSpec(memory_space=pltpu.SMEM)
ALL = ("gz", "gy")


def line_tables(total, parts):
    rows = total // parts
    theta = math.acosh(1.0 + SHIFT / 2.0)
    near = np.cosh(theta * (np.arange(total) + 0.5))
    far = near[::-1]
    norm = math.sinh(theta) * math.sinh(total * theta)
    at = np.arange(total)
    green = np.where(at[:, None] <= at[None, :], near[:, None] * far[None, :], far[:, None] * near[None, :]) / norm
    blocks, vectors, scalars = [], [], np.zeros((parts, 8))
    for d in range(parts):
        own = slice(d * rows, (d + 1) * rows)
        low, high = math.cosh(theta * d * rows), math.cosh(theta * (d + 1) * rows)
        flow, fhigh = math.cosh(theta * (total - d * rows)), math.cosh(theta * (total - (d + 1) * rows))
        g = green[own, own].astype(np.float32)
        head = g.astype(ml_dtypes.bfloat16)
        tail = (g - head.astype(np.float32)).astype(ml_dtypes.bfloat16)
        blocks.append(np.concatenate([head, tail, head], axis=1))
        columns = [near[own] / high, far[own] / flow, low * far[own] / norm, fhigh * near[own] / norm]
        vectors.append(np.stack([np.broadcast_to(c[:, None], (rows, 128)) for c in columns]))
        for k in range(1, parts):
            if d >= k:
                scalars[d, k] = math.cosh(theta * (d - k + 1) * rows) / low
            else:
                scalars[d, 4 + k] = math.cosh(theta * (total - (d - k + parts) * rows)) / fhigh
    return np.stack(blocks), np.stack(vectors).astype(np.float32), scalars.astype(np.float32)


def call(body, outs, ins, scratch=()):
    return pl.pallas_call(
        body,
        out_shape=[jax.ShapeDtypeStruct(s, F32) for s in outs],
        in_specs=ins,
        out_specs=[VMEM] * len(outs),
        scratch_shapes=list(scratch),
        compiler_params=pltpu.CompilerParams(vmem_limit_bytes=24 * 2**20),
    )


def rows_of(c):
    return pl.ds(pl.multiple_of(c * 8, 8), 8)


def sublane(shape):
    return lax.broadcasted_iota(jnp.int32, shape, 0)


def lane(shape):
    return lax.broadcasted_iota(jnp.int32, shape, 1)


def recip(x):
    return 1.0 / x


def lookup(labels, table):
    low = jnp.where(labels == 1, table[1], table[0])
    high = jnp.where(labels == 3, table[3], table[2])
    return jnp.where(labels >= 2, high, low)


def wide(column, width):
    return jnp.concatenate([column] * (width // 128), axis=1)


def ends(value, low, high):
    return jnp.concatenate([value[:, :128] + low, value[:, 128:-128], value[:, -128:] + high], axis=1)


def local(labels, phase_table, collector_mask, collector_value, source):
    nz, ny, nx = labels.shape
    parts = lax.axis_size("gy")
    layers = lax.axis_size("gz")
    chunks = ny // 8
    block = (nz, ny, nx)
    plane = (1, ny, nx)
    edge = (nz, 8, nx)
    green, vectors, scalars = line_tables(ny * parts, parts)
    green, vectors, scalars = jnp.asarray(green), jnp.asarray(vectors), jnp.asarray(scalars)

    def ring(value, axis, size, step):
        return lax.ppermute(value, axis, [(i, (i + step) % size) for i in range(size)])

    table = 0.5 / phase_table
    zlo = ring(labels[-1:], "gz", layers, 1)
    zhi = ring(labels[:1], "gz", layers, -1)
    ylo = ring(labels[:, -1, :], "gy", parts, 1)
    yhi = ring(labels[:, 0, :], "gy", parts, -1)
    masks = collector_mask.astype(F32)[..., None]

    def faces(labels, table, values, masks, source, k_o, fx_o, fy_o, fz_o, d_o, e_o, b_o):
        for z in range(nz):
            def fill(c, _):
                k_o[z, rows_of(c), :] = lookup(labels[z, rows_of(c), :], table)
                return 0
            lax.fori_loop(0, chunks, fill, 0)
        sub = sublane((8, nx))
        for z in range(nz):
            def body(c, carry):
                at = rows_of(c)
                k = k_o[z, at, :]
                after = k_o[z, rows_of(jnp.minimum(c + 1, chunks - 1)), :]
                up = jnp.where(sub == 7, pltpu.roll(after, 7, 0), pltpu.roll(k, 7, 0))
                fy = jnp.where(sub + c * 8 == ny - 1, 0.0, recip(k + up))
                turned = pltpu.roll(fy, 1, 0)
                d = fy + jnp.where(sub == 0, carry, turned)
                fx = jnp.where(lane((8, nx)) == nx - 1, 0.0, recip(k + pltpu.roll(k, nx - 1, 1)))
                d = d + (fx + pltpu.roll(fx, 1, 1))
                if z > 0:
                    d = d + fz_o[z - 1, at, :]
                if z < nz - 1:
                    fz = recip(k + k_o[z + 1, at, :])
                    fz_o[z, at, :] = fz
                    d = d + fz
                side = lane((8, 128))
                low = jnp.where(side == 0, recip(k[:, :128]) * masks[0, z, at, :], 0.0)
                high = jnp.where(side == 127, recip(k[:, -128:]) * masks[1, z, at, :], 0.0)
                e_o[z, at, :] = jnp.concatenate([low, high], axis=1)
                d_o[z, at, :] = ends(d, low, high)
                b_o[z, at, :] = ends(source[z, at, :], low * values[0], high * values[1])
                fx_o[z, at, :] = fx
                fy_o[z, at, :] = fy
                return turned
            lax.fori_loop(0, chunks, body, jnp.zeros((8, nx), F32), unroll=True)

    k, fx, fy, fz, d, e, b = call(
        faces,
        [block, block, block, (nz - 1, ny, nx), block, (nz, ny, 256), block],
        [VMEM, SMEM, SMEM, VMEM, VMEM],
    )(labels, table, collector_value, masks, source)

    def payloads(my, sums, outs):
        for step, out in enumerate(outs, 1):
            for z in range(nz):
                out[z : z + 1, :] = jnp.where(my + step < parts, sums[z][0], sums[z][1])

    def scaled(table, k, ylo, yhi, zlo, zhi, d, b, vectors, s_o, x_o, fye_o, fze_o, one, two, three):
        my, level = lax.axis_index("gy"), lax.axis_index("gz")
        has_low, has_high = (my > 0).astype(F32), (my < parts - 1).astype(F32)
        has_below, has_above = (level > 0).astype(F32), (level < layers - 1).astype(F32)
        sub = sublane((8, nx))
        sums = []
        for z in range(nz):
            first = has_low * recip(lookup(ylo[z : z + 1, :], table) + k[z, 0:1, :])
            last = has_high * recip(lookup(yhi[z : z + 1, :], table) + k[z, ny - 1 : ny, :])
            fye_o[z, 0:1, :] = first
            fye_o[z, 1:2, :] = last

            def body(c, carry):
                at = rows_of(c)
                diagonal = d[z, at, :]
                diagonal = diagonal + jnp.where(sub + c * 8 == 0, first, 0.0)
                diagonal = diagonal + jnp.where(sub + c * 8 == ny - 1, last, 0.0)
                if z == 0:
                    face = has_below * recip(lookup(zlo[0, at, :], table) + k[z, at, :])
                    fze_o[0, at, :] = face
                    diagonal = diagonal + face
                if z == nz - 1:
                    face = has_above * recip(lookup(zhi[0, at, :], table) + k[z, at, :])
                    fze_o[1, at, :] = face
                    diagonal = diagonal + face
                s = lax.rsqrt(diagonal)
                x = s * b[z, at, :]
                s_o[z, at, :] = s
                x_o[z, at, :] = x
                return (
                    carry[0] + x * wide(vectors[my, 0, at, :], nx),
                    carry[1] + x * wide(vectors[my, 1, at, :], nx),
                )
            zero = jnp.zeros((8, nx), F32)
            right, left = lax.fori_loop(0, chunks, body, (zero, zero))
            sums.append((jnp.sum(right, 0, keepdims=True), jnp.sum(left, 0, keepdims=True)))
        payloads(my, sums, (one, two, three))
        for z in range(nz):
            one[nz + z : nz + z + 1, :] = s_o[z, ny - 1 : ny, :]
            three[nz + z : nz + z + 1, :] = s_o[z, 0:1, :]

    s, x, fye, fze, one, two, three = call(
        scaled,
        [block, block, edge, (2, ny, nx), (2 * nz, nx), (nz, nx), (2 * nz, nx)],
        [SMEM] + [VMEM] * 8,
    )(table, k, ylo, yhi, zlo, zhi, d, b, vectors)

    def lines(x, green, out):
        my = lax.axis_index("gy")
        for z in range(nz):
            head = x[z].astype(jnp.bfloat16)
            tail = (x[z] - head.astype(F32)).astype(jnp.bfloat16)
            stack = jnp.concatenate([head, head, tail], axis=0)
            out[z] = jnp.dot(green[my], stack, preferred_element_type=F32)

    def solved(part, s, x, vectors, scalars, one, two, three, below, above, p_o, low_o, high_o, side_o):
        my = lax.axis_index("gy")
        for z in range(nz):
            got = [r[z : z + 1, :] for r in (one, two, three)]
            left = sum(scalars[my, n + 1] * got[n] for n in range(3))
            right = sum(scalars[my, 5 + n] * got[n] for n in range(3))

            def value(at):
                return part[z, at, :] + (
                    wide(vectors[my, 2, at, :], nx) * left + wide(vectors[my, 3, at, :], nx) * right
                )

            def body(c, _):
                at = rows_of(c)
                p = s[z, at, :] * value(at)
                p_o[z, at, :] = p
                if z == 0:
                    low_o[0, at, :] = p
                if z == nz - 1:
                    high_o[0, at, :] = p
                return 0
            lax.fori_loop(0, chunks, body, 0)
            g = value(pl.ds(0, 8))
            side_o[z, 0:1, :] = below[nz + z : nz + z + 1, :] * ((2.0 + SHIFT) * g[0:1] - g[1:2] - x[z, 0:1, :])
            g = value(pl.ds(ny - 8, 8))
            side_o[z, 1:2, :] = above[nz + z : nz + z + 1, :] * (
                (2.0 + SHIFT) * g[7:8] - g[6:7] - x[z, ny - 1 : ny, :]
            )

    def precondition(x, one, two, three, below, above):
        one, two, three = (ring(v, "gy", parts, n) for n, v in ((1, one), (2, two), (3, three)))
        part = call(lines, [block], [VMEM, VMEM])(x, green)[0]
        if below is None:
            below, above = one, three
        out = call(solved, [block, plane, plane, edge], [VMEM] * 4 + [SMEM] + [VMEM] * 5)(
            part, s, x, vectors, scalars, one, two, three, below, above
        )
        return out, below, above

    def total(value):
        return jnp.sum(jnp.sum(value, 0, keepdims=True), 1, keepdims=True)

    def operator(p, side, fx, fy, fz, fye, e, q_o, z):
        sub = sublane((8, nx))
        bottom = fye[z, 0:1, :] * (side[z, 0:1, :] - p[z, 0:1, :])
        top = fye[z, 1:2, :] * (p[z, ny - 1 : ny, :] - side[z, 1:2, :])

        def body(c, carry):
            at = rows_of(c)
            v = p[z, at, :]
            after = p[z, rows_of(jnp.minimum(c + 1, chunks - 1)), :]
            up = jnp.where(sub == 7, pltpu.roll(after, 7, 0), pltpu.roll(v, 7, 0))
            flow = fy[z, at, :] * (v - up)
            turned = pltpu.roll(flow, 1, 0)
            q = flow - jnp.where(sub == 0, carry, turned)
            q = q + jnp.where(sub + c * 8 == ny - 1, top, 0.0)
            flow = fx[z, at, :] * (v - pltpu.roll(v, nx - 1, 1))
            q = q + (flow - pltpu.roll(flow, 1, 1))
            if z > 0:
                q = q + fz[z - 1, at, :] * (v - p[z - 1, at, :])
            if z < nz - 1:
                q = q + fz[z, at, :] * (v - p[z + 1, at, :])
            edges = e[z, at, :]
            q_o[z, at, :] = ends(q, edges[:, :128] * v[:, :128], edges[:, 128:] * v[:, -128:])
            return turned
        lax.fori_loop(0, chunks, body, jnp.broadcast_to(bottom, (8, nx)), unroll=True)

    def inner(p, side, fx, fy, fz, fye, e, q_o):
        for z in range(nz):
            operator(p, side, fx, fy, fz, fye, e, q_o, z)

    def dots_out(out, sums):
        at = lane((1, 128))
        row = jnp.zeros((1, 128), F32)
        for n, value in enumerate(sums):
            row = jnp.where(at == n, total(value), row)
        out[0:1, :] = row

    def outer_first(p, q, zlo, zhi, fze, s, b, vectors, q_o, x_o, one, two, three, dots):
        my = lax.axis_index("gy")
        zero = jnp.zeros((8, nx), F32)
        bp, pq = zero, zero
        sums = []
        for z in range(nz):
            def body(c, carry):
                at = rows_of(c)
                v, image = p[z, at, :], q[z, at, :]
                if z == 0:
                    image = image + fze[0, at, :] * (v - zlo[0, at, :])
                if z == nz - 1:
                    image = image + fze[1, at, :] * (v - zhi[0, at, :])
                x = s[z, at, :] * image
                q_o[z, at, :] = image
                x_o[z, at, :] = x
                return (
                    carry[0] + x * wide(vectors[my, 0, at, :], nx),
                    carry[1] + x * wide(vectors[my, 1, at, :], nx),
                    carry[2] + b[z, at, :] * v,
                    carry[3] + v * image,
                )
            right, left, bp, pq = lax.fori_loop(0, chunks, body, (zero, zero, bp, pq))
            sums.append((jnp.sum(right, 0, keepdims=True), jnp.sum(left, 0, keepdims=True)))
        payloads(my, sums, (one, two, three))
        dots_out(dots, (bp, pq))

    def outer_last(w, v, zlo, zhi, fze, b, q, first, v_o, dots):
        zero = jnp.zeros((8, nx), F32)
        carry = (zero, zero, zero)
        for z in range(nz):
            def body(c, carry):
                at = rows_of(c)
                field, image = w[z, at, :], v[z, at, :]
                if z == 0:
                    image = image + fze[0, at, :] * (field - zlo[0, at, :])
                if z == nz - 1:
                    image = image + fze[1, at, :] * (field - zhi[0, at, :])
                v_o[z, at, :] = image
                return (
                    carry[0] + b[z, at, :] * field,
                    carry[1] + q[z, at, :] * field,
                    carry[2] + image * field,
                )
            carry = lax.fori_loop(0, chunks, body, carry)
        at = lane((1, 128))
        row = first[...]
        for n, value in enumerate(carry):
            row = jnp.where(at == n + 2, total(value), row)
        dots[...] = row

    def combine(gathered, p, w, q, v, b, x_o, r_o):
        sums = jnp.sum(gathered[...], 0, keepdims=True)
        at = lane((1, 128))
        bp, pq, bw, qw, wv = (jnp.sum(jnp.where(at == n, sums, 0.0), 1, keepdims=True) for n in range(5))
        step = bp / pq
        product = bp - step * (bw + pq) + step * step * qw
        more = 1.0 + product / bp
        curvature = more * more * pq - 2.0 * more * step * qw + step * step * wv
        second = product / curvature
        along, across = step + second * more, second * step
        for z in range(nz):
            def body(c, _):
                at = rows_of(c)
                x_o[z, at, :] = along * p[z, at, :] - across * w[z, at, :]
                r_o[z, at, :] = b[z, at, :] - along * q[z, at, :] + across * v[z, at, :]
                return 0
            lax.fori_loop(0, chunks, body, 0)

    def image_part(p, side):
        return call(inner, [block], [VMEM] * 7)(p, side, fx, fy, fz, fye, e)[0]

    (p, low, high, side), below, above = precondition(x, one, two, three, None, None)
    zlo, zhi = ring(high, "gz", layers, 1), ring(low, "gz", layers, -1)
    q, x, one, two, three, dots = call(
        outer_first, [block, block, (nz, nx), (nz, nx), (nz, nx), (1, 128)], [VMEM] * 8
    )(p, image_part(p, side), zlo, zhi, fze, s, b, vectors)
    (w, low, high, side), _, _ = precondition(x, one, two, three, below, above)
    zlo, zhi = ring(high, "gz", layers, 1), ring(low, "gz", layers, -1)
    v, dots = call(outer_last, [block, (1, 128)], [VMEM] * 8)(w, image_part(w, side), zlo, zhi, fze, b, q, dots)
    count = parts * layers
    gathered = lax.all_to_all(jnp.broadcast_to(dots, (count, 128)), ALL, 0, 0, tiled=True)
    return tuple(call(combine, [block, block], [VMEM] * 6)(gathered, p, w, q, v, b))


def solution(mesh):
    return jax.shard_map(
        local,
        mesh=mesh,
        in_specs=(P("gz", "gy", None), P(), P(None, "gz", "gy"), P(), P("gz", "gy", None)),
        out_specs=(P("gz", "gy", None), P("gz", "gy", None)),
        check_vma=False,
    )
```

time: 468 us -> 86.9 us (0.19); the launches traced: 463 us -> 86.7 us
  blocking collectives: 291 us -> 26.7 us
  other arithmetic: 41 us -> 0.01 us
  waiting for transfers between devices: 39 us -> 4.79 us
  matrix products: 24.7 us -> 0 us
  Pallas kernels: 0 us -> 22.7 us
  local copies, waits for them, and re-layouts: 24.2 us -> 4.66 us
  starting transfers between devices: 38 us -> 27 us
    psum x3 -> x0, blocking collectives: 228 us -> none  [the longest x2 152 us: residual_dot(): return lax.psum(jnp.sum(residual * pre), ('gz', 'gy'))]
    all_to_all x3 -> x1, blocking collectives: 62.9 us -> 26.7 us  [local(): lax.all_to_all(jnp.broadcast_to(dots, (count, 128)), ALL, 0, 0, tiled=True)]
    dot_general x4 -> x0, matrix products: 24.7 us -> none  [the longest x2 12.5 us: line_solve(): jnp.einsum('yj,zyx->zjx', basis, lines, precision=HIGHEST)]
    pallas_call x0 -> x11, Pallas kernels: none -> 22.7 us  [the longest x2 7.66 us: image_part(): return call(inner, [block], [VMEM] * 7)(p, side, fx, fy, fz, fye, e)[0]]
    ppermute x12 -> x14, waiting for transfers between devices: 25.8 us -> 4.79 us  [ring(): lax.ppermute(value, axis, [(i, (i + step) % size) for i in range(size)])]
    reduce_sum x3 -> x0, other arithmetic: 16.9 us -> none  [the longest x2 13.2 us: local(): curvature_sum = lax.psum(jnp.sum(direction * image), ('gz', 'gy'))]
    all_to_all x1 -> x0, waiting for transfers between devices: 13.2 us -> none  [precondition(): lax.all_to_all(values * scale, 'gy', split_axis=2, concat_axis=1, tiled=T...]
    all_to_all x8 -> x0, local copies, waits for them, and re-layouts: 12.5 us -> none  [the longest x4 6.34 us: line_solve(): return lax.all_to_all(result, 'gy', split_axis=1, concat_axis=2, tiled=True)]
  transfers between devices with their start and end apart: 13 -> 14, of which waited for: 10 -> 4; matrix products, arithmetic and copies ran while one was open for 0% -> 2% of each run, Pallas kernels for 0% -> 16%
where the time goes in v1:
time: 86.9 us; the launch traced here: 86.7 us
  starting transfers between devices  27 us (31%)
  blocking collectives  26.7 us (31%)
  Pallas kernels  22.7 us (26%)
  waiting for transfers between devices  4.79 us (6%)
  local copies, waits for them, and re-layouts  4.66 us (5%)
    ppermute x14, starting transfers between devices, ring(): lax.ppermute(value, axis, [(i, (i + step) % size) for i in range(size)])  27 us
    all_to_all x1, blocking collectives, local(): lax.all_to_all(jnp.broadcast_to(dots, (count, 128)), ALL, 0, 0, tiled=True)  26.7 us
    pallas_call x2, Pallas kernels, image_part(): return call(inner, [block], [VMEM] * 7)(p, side, fx, fy, fz, fye, e)[0]  7.66 us
    pallas_call x1, Pallas kernels, local(): call(faces, [block, block, block, (nz - 1, ny, nx), block, (nz, ny, 256),...  5.6 us
    ppermute x14, waiting for transfers between devices, ring(): lax.ppermute(value, axis, [(i, (i + step) % size) for i in range(size)])  4.79 us
    pallas_call x2, Pallas kernels, precondition(): call(solved, [block, plane, plane, edge], [VMEM] * 4 + [SMEM] + [VMEM] * 5)  2.57 us
    unnamed x18, local copies, waits for them, and re-layouts  2.32 us
    pallas_call x1, Pallas kernels, local(): call(scaled, [block, block, edge, (2, ny, nx), (2 * nz, nx), (nz, nx), (2...  2.09 us
  transfers between devices with their start and end apart: 14, of which 4 were waited for; matrix products, arithmetic and copies ran while one was open for 2% of the time, Pallas kernels for 16%

profile of v1, /device:TPU:1, one launch (start us, length us, event | category | flops | bytes accessed | tf_op | source)
XLA Modules:
  0.0 86.7 jit_solution(2732441123519731431)
XLA Ops:
  0.6 1.0 %fusion.1 = (s32[4,1,512]{2,1,0:T(1,128)S(1)}, s32[4,1,512]{2,1,0:T(1,128)S(1)}) fusion(s32[4,128,512]{2,1,0:T(8,128)} %labels.1), kind=kLoop, calls=%fused_computation.5 | loop fusion | bytes 32768 | tf_op jit(solution)/shard_map/slice | solution.py:105
  1.6 2.2 %collective-permute-start = (s32[4,512]{1,0:T(4,128)S(1)}, s32[4,512]{1,0:T(4,128)S(1)}, u32[]{:S(2)}, u32[]{:S(2)}) collective-permute-start(s32[4,512]{1,0:T(4,128)S(1)} %bitcast.12), channel_id=1, source_target_pairs={{0,1},{1,2},{2,3},{3,0},{4,5},{5,6},{6,7},{7,4},{8,9},{9,10},{10,1... | collective-permute-start | bytes 24584 | tf_op jit(solution)/shard_map/ppermute | solution.py:99
  3.8 1.5 %collective-permute-start.1 = (s32[4,512]{1,0:T(4,128)S(1)}, s32[4,512]{1,0:T(4,128)S(1)}, u32[]{:S(2)}, u32[]{:S(2)}) collective-permute-start(s32[4,512]{1,0:T(4,128)S(1)} %bitcast.13), channel_id=1, source_target_pairs={{0,3},{1,0},{2,1},{3,2},{4,7},{5,4},{6,5},{7,6},{8,11},{9,8},{10,9... | collective-permute-start | bytes 24584 | tf_op jit(solution)/shard_map/ppermute | solution.py:99
  5.4 1.1 %fusion = (s32[1,128,512]{2,1,0:T(8,128)S(1)}, s32[1,128,512]{2,1,0:T(8,128)S(1)}) fusion(s32[4,128,512]{2,1,0:T(8,128)} %labels.1), kind=kLoop, calls=%fused_computation.4 | loop fusion | bytes 1048576 | tf_op jit(solution)/shard_map/slice | solution.py:103
  6.5 2.9 %collective-permute-start.3 = (s32[1,128,512]{2,1,0:T(8,128)S(1)}, s32[1,128,512]{2,1,0:T(8,128)S(1)}, u32[]{:S(2)}, u32[]{:S(2)}) collective-permute-start(s32[1,128,512]{2,1,0:T(8,128)S(1)} %get-tuple-element.62), channel_id=1, source_target_pairs={{0,252},{4,0},{8,4},{12,8},{16,12},{20,16},{24,20},{28,24},{32,28}... | collective-permute-start | bytes 786440 | tf_op jit(solution)/shard_map/ppermute | solution.py:99
  9.4 0.6 copy-done.7
  10.0 0.2 copy.15.masks
  10.2 0.4 copy-done.5
  10.7 1.2 %copy-done.3 = f32[4,128,512]{2,1,0:T(8,128)S(1)} copy-done((f32[4,128,512]{2,1,0:T(8,128)S(1)}, f32[4,128,512]{2,1,0:T(8,128)}, u32[]{:S(2)}) %copy-start.3) | copy-done | bytes 1048600
  11.9 5.6 %shard_map.95 = (f32[4,128,512]{2,1,0:T(8,128)S(1)}, f32[4,128,512]{2,1,0:T(8,128)S(1)}, f32[4,128,512]{2,1,0:T(8,128)S(1)}, f32[3,128,512]{2,1,0:T(8,128)S(1)},...) custom-call(s32[4,128,512]{2,1,0:T(8,128)S(1)} %copy-done.1, ...), custom_call_target="tpu_custom_call" | custom-call | tf_op jit(solution)/shard_map/pallas_call | solution.py:143
  17.6 2.1 %shard_map.96 = (f32[4,128,512]{2,1,0:T(8,128)S(1)}, f32[4,128,512]{2,1,0:T(8,128)S(1)}, f32[4,8,512]{2,1,0:T(8,128)S(1)}, f32[2,128,512]{2,1,0:T(8,128)S(1)}, f...) custom-call(f32[4]{0:T(128)S(1)} %broadcast_divide_fusion.table, ...), custom_call_target="tpu_custom_call" | custom-call | tf_op jit(solution)/shard_map/pallas_call | solution.py:195
  19.7 0.1 collective-permute-start.4
  19.8 2.7 %collective-permute-start.6 = (f32[8,512]{1,0:T(8,128)S(1)}, f32[8,512]{1,0:T(8,128)S(1)}, u32[]{:S(2)}, u32[]{:S(2)}) collective-permute-start(f32[8,512]{1,0:T(8,128)S(1)} %get-tuple-element.39), channel_id=1, source_target_pairs={{0,3},{1,0},{2,1},{3,2},{4,7},{5,4},{6,5},{7,6},{8,11},{9,8},{10,9... | collective-permute-start | bytes 49160 | tf_op jit(solution)/shard_map/ppermute | solution.py:99
  22.4 0.5 shard_map.97.part
  22.9 3.5 %collective-permute-done.5.two = f32[4,512]{1,0:T(4,128)S(1)} collective-permute-done((f32[4,512]{1,0:T(4,128)S(1)}, f32[4,512]{1,0:T(4,128)S(1)}, u32[]{:S(2)}, u32[]{:S(2)}) %collective-permute-start.5) | collective-permute-done | bytes 8224 | tf_op jit(solution)/shard_map/ppermute | solution.py:99
  26.4 1.3 %shard_map.98 = (f32[4,128,512]{2,1,0:T(8,128)S(1)}, f32[1,128,512]{2,1,0:T(8,128)S(1)}, f32[1,128,512]{2,1,0:T(8,128)S(1)}, f32[4,8,512]{2,1,0:T(8,128)S(1)}) custom-call(f32[4,128,512]{2,1,0:T(8,128)S(1)} %shard_map.97.part, f32[4,128,512]{2,1,0:T(8,128)S(1)} %get-tuple-element.36.s, f32[4,128,512]{2,1,0:T(8,128)S(1)} %get-tuple-element.35.x, ...), custom_call_target="tpu_custom_call" | custom-call | tf_op jit(solution)/shard_map/pallas_call | solution.py:243
  27.7 1.6 %collective-permute-start.7 = (f32[1,128,512]{2,1,0:T(8,128)S(1)}, f32[1,128,512]{2,1,0:T(8,128)S(1)}, u32[]{:S(2)}, u32[]{:S(2)}) collective-permute-start(f32[1,128,512]{2,1,0:T(8,128)S(1)} %get-tuple-element.47), channel_id=1, source_target_pairs={{0,4},{4,8},{8,12},{12,16},{16,20},{20,24},{24,28},{28,32},{32,36}... | collective-permute-start | bytes 786440 | tf_op jit(solution)/shard_map/ppermute | solution.py:99
  29.4 6.5 %collective-permute-start.8 = (f32[1,128,512]{2,1,0:T(8,128)S(1)}, f32[1,128,512]{2,1,0:T(8,128)S(1)}, u32[]{:S(2)}, u32[]{:S(2)}) collective-permute-start(f32[1,128,512]{2,1,0:T(8,128)S(1)} %get-tuple-element.48), channel_id=1, source_target_pairs={{0,252},{4,0},{8,4},{12,8},{16,12},{20,16},{24,20},{28,24},{32,28}... | collective-permute-start | bytes 786440 | tf_op jit(solution)/shard_map/ppermute | solution.py:99
  35.9 3.8 %shard_map.99.q = f32[4,128,512]{2,1,0:T(8,128)S(1)} custom-call(f32[4,128,512]{2,1,0:T(8,128)S(1)} %get-tuple-element.40.p, f32[4,8,512]{2,1,0:T(8,128)S(1)} %get-tuple-element.41.side, f32[4,128,512]{2,1,0:T(8,128)S(1)} %get-tuple-element.42.fx, f32[4,128,512]{2,1,0:T(8,128)S(1)} %get-tuple-element.43.fy, f32[3,128,512]{2,1,0:T(8,128)S(1)} %get-tuple-element.44.fz, ...), custom_call_target="tpu_custom_call" | custom-call | tf_op jit(solution)/shard_map/pallas_call | solution.py:357
  39.7 1.0 %shard_map.100 = (f32[4,128,512]{2,1,0:T(8,128)S(1)}, f32[4,128,512]{2,1,0:T(8,128)S(1)}, f32[4,512]{1,0:T(4,128)S(1)}, f32[4,512]{1,0:T(4,128)S(1)}, f32[4,512]{1,0:T(4,128)S(1)}, /*index=5*/f32[1,128]{1,0:T(1,128)S(1)}) custom-call(f32[4,128,512]{2,1,0:T(8,128)S(1)} %get-tuple-element.40.p, f32[4,128,512]{2,1,0:T(8,128)S(1)} %shard_map.99.q, ...), custom_call_target="tpu_custom_call" | custom-call | tf_op jit(solution)/shard_map/pallas_call | solution.py:361
  40.7 1.3 %collective-permute-start.10 = (f32[4,512]{1,0:T(4,128)S(1)}, f32[4,512]{1,0:T(4,128)S(1)}, u32[]{:S(2)}, u32[]{:S(2)}) collective-permute-start(f32[4,512]{1,0:T(4,128)S(1)} %get-tuple-element.52), channel_id=1, source_target_pairs={{0,2},{1,3},{2,0},{3,1},{4,6},{5,7},{6,4},{7,5},{8,10},{9,11},{10,... | collective-permute-start | bytes 24584 | tf_op jit(solution)/shard_map/ppermute | solution.py:99
  42.1 1.3 %collective-permute-start.11 = (f32[4,512]{1,0:T(4,128)S(1)}, f32[4,512]{1,0:T(4,128)S(1)}, u32[]{:S(2)}, u32[]{:S(2)}) collective-permute-start(f32[4,512]{1,0:T(4,128)S(1)} %get-tuple-element.53), channel_id=1, source_target_pairs={{0,3},{1,0},{2,1},{3,2},{4,7},{5,4},{6,5},{7,6},{8,11},{9,8},{10,9... | collective-permute-start | bytes 24584 | tf_op jit(solution)/shard_map/ppermute | solution.py:99
  43.4 0.4 shard_map.101.part
  43.9 0.6 collective-permute-done.9.one
  44.5 0.3 collective-permute-done.10.two
  44.8 0.3 collective-permute-done.11.three
  45.1 1.3 %shard_map.102 = (f32[4,128,512]{2,1,0:T(8,128)S(1)}, f32[1,128,512]{2,1,0:T(8,128)S(1)}, f32[1,128,512]{2,1,0:T(8,128)S(1)}, f32[4,8,512]{2,1,0:T(8,128)S(1)}) custom-call(f32[4,128,512]{2,1,0:T(8,128)S(1)} %shard_map.101.part, f32[4,128,512]{2,1,0:T(8,128)S(1)} %get-tuple-element.36.s, f32[4,128,512]{2,1,0:T(8,128)S(1)} %get-tuple-element.50.x, ...), custom_call_target="tpu_custom_call" | custom-call | tf_op jit(solution)/shard_map/pallas_call | solution.py:243
  46.5 6.7 %collective-permute-start.13 = (f32[1,128,512]{2,1,0:T(8,128)S(1)}, f32[1,128,512]{2,1,0:T(8,128)S(1)}, u32[]{:S(2)}, u32[]{:S(2)}) collective-permute-start(f32[1,128,512]{2,1,0:T(8,128)S(1)} %get-tuple-element.57), channel_id=1, source_target_pairs={{0,252},{4,0},{8,4},{12,8},{16,12},{20,16},{24,20},{28,24},{32,28}... | collective-permute-start | bytes 786440 | tf_op jit(solution)/shard_map/ppermute | solution.py:99
  53.2 3.9 %shard_map.103.v = f32[4,128,512]{2,1,0:T(8,128)S(1)} custom-call(f32[4,128,512]{2,1,0:T(8,128)S(1)} %get-tuple-element.54.p.w, f32[4,8,512]{2,1,0:T(8,128)S(1)} %get-tuple-element.55.side, f32[4,128,512]{2,1,0:T(8,128)S(1)} %get-tuple-element.42.fx, f32[4,128,512]{2,1,0:T(8,128)S(1)} %get-tuple-element.43.fy, f32[3,128,512]{2,1,0:T(8,128)S(1)} %get-tuple-element.44.fz, ...), custom_call_target="tpu_custom_call" | custom-call | tf_op jit(solution)/shard_map/pallas_call | solution.py:357
  57.1 0.8 shard_map.104
  57.9 26.7 %all_to_all.8 = f32[256,1,128]{2,1,0:T(1,128)S(1)} all-to-all(f32[256,1,128]{2,1,0:T(1,128)S(1)} %broadcast_in_dim.9), channel_id=1, replica_groups=mesh['gz'=64,'gy'=4] {'gz','gy'}, dimensions={0} | all-to-all | bytes 262144 | tf_op jit(solution)/shard_map/all_to_all | solution.py:368
  84.6 2.1 %shard_map.105 = (f32[4,128,512]{2,1,0:T(8,128)}, f32[4,128,512]{2,1,0:T(8,128)}) custom-call(f32[256,128]{1,0:T(8,128)S(1)} %bitcast.10, f32[4,128,512]{2,1,0:T(8,128)S(1)} %get-tuple-element.40.p, f32[4,128,512]{2,1,0:T(8,128)S(1)} %get-tuple-element.54.p.w, f32[4,128,512]{2,1,0:T(8,128)S(1)} %get-tuple-element.58.q, ...), custom_call_target="tpu_custom_call" | custom-call | tf_op jit(solution)/shard_map/pallas_call | solution.py:369
  (32 shorter events, 0.3 us)
Async XLA Ops:
  0.6 9.6 %copy-start.1 = (s32[4,128,512]{2,1,0:T(8,128)S(1)}, s32[4,128,512]{2,1,0:T(8,128)}, u32[]{:S(2)}) copy-start(s32[4,128,512]{2,1,0:T(8,128)} %labels.1) | copy-start | bytes 3145732
  1.6 15.9 %collective-permute-start = (s32[4,512]{1,0:T(4,128)S(1)}, s32[4,512]{1,0:T(4,128)S(1)}, u32[]{:S(2)}, u32[]{:S(2)}) collective-permute-start(s32[4,512]{1,0:T(4,128)S(1)} %bitcast.12), channel_id=1, source_target_pairs={{0,1},{1,2},{2,3},{3,0},{4,5},{5,6},{6,7},{7,4},{8,9},{9,10},{10,1... | collective-permute-start | bytes 24584 | tf_op jit(solution)/shard_map/ppermute | solution.py:99
  3.8 13.7 %collective-permute-start.1 = (s32[4,512]{1,0:T(4,128)S(1)}, s32[4,512]{1,0:T(4,128)S(1)}, u32[]{:S(2)}, u32[]{:S(2)}) collective-permute-start(s32[4,512]{1,0:T(4,128)S(1)} %bitcast.13), channel_id=1, source_target_pairs={{0,3},{1,0},{2,1},{3,2},{4,7},{5,4},{6,5},{7,6},{8,11},{9,8},{10,9... | collective-permute-start | bytes 24584 | tf_op jit(solution)/shard_map/ppermute | solution.py:99
  5.4 4.0 %copy-start.6 = (s32[2,4,128]{2,1,0:T(4,128)S(1)}, s32[2,4,128]{2,1,0:T(4,128)}, u32[]{:S(2)}) copy-start(s32[2,4,128]{2,1,0:T(4,128)} %param.10) | copy-start | bytes 12292
  6.5 11.1 %collective-permute-start.3 = (s32[1,128,512]{2,1,0:T(8,128)S(1)}, s32[1,128,512]{2,1,0:T(8,128)S(1)}, u32[]{:S(2)}, u32[]{:S(2)}) collective-permute-start(s32[1,128,512]{2,1,0:T(8,128)S(1)} %get-tuple-element.62), channel_id=1, source_target_pairs={{0,252},{4,0},{8,4},{12,8},{16,12},{20,16},{24,20},{28,24},{32,28}... | collective-permute-start | bytes 786440 | tf_op jit(solution)/shard_map/ppermute | solution.py:99
  9.3 0.7 copy-start.7
  9.3 8.2 %collective-permute-start.2 = (s32[1,128,512]{2,1,0:T(8,128)S(1)}, s32[1,128,512]{2,1,0:T(8,128)S(1)}, u32[]{:S(2)}, u32[]{:S(2)}) collective-permute-start(s32[1,128,512]{2,1,0:T(8,128)S(1)} %get-tuple-element.63), channel_id=1, source_target_pairs={{0,4},{4,8},{8,12},{12,16},{16,20},{20,24},{24,28},{28,32},{32,36}... | collective-permute-start | bytes 786440 | tf_op jit(solution)/shard_map/ppermute | solution.py:99
  10.0 0.7 copy-start.5
  10.7 1.2 %copy-start.3 = (f32[4,128,512]{2,1,0:T(8,128)S(1)}, f32[4,128,512]{2,1,0:T(8,128)}, u32[]{:S(2)}) copy-start(f32[4,128,512]{2,1,0:T(8,128)} %source.1) | copy-start | bytes 3145732
  11.9 5.7 %copy-start = (f32[4,4,128,128]{3,2,1,0:T(8,128)S(1)}, f32[4,4,128,128]{3,2,1,0:T(8,128)}, u32[]{:S(2)}) copy-start(f32[4,4,128,128]{3,2,1,0:T(8,128)} %constant.9.clone.vectors) | copy-start | bytes 3145732
  17.6 4.9 %copy-start.2 = (bf16[4,128,384]{2,1,0:T(8,128)(2,1)S(1)}, bf16[4,128,384]{2,1,0:T(8,128)(2,1)}, u32[]{:S(2)}) copy-start(bf16[4,128,384]{2,1,0:T(8,128)(2,1)} %constant.8.clone.green) | copy-start | bytes 1179652
  19.7 6.8 %collective-permute-start.4 = (f32[8,512]{1,0:T(8,128)S(1)}, f32[8,512]{1,0:T(8,128)S(1)}, u32[]{:S(2)}, u32[]{:S(2)}) collective-permute-start(f32[8,512]{1,0:T(8,128)S(1)} %get-tuple-element.37), channel_id=1, source_target_pairs={{0,1},{1,2},{2,3},{3,0},{4,5},{5,6},{6,7},{7,4},{8,9},{9,10},{10,1... | collective-permute-start | bytes 49160 | tf_op jit(solution)/shard_map/ppermute | solution.py:99
  19.8 6.7 %collective-permute-start.6 = (f32[8,512]{1,0:T(8,128)S(1)}, f32[8,512]{1,0:T(8,128)S(1)}, u32[]{:S(2)}, u32[]{:S(2)}) collective-permute-start(f32[8,512]{1,0:T(8,128)S(1)} %get-tuple-element.39), channel_id=1, source_target_pairs={{0,3},{1,0},{2,1},{3,2},{4,7},{5,4},{6,5},{7,6},{8,11},{9,8},{10,9... | collective-permute-start | bytes 49160 | tf_op jit(solution)/shard_map/ppermute | solution.py:99
  22.4 4.0 %collective-permute-start.5 = (f32[4,512]{1,0:T(4,128)S(1)}, f32[4,512]{1,0:T(4,128)S(1)}, u32[]{:S(2)}, u32[]{:S(2)}) collective-permute-start(f32[4,512]{1,0:T(4,128)S(1)} %get-tuple-element.38), channel_id=1, source_target_pairs={{0,2},{1,3},{2,0},{3,1},{4,6},{5,7},{6,4},{7,5},{8,10},{9,11},{10,... | collective-permute-start | bytes 24584 | tf_op jit(solution)/shard_map/ppermute | solution.py:99
  22.4 4.0 %copy-start.4 = (f32[4,8]{1,0:T(4,128)S(1)}, f32[4,8]{1,0:T(4,128)}, u32[]{:S(2)}) copy-start(f32[4,8]{1,0:T(4,128)} %constant.10.clone.scalars) | copy-start | bytes 388
  27.7 11.9 %collective-permute-start.7 = (f32[1,128,512]{2,1,0:T(8,128)S(1)}, f32[1,128,512]{2,1,0:T(8,128)S(1)}, u32[]{:S(2)}, u32[]{:S(2)}) collective-permute-start(f32[1,128,512]{2,1,0:T(8,128)S(1)} %get-tuple-element.47), channel_id=1, source_target_pairs={{0,4},{4,8},{8,12},{12,16},{16,20},{20,24},{24,28},{28,32},{32,36}... | collective-permute-start | bytes 786440 | tf_op jit(solution)/shard_map/ppermute | solution.py:99
  29.4 10.3 %collective-permute-start.8 = (f32[1,128,512]{2,1,0:T(8,128)S(1)}, f32[1,128,512]{2,1,0:T(8,128)S(1)}, u32[]{:S(2)}, u32[]{:S(2)}) collective-permute-start(f32[1,128,512]{2,1,0:T(8,128)S(1)} %get-tuple-element.48), channel_id=1, source_target_pairs={{0,252},{4,0},{8,4},{12,8},{16,12},{20,16},{24,20},{28,24},{32,28}... | collective-permute-start | bytes 786440 | tf_op jit(solution)/shard_map/ppermute | solution.py:99
  40.7 3.8 %collective-permute-start.9 = (f32[4,512]{1,0:T(4,128)S(1)}, f32[4,512]{1,0:T(4,128)S(1)}, u32[]{:S(2)}, u32[]{:S(2)}) collective-permute-start(f32[4,512]{1,0:T(4,128)S(1)} %get-tuple-element.51), channel_id=1, source_target_pairs={{0,1},{1,2},{2,3},{3,0},{4,5},{5,6},{6,7},{7,4},{8,9},{9,10},{10,1... | collective-permute-start | bytes 24584 | tf_op jit(solution)/shard_map/ppermute | solution.py:99
  40.7 4.1 %collective-permute-start.10 = (f32[4,512]{1,0:T(4,128)S(1)}, f32[4,512]{1,0:T(4,128)S(1)}, u32[]{:S(2)}, u32[]{:S(2)}) collective-permute-start(f32[4,512]{1,0:T(4,128)S(1)} %get-tuple-element.52), channel_id=1, source_target_pairs={{0,2},{1,3},{2,0},{3,1},{4,6},{5,7},{6,4},{7,5},{8,10},{9,11},{10,... | collective-permute-start | bytes 24584 | tf_op jit(solution)/shard_map/ppermute | solution.py:99
  42.1 3.0 %collective-permute-start.11 = (f32[4,512]{1,0:T(4,128)S(1)}, f32[4,512]{1,0:T(4,128)S(1)}, u32[]{:S(2)}, u32[]{:S(2)}) collective-permute-start(f32[4,512]{1,0:T(4,128)S(1)} %get-tuple-element.53), channel_id=1, source_target_pairs={{0,3},{1,0},{2,1},{3,2},{4,7},{5,4},{6,5},{7,6},{8,11},{9,8},{10,9... | collective-permute-start | bytes 24584 | tf_op jit(solution)/shard_map/ppermute | solution.py:99
  46.4 10.7 %collective-permute-start.12 = (f32[1,128,512]{2,1,0:T(8,128)S(1)}, f32[1,128,512]{2,1,0:T(8,128)S(1)}, u32[]{:S(2)}, u32[]{:S(2)}) collective-permute-start(f32[1,128,512]{2,1,0:T(8,128)S(1)} %get-tuple-element.56), channel_id=1, source_target_pairs={{0,4},{4,8},{8,12},{12,16},{16,20},{20,24},{24,28},{28,32},{32,36}... | collective-permute-start | bytes 786440 | tf_op jit(solution)/shard_map/ppermute | solution.py:99
  46.5 10.6 %collective-permute-start.13 = (f32[1,128,512]{2,1,0:T(8,128)S(1)}, f32[1,128,512]{2,1,0:T(8,128)S(1)}, u32[]{:S(2)}, u32[]{:S(2)}) collective-permute-start(f32[1,128,512]{2,1,0:T(8,128)S(1)} %get-tuple-element.57), channel_id=1, source_target_pairs={{0,252},{4,0},{8,4},{12,8},{16,12},{20,16},{24,20},{28,24},{32,28}... | collective-permute-start | bytes 786440 | tf_op jit(solution)/shard_map/ppermute | solution.py:99

commit v2 on v1

v2 whole, which is shorter than its diff:
```python
import math

import jax
import jax.numpy as jnp
import ml_dtypes
import numpy as np
from jax import lax
from jax.experimental import pallas as pl
from jax.experimental.pallas import tpu as pltpu
from jax.sharding import PartitionSpec as P

F32 = jnp.float32
SHIFT = 0.0016
VMEM = pl.BlockSpec(memory_space=pltpu.VMEM)
HBM = pl.BlockSpec(memory_space=pltpu.HBM)
SMEM = pl.BlockSpec(memory_space=pltpu.SMEM)
ALL = ("gz", "gy")
STEP = 64


def line_tables(total, parts):
    rows = total // parts
    theta = math.acosh(1.0 + SHIFT / 2.0)
    near = np.cosh(theta * (np.arange(total) + 0.5))
    far = near[::-1]
    norm = math.sinh(theta) * math.sinh(total * theta)
    at = np.arange(total)
    green = np.where(at[:, None] <= at[None, :], near[:, None] * far[None, :], far[:, None] * near[None, :]) / norm
    blocks, vectors, scalars = [], [], np.zeros((parts, 8))
    for d in range(parts):
        own = slice(d * rows, (d + 1) * rows)
        low, high = math.cosh(theta * d * rows), math.cosh(theta * (d + 1) * rows)
        flow, fhigh = math.cosh(theta * (total - d * rows)), math.cosh(theta * (total - (d + 1) * rows))
        g = green[own, own].astype(np.float32)
        head = g.astype(ml_dtypes.bfloat16)
        tail = (g - head.astype(np.float32)).astype(ml_dtypes.bfloat16)
        blocks.append(np.concatenate([head, tail, head], axis=1))
        columns = [near[own] / high, far[own] / flow, low * far[own] / norm, fhigh * near[own] / norm]
        vectors.append(np.stack([np.broadcast_to(c[:, None], (rows, 128)) for c in columns]))
        for k in range(1, parts):
            if d >= k:
                scalars[d, k] = math.cosh(theta * (d - k + 1) * rows) / low
            else:
                scalars[d, 4 + k] = math.cosh(theta * (total - (d - k + parts) * rows)) / fhigh
    return np.stack(blocks), np.stack(vectors).astype(np.float32), scalars.astype(np.float32)


def call(body, outs, ins, scratch=(), dtype=F32, out_space=VMEM):
    return pl.pallas_call(
        body,
        out_shape=[jax.ShapeDtypeStruct(s, dtype) for s in outs],
        in_specs=ins,
        out_specs=[out_space] * len(outs),
        scratch_shapes=list(scratch),
        compiler_params=pltpu.CompilerParams(vmem_limit_bytes=24 * 2**20),
    )


def rows_at(start):
    return slice(start, start + STEP)


def sublane(shape):
    return lax.broadcasted_iota(jnp.int32, shape, 0)


def lane(shape):
    return lax.broadcasted_iota(jnp.int32, shape, 1)


def recip(x):
    r = pl.reciprocal(x, approx=True)
    return r * (2.0 - x * r)


def fold(x):
    return sum(x[r : r + 8] for r in range(0, x.shape[0], 8))


def folded(x):
    x = fold(x)
    return sum(x[:, c : c + 128] for c in range(0, x.shape[1], 128))


def lookup(labels, table):
    low = jnp.where(labels == 1, table[1], table[0])
    high = jnp.where(labels == 3, table[3], table[2])
    return jnp.where(labels >= 2, high, low)


def wide(column, width):
    return jnp.concatenate([column] * (width // 128), axis=1)


def ends(value, low, high):
    return jnp.concatenate([value[:, :128] + low, value[:, 128:-128], value[:, -128:] + high], axis=1)


def local(labels, phase_table, collector_mask, collector_value, source):
    nz, ny, nx = labels.shape
    parts = lax.axis_size("gy")
    layers = lax.axis_size("gz")
    block = (nz, ny, nx)
    plane = (1, ny, nx)
    edge = (nz, 8, nx)
    framed = (nz, ny + 16, nx)
    starts = range(0, ny, STEP)
    outer = sorted({0, nz - 1})
    middle = [z for z in range(nz) if z not in outer]
    ends_shape, middle_shape = (len(outer), ny, nx), (len(middle), ny, nx)
    green, vectors, scalars = line_tables(ny * parts, parts)
    green, vectors, scalars = jnp.asarray(green), jnp.asarray(vectors), jnp.asarray(scalars)

    def pick(z, first, second):
        return first.at[outer.index(z)] if z in outer else second.at[middle.index(z)]

    def ring(value, axis, size, step):
        return lax.ppermute(value, axis, [(i, (i + step) % size) for i in range(size)])

    def borders(labels, below_o, above_o, first_o, last_o, first, last, sems):
        copies = [
            pltpu.make_async_copy(labels.at[pl.ds(0, 1)], below_o, sems.at[0]),
            pltpu.make_async_copy(labels.at[pl.ds(nz - 1, 1)], above_o, sems.at[1]),
            pltpu.make_async_copy(labels.at[:, pl.ds(0, 8)], first, sems.at[2]),
            pltpu.make_async_copy(labels.at[:, pl.ds(ny - 8, 8)], last, sems.at[3]),
        ]
        for copy in copies:
            copy.start()
        for copy in copies:
            copy.wait()
        for z in range(nz):
            first_o[z : z + 1, :] = first[z, 0:1, :]
            last_o[z : z + 1, :] = last[z, 7:8, :]

    below, above, first, last = call(
        borders,
        [plane, plane, (nz, nx), (nz, nx)],
        [HBM],
        [pltpu.VMEM(edge, jnp.int32)] * 2 + [pltpu.SemaphoreType.DMA((4,))],
        jnp.int32,
    )(labels)
    table = 0.5 / phase_table
    ylo, yhi = ring(last, "gy", parts, 1), ring(first, "gy", parts, -1)
    zlo, zhi = ring(above, "gz", layers, 1), ring(below, "gz", layers, -1)
    masks = collector_mask.astype(F32)[..., None]

    def faces(labels, table, values, masks, source, k_o, fx_o, fy_o, fz_o, d_o, e_o, b_o, held, framed_k, sem):
        copy = pltpu.make_async_copy(source, held, sem)
        copy.start()
        for z in range(nz):
            for r in starts:
                k = lookup(labels[z, rows_at(r), :], table)
                k_o[z, rows_at(r), :] = k
                framed_k[z, rows_at(r + 8), :] = k
            framed_k[z, ny + 8 : ny + 16, :] = framed_k[z, ny : ny + 8, :]
            fy_o[z, 0:8, :] = jnp.zeros((8, nx), F32)
        copy.wait()
        sub, across, side = sublane((STEP, nx)), lane((STEP, nx)), lane((STEP, 128))
        for z in range(nz):
            for r in starts:
                at = rows_at(r)
                k = k_o[z, at, :]
                fy = recip(k + framed_k[z, rows_at(r + 9), :])
                if r + STEP == ny:
                    fy = jnp.where(sub == STEP - 1, 0.0, fy)
                fy_o[z, rows_at(r + 8), :] = fy
                fx = jnp.where(across == nx - 1, 0.0, recip(k + pltpu.roll(k, nx - 1, 1)))
                d = fy + fy_o[z, rows_at(r + 7), :] + (fx + pltpu.roll(fx, 1, 1))
                if z > 0:
                    d = d + fz_o[z - 1, at, :]
                if z < nz - 1:
                    fz = recip(k + k_o[z + 1, at, :])
                    fz_o[z, at, :] = fz
                    d = d + fz
                low = jnp.where(side == 0, recip(k[:, :128]) * masks[0, z, at, :], 0.0)
                high = jnp.where(side == 127, recip(k[:, -128:]) * masks[1, z, at, :], 0.0)
                e_o[z, at, :] = jnp.concatenate([low, high], axis=1)
                d_o[z, at, :] = ends(d, low, high)
                b_o[z, at, :] = ends(held[z, at, :], low * values[0], high * values[1])
                fx_o[z, at, :] = fx

    k, fx, fy, fz, d, e, b = call(
        faces,
        [block, block, (nz, ny + 8, nx), (nz - 1, ny, nx), block, (nz, ny, 256), block],
        [VMEM, SMEM, SMEM, VMEM, HBM],
        [pltpu.VMEM(block, F32), pltpu.VMEM(framed, F32), pltpu.SemaphoreType.DMA],
    )(labels, table, collector_value, masks, source)

    def weighted(x, my, vectors, r, carry):
        return (
            carry[0] + fold(x * wide(vectors[my, 0, rows_at(r), :], nx)),
            carry[1] + fold(x * wide(vectors[my, 1, rows_at(r), :], nx)),
        )

    def sums_out(my, sums, z, outs):
        right, left = (jnp.sum(v, 0, keepdims=True) for v in sums)
        for step, out in enumerate(outs, 1):
            out[z : z + 1, :] = jnp.where(my + step < parts, right, left)

    zero = lambda: jnp.zeros((8, nx), F32)
    none = lambda: jnp.zeros((8, 128), F32)

    def scaled(table, k, ylo, yhi, zlo, zhi, d, b, vectors, s_o, xo_o, xm_o, fye_o, fze_o, one, two, three):
        my, level = lax.axis_index("gy"), lax.axis_index("gz")
        has_low, has_high = (my > 0).astype(F32), (my < parts - 1).astype(F32)
        has_below, has_above = (level > 0).astype(F32), (level < layers - 1).astype(F32)
        sub = sublane((STEP, nx))
        for z in range(nz):
            first = has_low * recip(lookup(ylo[z : z + 1, :], table) + k[z, 0:1, :])
            last = has_high * recip(lookup(yhi[z : z + 1, :], table) + k[z, ny - 1 : ny, :])
            fye_o[z, 0:1, :] = first
            fye_o[z, 1:2, :] = last
            carry = (zero(), zero())
            for r in starts:
                at = rows_at(r)
                diagonal = d[z, at, :]
                if r == 0:
                    diagonal = diagonal + jnp.where(sub == 0, first, 0.0)
                if r + STEP == ny:
                    diagonal = diagonal + jnp.where(sub == STEP - 1, last, 0.0)
                if z == 0:
                    face = has_below * recip(lookup(zlo[0, at, :], table) + k[z, at, :])
                    fze_o[0, at, :] = face
                    diagonal = diagonal + face
                if z == nz - 1:
                    face = has_above * recip(lookup(zhi[0, at, :], table) + k[z, at, :])
                    fze_o[1, at, :] = face
                    diagonal = diagonal + face
                s = lax.rsqrt(diagonal)
                x = s * b[z, at, :]
                s_o[z, at, :] = s
                pick(z, xo_o, xm_o)[at, :] = x
                carry = weighted(x, my, vectors, r, carry)
            sums_out(my, carry, z, (one, two, three))
            one[nz + z : nz + z + 1, :] = s_o[z, ny - 1 : ny, :]
            three[nz + z : nz + z + 1, :] = s_o[z, 0:1, :]

    s, xo, xm, fye, fze, one, two, three = call(
        scaled,
        [block, ends_shape, middle_shape, edge, (2, ny, nx), (2 * nz, nx), (nz, nx), (2 * nz, nx)],
        [SMEM] + [VMEM] * 8,
    )(table, k, ylo, yhi, zlo, zhi, d, b, vectors)

    def lines(xo, xm, green, out):
        my = lax.axis_index("gy")
        for z in range(nz):
            x = pick(z, xo, xm)[...]
            head = x.astype(jnp.bfloat16)
            tail = (x - head.astype(F32)).astype(jnp.bfloat16)
            stack = jnp.concatenate([head, head, tail], axis=0)
            out[z] = jnp.dot(green[my], stack, preferred_element_type=F32)

    def solve(z, part, s, xo, xm, vectors, scalars, one, two, three, below, above, put):
        my = lax.axis_index("gy")
        got = [r[z : z + 1, :] for r in (one, two, three)]
        left = sum(scalars[my, n + 1] * got[n] for n in range(3))
        right = sum(scalars[my, 5 + n] * got[n] for n in range(3))
        for r in starts:
            at = rows_at(r)
            g = part[z, at, :] + (wide(vectors[my, 2, at, :], nx) * left + wide(vectors[my, 3, at, :], nx) * right)
            put(r + 8, s[z, at, :] * g)
            if r == 0:
                beside = (2.0 + SHIFT) * g[0:1] - g[1:2] - pick(z, xo, xm)[0:1, :]
                put(7, below[nz + z : nz + z + 1, :] * beside)
            if r + STEP == ny:
                beside = (2.0 + SHIFT) * g[-1:] - g[-2:-1] - pick(z, xo, xm)[ny - 1 : ny, :]
                put(ny + 8, above[nz + z : nz + z + 1, :] * beside)

    def solve_outer(part, s, xo, xm, vectors, scalars, one, two, three, below, above, p_o, low_o, high_o):
        for n, z in enumerate(outer):
            def put(r, value):
                p_o[n, r : r + value.shape[0], :] = value
                if z == 0 and value.shape[0] == STEP:
                    low_o[0, rows_at(r - 8), :] = value
                if z == nz - 1 and value.shape[0] == STEP:
                    high_o[0, rows_at(r - 8), :] = value
            solve(z, part, s, xo, xm, vectors, scalars, one, two, three, below, above, put)

    def total(value):
        return jnp.sum(jnp.sum(value, 0, keepdims=True), 1, keepdims=True)

    def dots_out(out, sums, first):
        at = lane((1, 128))
        row = jnp.zeros((1, 128), F32)
        for n, value in enumerate(sums, first):
            row = jnp.where(at == n, total(value), row)
        out[...] = row

    def operator(read, z, r, fx, fy, fz, fye, e):
        at = rows_at(r)
        v = read(z, r + 8)
        q = fy[z, rows_at(r + 8), :] * (v - read(z, r + 9)) + fy[z, rows_at(r + 7), :] * (v - read(z, r + 7))
        sub = sublane((STEP, nx))
        if r == 0:
            q = q + jnp.where(sub == 0, fye[z, 0:1, :], 0.0) * (v - read(z, r + 7))
        if r + STEP == ny:
            q = q + jnp.where(sub == STEP - 1, fye[z, 1:2, :], 0.0) * (v - read(z, r + 9))
        flow = fx[z, at, :] * (v - pltpu.roll(v, nx - 1, 1))
        q = q + (flow - pltpu.roll(flow, 1, 1))
        if z > 0:
            q = q + fz[z - 1, at, :] * (v - read(z - 1, r + 8))
        if z < nz - 1:
            q = q + fz[z, at, :] * (v - read(z + 1, r + 8))
        edges = e[z, at, :]
        return v, ends(q, edges[:, :128] * v[:, :128], edges[:, 128:] * v[:, -128:])

    def fill(part, s, xo, xm, vectors, scalars, one, two, three, below, above, p_outer, p_o, field):
        for z in middle:
            def put(r, value):
                field[z, r : r + value.shape[0], :] = value
                if value.shape[0] == STEP:
                    p_o[z, rows_at(r - 8), :] = value
            solve(z, part, s, xo, xm, vectors, scalars, one, two, three, below, above, put)
        for n, z in enumerate(outer):
            for r in starts:
                p_o[z, rows_at(r), :] = p_outer[n, rows_at(r + 8), :]

        def read(z, r):
            return p_outer[outer.index(z), rows_at(r), :] if z in outer else field[z, rows_at(r), :]
        return read

    def inner_first(part, s, xo, xm, vectors, scalars, one, two, three, below, above, p_outer, fx, fy, fz, fye, e, b,
                    p_o, q_o, xm_o, one_o, two_o, three_o, dots, field):
        my = lax.axis_index("gy")
        read = fill(part, s, xo, xm, vectors, scalars, one, two, three, below, above, p_outer, p_o, field)
        bp, pq = none(), none()
        for z in outer + middle:
            carry = (zero(), zero())
            for r in starts:
                at = rows_at(r)
                v, image = operator(read, z, r, fx, fy, fz, fye, e)
                bp = bp + folded(b[z, at, :] * v)
                q_o[z, at, :] = image
                if z in middle:
                    scaled_image = s[z, at, :] * image
                    xm_o[middle.index(z), at, :] = scaled_image
                    carry = weighted(scaled_image, my, vectors, r, carry)
                    pq = pq + folded(v * image)
            if z in middle:
                sums_out(my, carry, z, (one_o, two_o, three_o))
        dots_out(dots, (bp, pq), 0)

    def image_of(z, ends, whole, at):
        return ends[outer.index(z), at, :] if z in outer else whole[z, at, :]

    def outside(z, r, v, image, zlo, zhi, fze):
        at = rows_at(r)
        if z == 0:
            image = image + fze[0, at, :] * (v - zlo[0, at, :])
        if z == nz - 1:
            image = image + fze[1, at, :] * (v - zhi[0, at, :])
        return image

    def outer_first(p, q, one, two, three, zlo, zhi, fze, s, vectors, dots, qo_o, xo_o, one_o, two_o, three_o, dots_o):
        my = lax.axis_index("gy")
        pq = none()
        for z in outer:
            carry = (zero(), zero())
            for r in starts:
                at = rows_at(r)
                v = p[z, at, :]
                image = outside(z, r, v, q[z, at, :], zlo, zhi, fze)
                scaled_image = s[z, at, :] * image
                qo_o[outer.index(z), at, :] = image
                xo_o[outer.index(z), at, :] = scaled_image
                carry = weighted(scaled_image, my, vectors, r, carry)
                pq = pq + folded(v * image)
            sums_out(my, carry, z, (one_o, two_o, three_o))
        for z in middle:
            for got, out in ((one, one_o), (two, two_o), (three, three_o)):
                out[z : z + 1, :] = got[z : z + 1, :]
        dots_out(dots_o, (none(), pq), 0)
        dots_o[...] = dots_o[...] + dots[...]

    def inner_last(part, s, xo, xm, vectors, scalars, one, two, three, below, above, p_outer, fx, fy, fz, fye, e, b, q, qo,
                   w_o, v_o, dots, field):
        read = fill(part, s, xo, xm, vectors, scalars, one, two, three, below, above, p_outer, w_o, field)
        bw, qw, wv = none(), none(), none()
        for z in range(nz):
            for r in starts:
                at = rows_at(r)
                w, image = operator(read, z, r, fx, fy, fz, fye, e)
                bw = bw + folded(b[z, at, :] * w)
                qw = qw + folded(image_of(z, qo, q, at) * w)
                wv = wv + folded(image * w)
                v_o[z, at, :] = image
        dots_out(dots, (bw, qw, wv), 2)

    def outer_last(w, v, zlo, zhi, fze, dots_first, dots, v_o, dots_o):
        wv = none()
        for n, z in enumerate(outer):
            for r in starts:
                at = rows_at(r)
                field, image = w[z, at, :], v[z, at, :]
                full = outside(z, r, field, image, zlo, zhi, fze)
                v_o[n, at, :] = full
                wv = wv + folded((full - image) * field)
        dots_out(dots_o, (wv,), 4)
        dots_o[...] = dots_o[...] + (dots[...] + dots_first[...])

    def combine(gathered, p, w, q, qo, v, vo, b, x_o, r_o, x_held, r_held, sems):
        sums = jnp.sum(gathered[...], 0, keepdims=True)
        at = lane((1, 128))
        bp, pq, bw, qw, wv = (jnp.sum(jnp.where(at == n, sums, 0.0), 1, keepdims=True) for n in range(5))
        step = bp / pq
        product = bp - step * (bw + pq) + step * step * qw
        more = 1.0 + product / bp
        curvature = more * more * pq - 2.0 * more * step * qw + step * step * wv
        second = product / curvature
        along = jnp.broadcast_to(step + second * more, (STEP, nx))
        across = jnp.broadcast_to(second * step, (STEP, nx))
        copies = []
        for z in range(nz):
            for r in starts:
                at = rows_at(r)
                x_held[z, at, :] = along * p[z, at, :] - across * w[z, at, :]
                r_held[z, at, :] = b[z, at, :] - along * image_of(z, qo, q, at) + across * image_of(z, vo, v, at)
            for n, (held, out) in enumerate(((x_held, x_o), (r_held, r_o))):
                copies.append(pltpu.make_async_copy(held.at[z], out.at[z], sems.at[n, z]))
                copies[-1].start()
        for copy in copies:
            copy.wait()

    def gather(sums):
        return [ring(v, "gy", parts, n) for n, v in enumerate(sums, 1)]

    field = [pltpu.VMEM(framed, F32)]
    rows = [(nz, nx)] * 3
    framed_pair = (len(outer), ny + 16, nx)

    def start(xo, xm, sums, beside):
        got = gather(sums)
        beside = beside or (got[0], got[2])
        part = call(lines, [block], [VMEM] * 3)(xo, xm, green)[0]
        known = (part, s, xo, xm, vectors, scalars, *got, *beside)
        pair, low, high = call(solve_outer, [framed_pair, plane, plane], places)(*known)
        return (*known, pair), ring(high, "gz", layers, 1), ring(low, "gz", layers, -1), beside

    places = [VMEM] * 5 + [SMEM] + [VMEM] * 5
    known, zlo, zhi, beside = start(xo, xm, (one, two, three), None)
    p, q, xm, *sums, dots = call(
        inner_first, [block, block, middle_shape, *rows, (1, 128)], places + [VMEM] * 7, field
    )(*known, fx, fy, fz, fye, e, b)
    qo, xo, *sums, dots = call(outer_first, [ends_shape, ends_shape, *rows, (1, 128)], [VMEM] * 11)(
        p, q, *sums, zlo, zhi, fze, s, vectors, dots
    )
    known, zlo, zhi, _ = start(xo, xm, sums, beside)
    w, v, last_dots = call(inner_last, [block, block, (1, 128)], places + [VMEM] * 9, field)(
        *known, fx, fy, fz, fye, e, b, q, qo
    )
    vo, dots = call(outer_last, [ends_shape, (1, 128)], [VMEM] * 7)(w, v, zlo, zhi, fze, last_dots, dots)
    count = parts * layers
    gathered = lax.all_to_all(jnp.broadcast_to(dots, (count, 128)), ALL, 0, 0, tiled=True)
    return tuple(
        call(
            combine,
            [block, block],
            [VMEM] * 8,
            [pltpu.VMEM(block, F32)] * 2 + [pltpu.SemaphoreType.DMA((2, nz))],
            out_space=HBM,
        )(gathered, p, w, q, qo, v, vo, b)
    )


def solution(mesh):
    return jax.shard_map(
        local,
        mesh=mesh,
        in_specs=(P("gz", "gy", None), P(), P(None, "gz", "gy"), P(), P("gz", "gy", None)),
        out_specs=(P("gz", "gy", None), P("gz", "gy", None)),
        check_vma=False,
    )
```

time: 86.9 us -> 78.8 us (0.907)
  Pallas kernels: 22.7 us -> 12.6 us
  local copies, waits for them, and re-layouts: 4.66 us -> 2.75 us
  blocking collectives: 26.7 us -> 28.3 us
  other arithmetic: 0.01 us -> 1.35 us
    pallas_call x11 -> x12, Pallas kernels: 22.7 us -> 12.6 us  [the longest x1 2.31 us: local(): call(faces, [block, block, (nz, ny + 8, nx), (nz - 1, ny, nx), block, (nz...]
    slice x2 -> x0, local copies, waits for them, and re-layouts: 2.05 us -> none  [the longest x1 1.08 us: local(): zhi = ring(labels[:1], 'gz', layers, -1)]
    all_to_all x1, blocking collectives: 26.7 us -> 28.3 us  [local(): lax.all_to_all(jnp.broadcast_to(dots, (count, 128)), ALL, 0, 0, tiled=True)]
    unnamed x18 -> x14, local copies, waits for them, and re-layouts: 2.32 us -> 2.46 us
  transfers between devices with their start and end apart: 14 -> 14, of which waited for: 4 -> 5; matrix products, arithmetic and copies ran while one was open for 2% -> 2% of each run, Pallas kernels for 16% -> 10%
where the time goes in v2:
time: 78.8 us; the launch traced here: 78.6 us
  blocking collectives  28.3 us (36%)
  starting transfers between devices  27.7 us (35%)
  Pallas kernels  12.6 us (16%)
  waiting for transfers between devices  5.02 us (6%)
  local copies, waits for them, and re-layouts  2.75 us (3%)
  other arithmetic  1.35 us (2%)
  between operations  0.93 us (1%)
    all_to_all x1, blocking collectives, local(): lax.all_to_all(jnp.broadcast_to(dots, (count, 128)), ALL, 0, 0, tiled=True)  28.3 us
    ppermute x14, starting transfers between devices, ring(): lax.ppermute(value, axis, [(i, (i + step) % size) for i in range(size)])  27.7 us
    ppermute x14, waiting for transfers between devices, ring(): lax.ppermute(value, axis, [(i, (i + step) % size) for i in range(size)])  5.02 us
    unnamed x14, local copies, waits for them, and re-layouts  2.46 us
    pallas_call x1, Pallas kernels, local(): call(faces, [block, block, (nz, ny + 8, nx), (nz - 1, ny, nx), block, (nz...  2.31 us
    pallas_call x1, Pallas kernels, local(): call(inner_last, [block, block, (1, 128)], places + [VMEM] * 9, field)  2.3 us
    pallas_call x1, Pallas kernels, local(): call(inner_first, [block, block, middle_shape, *rows, (1, 128)], places +...  2.22 us
    pallas_call x1, Pallas kernels, local(): call(combine, [block, block], [VMEM] * 8, [pltpu.VMEM(block, F32)] * 2 +...  1.59 us
  transfers between devices with their start and end apart: 14, of which 5 were waited for; matrix products, arithmetic and copies ran while one was open for 2% of the time, Pallas kernels for 10%

profile of v2, /device:TPU:1, one launch (start us, length us, event | category | flops | bytes accessed | tf_op | source)
XLA Modules:
  0.0 78.6 jit_solution(13357263866718918412)
XLA Ops:
  0.6 1.2 %copy-done.1 = s32[4,128,512]{2,1,0:T(8,128)S(1)} copy-done((s32[4,128,512]{2,1,0:T(8,128)S(1)}, s32[4,128,512]{2,1,0:T(8,128)}, u32[]{:S(2)}) %copy-start.1) | copy-done | bytes 1048600
  2.0 2.2 %collective-permute-start = (s32[4,512]{1,0:T(4,128)S(1)}, s32[4,512]{1,0:T(4,128)S(1)}, u32[]{:S(2)}, u32[]{:S(2)}) collective-permute-start(s32[4,512]{1,0:T(4,128)S(1)} %get-tuple-element.46), channel_id=1, source_target_pairs={{0,1},{1,2},{2,3},{3,0},{4,5},{5,6},{6,7},{7,4},{8,9},{9,10},{10,1... | collective-permute-start | bytes 24584 | tf_op jit(solution)/shard_map/ppermute | solution.py:118
  4.2 1.5 %collective-permute-start.1 = (s32[4,512]{1,0:T(4,128)S(1)}, s32[4,512]{1,0:T(4,128)S(1)}, u32[]{:S(2)}, u32[]{:S(2)}) collective-permute-start(s32[4,512]{1,0:T(4,128)S(1)} %get-tuple-element.47), channel_id=1, source_target_pairs={{0,3},{1,0},{2,1},{3,2},{4,7},{5,4},{6,5},{7,6},{8,11},{9,8},{10,9... | collective-permute-start | bytes 24584 | tf_op jit(solution)/shard_map/ppermute | solution.py:118
  5.7 2.6 %collective-permute-start.2 = (s32[1,128,512]{2,1,0:T(8,128)S(1)}, s32[1,128,512]{2,1,0:T(8,128)S(1)}, u32[]{:S(2)}, u32[]{:S(2)}) collective-permute-start(s32[1,128,512]{2,1,0:T(8,128)S(1)} %get-tuple-element.48), channel_id=1, source_target_pairs={{0,4},{4,8},{8,12},{12,16},{16,20},{20,24},{24,28},{28,32},{32,36}... | collective-permute-start | bytes 786440 | tf_op jit(solution)/shard_map/ppermute | solution.py:118
  8.5 0.7 convert_bitcast_fusion
  9.2 0.7 broadcast_divide_fusion.table
  10.2 1.2 %copy-done.4 = f32[4,128,512]{2,1,0:T(8,128)S(1)} copy-done((f32[4,128,512]{2,1,0:T(8,128)S(1)}, f32[4,128,512]{2,1,0:T(8,128)}, u32[]{:S(2)}) %copy-start.4) | copy-done | bytes 1048600
  11.4 2.3 %shard_map.95 = (f32[4,128,512]{2,1,0:T(8,128)S(1)}, f32[4,128,512]{2,1,0:T(8,128)S(1)}, f32[4,136,512]{2,1,0:T(8,128)S(1)}, f32[3,128,512]{2,1,0:T(8,128)S(1)},...) custom-call(s32[4,128,512]{2,1,0:T(8,128)S(1)} %copy-done.2, ...), custom_call_target="tpu_custom_call" | custom-call | tf_op jit(solution)/shard_map/pallas_call | solution.py:182
  13.7 0.4 collective-permute-done.3.zhi
  14.1 1.1 %shard_map.97 = (f32[4,128,512]{2,1,0:T(8,128)S(1)}, f32[2,128,512]{2,1,0:T(8,128)S(1)}, f32[2,128,512]{2,1,0:T(8,128)S(1)}, f32[4,8,512]{2,1,0:T(8,128)S(1)}, f...) custom-call(f32[4]{0:T(128)S(1)} %broadcast_divide_fusion.table, ...), custom_call_target="tpu_custom_call" | custom-call | tf_op jit(solution)/shard_map/pallas_call | solution.py:238
  15.4 2.6 %collective-permute-start.6 = (f32[8,512]{1,0:T(8,128)S(1)}, f32[8,512]{1,0:T(8,128)S(1)}, u32[]{:S(2)}, u32[]{:S(2)}) collective-permute-start(f32[8,512]{1,0:T(8,128)S(1)} %get-tuple-element.57), channel_id=1, source_target_pairs={{0,3},{1,0},{2,1},{3,2},{4,7},{5,4},{6,5},{7,6},{8,11},{9,8},{10,9... | collective-permute-start | bytes 49160 | tf_op jit(solution)/shard_map/ppermute | solution.py:118
  18.0 0.5 collective-permute-start.5
  18.5 0.4 shard_map.98.part
  18.9 3.1 %collective-permute-done.5.two = f32[4,512]{1,0:T(4,128)S(1)} collective-permute-done((f32[4,512]{1,0:T(4,128)S(1)}, f32[4,512]{1,0:T(4,128)S(1)}, u32[]{:S(2)}, u32[]{:S(2)}) %collective-permute-start.5) | collective-permute-done | bytes 8224 | tf_op jit(solution)/shard_map/ppermute | solution.py:118
  22.0 0.7 shard_map.99
  22.7 2.9 %collective-permute-start.7 = (f32[1,128,512]{2,1,0:T(8,128)S(1)}, f32[1,128,512]{2,1,0:T(8,128)S(1)}, u32[]{:S(2)}, u32[]{:S(2)}) collective-permute-start(f32[1,128,512]{2,1,0:T(8,128)S(1)} %get-tuple-element.69), channel_id=1, source_target_pairs={{0,4},{4,8},{8,12},{12,16},{16,20},{20,24},{24,28},{28,32},{32,36}... | collective-permute-start | bytes 786440 | tf_op jit(solution)/shard_map/ppermute | solution.py:118
  25.7 3.9 %collective-permute-start.8 = (f32[1,128,512]{2,1,0:T(8,128)S(1)}, f32[1,128,512]{2,1,0:T(8,128)S(1)}, u32[]{:S(2)}, u32[]{:S(2)}) collective-permute-start(f32[1,128,512]{2,1,0:T(8,128)S(1)} %get-tuple-element.70), channel_id=1, source_target_pairs={{0,252},{4,0},{8,4},{12,8},{16,12},{20,16},{24,20},{28,24},{32,28}... | collective-permute-start | bytes 786440 | tf_op jit(solution)/shard_map/ppermute | solution.py:118
  29.6 2.2 %shard_map.100 = (f32[4,128,512]{2,1,0:T(8,128)S(1)}, f32[4,128,512]{2,1,0:T(8,128)S(1)}, f32[2,128,512]{2,1,0:T(8,128)S(1)}, f32[4,512]{1,0:T(4,128)S(1)}, f32[...) custom-call(f32[4,128,512]{2,1,0:T(8,128)S(1)} %shard_map.98.part, ...), custom_call_target="tpu_custom_call" | custom-call | tf_op jit(solution)/shard_map/pallas_call | solution.py:441
  31.8 0.3 shard_map.101
  32.4 1.3 %collective-permute-start.10 = (f32[4,512]{1,0:T(4,128)S(1)}, f32[4,512]{1,0:T(4,128)S(1)}, u32[]{:S(2)}, u32[]{:S(2)}) collective-permute-start(f32[4,512]{1,0:T(4,128)S(1)} %get-tuple-element.76), channel_id=1, source_target_pairs={{0,2},{1,3},{2,0},{3,1},{4,6},{5,7},{6,4},{7,5},{8,10},{9,11},{10,... | collective-permute-start | bytes 24584 | tf_op jit(solution)/shard_map/ppermute | solution.py:118
  33.7 1.3 %collective-permute-start.11 = (f32[4,512]{1,0:T(4,128)S(1)}, f32[4,512]{1,0:T(4,128)S(1)}, u32[]{:S(2)}, u32[]{:S(2)}) collective-permute-start(f32[4,512]{1,0:T(4,128)S(1)} %get-tuple-element.77), channel_id=1, source_target_pairs={{0,3},{1,0},{2,1},{3,2},{4,7},{5,4},{6,5},{7,6},{8,11},{9,8},{10,9... | collective-permute-start | bytes 24584 | tf_op jit(solution)/shard_map/ppermute | solution.py:118
  35.1 0.4 shard_map.102.part
  35.5 0.9 %collective-permute-done.9.one = f32[4,512]{1,0:T(4,128)S(1)} collective-permute-done((f32[4,512]{1,0:T(4,128)S(1)}, f32[4,512]{1,0:T(4,128)S(1)}, u32[]{:S(2)}, u32[]{:S(2)}) %collective-permute-start.9) | collective-permute-done | bytes 8224 | tf_op jit(solution)/shard_map/ppermute | solution.py:118
  36.4 0.4 collective-permute-done.10.two
  36.8 0.3 collective-permute-done.11.three
  37.1 0.7 shard_map.103
  37.8 0.9 %collective-permute-start.12 = (f32[1,128,512]{2,1,0:T(8,128)S(1)}, f32[1,128,512]{2,1,0:T(8,128)S(1)}, u32[]{:S(2)}, u32[]{:S(2)}) collective-permute-start(f32[1,128,512]{2,1,0:T(8,128)S(1)} %get-tuple-element.82), channel_id=1, source_target_pairs={{0,4},{4,8},{8,12},{12,16},{16,20},{20,24},{24,28},{28,32},{32,36}... | collective-permute-start | bytes 786440 | tf_op jit(solution)/shard_map/ppermute | solution.py:118
  38.6 7.2 %collective-permute-start.13 = (f32[1,128,512]{2,1,0:T(8,128)S(1)}, f32[1,128,512]{2,1,0:T(8,128)S(1)}, u32[]{:S(2)}, u32[]{:S(2)}) collective-permute-start(f32[1,128,512]{2,1,0:T(8,128)S(1)} %get-tuple-element.83), channel_id=1, source_target_pairs={{0,252},{4,0},{8,4},{12,8},{16,12},{20,16},{24,20},{28,24},{32,28}... | collective-permute-start | bytes 786440 | tf_op jit(solution)/shard_map/ppermute | solution.py:118
  45.9 2.3 %shard_map.104 = (f32[4,128,512]{2,1,0:T(8,128)S(1)}, f32[4,128,512]{2,1,0:T(8,128)S(1)}, f32[1,128]{1,0:T(1,128)S(1)}) custom-call(f32[4,128,512]{2,1,0:T(8,128)S(1)} %shard_map.102.part, f32[4,128,512]{2,1,0:T(8,128)S(1)} %get-tuple-element.54.s, f32[2,128,512]{2,1,0:T(8,128)S(1)} %get-tuple-element.73.xo, f32[2,128,512]{2,1,0:T(8,128)S(1)} %get-tuple-element.74.xm, ...), custom_call_target="tpu_custom_call" | custom-call | tf_op jit(solution)/shard_map/pallas_call | solution.py:448
  48.2 0.3 shard_map.105
  48.6 28.3 %all_to_all.8 = f32[256,1,128]{2,1,0:T(1,128)S(1)} all-to-all(f32[256,1,128]{2,1,0:T(1,128)S(1)} %broadcast_in_dim.9), channel_id=1, replica_groups=mesh['gz'=64,'gy'=4] {'gz','gy'}, dimensions={0} | all-to-all | bytes 262144 | tf_op jit(solution)/shard_map/all_to_all | solution.py:453
  76.9 1.6 %shard_map.106 = (f32[4,128,512]{2,1,0:T(8,128)}, f32[4,128,512]{2,1,0:T(8,128)}) custom-call(f32[256,128]{1,0:T(8,128)S(1)} %bitcast.4, f32[4,128,512]{2,1,0:T(8,128)S(1)} %get-tuple-element.64.p, f32[4,128,512]{2,1,0:T(8,128)S(1)} %get-tuple-element.80.w, f32[4,128,512]{2,1,0:T(8,128)S(1)} %get-tuple-element.65.q, ...), custom_call_target="tpu_custom_call" | custom-call | tf_op jit(solution)/shard_map/pallas_call | solution.py:455
  (27 shorter events, 1.1 us)
Async XLA Ops:
  0.6 1.2 %copy-start.1 = (s32[4,128,512]{2,1,0:T(8,128)S(1)}, s32[4,128,512]{2,1,0:T(8,128)}, u32[]{:S(2)}) copy-start(s32[4,128,512]{2,1,0:T(8,128)} %labels.3) | copy-start | bytes 3145732
  1.9 8.3 %copy-start.2 = (s32[4,128,512]{2,1,0:T(8,128)S(1)}, s32[4,128,512]{2,1,0:T(8,128)}, u32[]{:S(2)}) copy-start(s32[4,128,512]{2,1,0:T(8,128)} %labels.3) | copy-start | bytes 3145732
  1.9 8.3 %copy-start.6 = (f32[2]{0:T(128)S(1)}, f32[2]{0:T(128)}, u32[]{:S(2)}) copy-start(f32[2]{0:T(128)} %values.1) | copy-start | bytes 28
  2.0 11.7 %collective-permute-start = (s32[4,512]{1,0:T(4,128)S(1)}, s32[4,512]{1,0:T(4,128)S(1)}, u32[]{:S(2)}, u32[]{:S(2)}) collective-permute-start(s32[4,512]{1,0:T(4,128)S(1)} %get-tuple-element.46), channel_id=1, source_target_pairs={{0,1},{1,2},{2,3},{3,0},{4,5},{5,6},{6,7},{7,4},{8,9},{9,10},{10,1... | collective-permute-start | bytes 24584 | tf_op jit(solution)/shard_map/ppermute | solution.py:118
  4.2 9.5 %collective-permute-start.1 = (s32[4,512]{1,0:T(4,128)S(1)}, s32[4,512]{1,0:T(4,128)S(1)}, u32[]{:S(2)}, u32[]{:S(2)}) collective-permute-start(s32[4,512]{1,0:T(4,128)S(1)} %get-tuple-element.47), channel_id=1, source_target_pairs={{0,3},{1,0},{2,1},{3,2},{4,7},{5,4},{6,5},{7,6},{8,11},{9,8},{10,9... | collective-permute-start | bytes 24584 | tf_op jit(solution)/shard_map/ppermute | solution.py:118
  5.7 8.0 %collective-permute-start.2 = (s32[1,128,512]{2,1,0:T(8,128)S(1)}, s32[1,128,512]{2,1,0:T(8,128)S(1)}, u32[]{:S(2)}, u32[]{:S(2)}) collective-permute-start(s32[1,128,512]{2,1,0:T(8,128)S(1)} %get-tuple-element.48), channel_id=1, source_target_pairs={{0,4},{4,8},{8,12},{12,16},{16,20},{20,24},{24,28},{28,32},{32,36}... | collective-permute-start | bytes 786440 | tf_op jit(solution)/shard_map/ppermute | solution.py:118
  8.3 5.8 %collective-permute-start.3 = (s32[1,128,512]{2,1,0:T(8,128)S(1)}, s32[1,128,512]{2,1,0:T(8,128)S(1)}, u32[]{:S(2)}, u32[]{:S(2)}) collective-permute-start(s32[1,128,512]{2,1,0:T(8,128)S(1)} %get-tuple-element.49), channel_id=1, source_target_pairs={{0,252},{4,0},{8,4},{12,8},{16,12},{20,16},{24,20},{28,24},{32,28}... | collective-permute-start | bytes 786440 | tf_op jit(solution)/shard_map/ppermute | solution.py:118
  10.1 1.2 %copy-start.4 = (f32[4,128,512]{2,1,0:T(8,128)S(1)}, f32[4,128,512]{2,1,0:T(8,128)}, u32[]{:S(2)}) copy-start(f32[4,128,512]{2,1,0:T(8,128)} %source.1) | copy-start | bytes 3145732
  11.4 2.8 %copy-start = (f32[4,4,128,128]{3,2,1,0:T(8,128)S(1)}, f32[4,4,128,128]{3,2,1,0:T(8,128)}, u32[]{:S(2)}) copy-start(f32[4,4,128,128]{3,2,1,0:T(8,128)} %constant.9.clone.vectors) | copy-start | bytes 3145732
  14.1 4.3 %copy-start.3 = (bf16[4,128,384]{2,1,0:T(8,128)(2,1)S(1)}, bf16[4,128,384]{2,1,0:T(8,128)(2,1)}, u32[]{:S(2)}) copy-start(bf16[4,128,384]{2,1,0:T(8,128)(2,1)} %constant.8.clone.green) | copy-start | bytes 1179652
  15.2 6.8 %collective-permute-start.4 = (f32[8,512]{1,0:T(8,128)S(1)}, f32[8,512]{1,0:T(8,128)S(1)}, u32[]{:S(2)}, u32[]{:S(2)}) collective-permute-start(f32[8,512]{1,0:T(8,128)S(1)} %get-tuple-element.55), channel_id=1, source_target_pairs={{0,1},{1,2},{2,3},{3,0},{4,5},{5,6},{6,7},{7,4},{8,9},{9,10},{10,1... | collective-permute-start | bytes 49160 | tf_op jit(solution)/shard_map/ppermute | solution.py:118
  15.4 6.6 %collective-permute-start.6 = (f32[8,512]{1,0:T(8,128)S(1)}, f32[8,512]{1,0:T(8,128)S(1)}, u32[]{:S(2)}, u32[]{:S(2)}) collective-permute-start(f32[8,512]{1,0:T(8,128)S(1)} %get-tuple-element.57), channel_id=1, source_target_pairs={{0,3},{1,0},{2,1},{3,2},{4,7},{5,4},{6,5},{7,6},{8,11},{9,8},{10,9... | collective-permute-start | bytes 49160 | tf_op jit(solution)/shard_map/ppermute | solution.py:118
  18.0 4.0 %collective-permute-start.5 = (f32[4,512]{1,0:T(4,128)S(1)}, f32[4,512]{1,0:T(4,128)S(1)}, u32[]{:S(2)}, u32[]{:S(2)}) collective-permute-start(f32[4,512]{1,0:T(4,128)S(1)} %get-tuple-element.56), channel_id=1, source_target_pairs={{0,2},{1,3},{2,0},{3,1},{4,6},{5,7},{6,4},{7,5},{8,10},{9,11},{10,... | collective-permute-start | bytes 24584 | tf_op jit(solution)/shard_map/ppermute | solution.py:118
  18.5 3.5 %copy-start.5 = (f32[4,8]{1,0:T(4,128)S(1)}, f32[4,8]{1,0:T(4,128)}, u32[]{:S(2)}) copy-start(f32[4,8]{1,0:T(4,128)} %constant.10.clone.scalars) | copy-start | bytes 388
  22.7 9.1 %collective-permute-start.7 = (f32[1,128,512]{2,1,0:T(8,128)S(1)}, f32[1,128,512]{2,1,0:T(8,128)S(1)}, u32[]{:S(2)}, u32[]{:S(2)}) collective-permute-start(f32[1,128,512]{2,1,0:T(8,128)S(1)} %get-tuple-element.69), channel_id=1, source_target_pairs={{0,4},{4,8},{8,12},{12,16},{16,20},{20,24},{24,28},{28,32},{32,36}... | collective-permute-start | bytes 786440 | tf_op jit(solution)/shard_map/ppermute | solution.py:118
  25.7 6.1 %collective-permute-start.8 = (f32[1,128,512]{2,1,0:T(8,128)S(1)}, f32[1,128,512]{2,1,0:T(8,128)S(1)}, u32[]{:S(2)}, u32[]{:S(2)}) collective-permute-start(f32[1,128,512]{2,1,0:T(8,128)S(1)} %get-tuple-element.70), channel_id=1, source_target_pairs={{0,252},{4,0},{8,4},{12,8},{16,12},{20,16},{24,20},{28,24},{32,28}... | collective-permute-start | bytes 786440 | tf_op jit(solution)/shard_map/ppermute | solution.py:118
  32.1 4.3 %collective-permute-start.9 = (f32[4,512]{1,0:T(4,128)S(1)}, f32[4,512]{1,0:T(4,128)S(1)}, u32[]{:S(2)}, u32[]{:S(2)}) collective-permute-start(f32[4,512]{1,0:T(4,128)S(1)} %get-tuple-element.75), channel_id=1, source_target_pairs={{0,1},{1,2},{2,3},{3,0},{4,5},{5,6},{6,7},{7,4},{8,9},{9,10},{10,1... | collective-permute-start | bytes 24584 | tf_op jit(solution)/shard_map/ppermute | solution.py:118
  32.4 4.4 %collective-permute-start.10 = (f32[4,512]{1,0:T(4,128)S(1)}, f32[4,512]{1,0:T(4,128)S(1)}, u32[]{:S(2)}, u32[]{:S(2)}) collective-permute-start(f32[4,512]{1,0:T(4,128)S(1)} %get-tuple-element.76), channel_id=1, source_target_pairs={{0,2},{1,3},{2,0},{3,1},{4,6},{5,7},{6,4},{7,5},{8,10},{9,11},{10,... | collective-permute-start | bytes 24584 | tf_op jit(solution)/shard_map/ppermute | solution.py:118
  33.7 3.3 %collective-permute-start.11 = (f32[4,512]{1,0:T(4,128)S(1)}, f32[4,512]{1,0:T(4,128)S(1)}, u32[]{:S(2)}, u32[]{:S(2)}) collective-permute-start(f32[4,512]{1,0:T(4,128)S(1)} %get-tuple-element.77), channel_id=1, source_target_pairs={{0,3},{1,0},{2,1},{3,2},{4,7},{5,4},{6,5},{7,6},{8,11},{9,8},{10,9... | collective-permute-start | bytes 24584 | tf_op jit(solution)/shard_map/ppermute | solution.py:118
  37.8 10.4 %collective-permute-start.12 = (f32[1,128,512]{2,1,0:T(8,128)S(1)}, f32[1,128,512]{2,1,0:T(8,128)S(1)}, u32[]{:S(2)}, u32[]{:S(2)}) collective-permute-start(f32[1,128,512]{2,1,0:T(8,128)S(1)} %get-tuple-element.82), channel_id=1, source_target_pairs={{0,4},{4,8},{8,12},{12,16},{16,20},{20,24},{24,28},{28,32},{32,36}... | collective-permute-start | bytes 786440 | tf_op jit(solution)/shard_map/ppermute | solution.py:118
  38.6 9.5 %collective-permute-start.13 = (f32[1,128,512]{2,1,0:T(8,128)S(1)}, f32[1,128,512]{2,1,0:T(8,128)S(1)}, u32[]{:S(2)}, u32[]{:S(2)}) collective-permute-start(f32[1,128,512]{2,1,0:T(8,128)S(1)} %get-tuple-element.83), channel_id=1, source_target_pairs={{0,252},{4,0},{8,4},{12,8},{16,12},{20,16},{24,20},{28,24},{32,28}... | collective-permute-start | bytes 786440 | tf_op jit(solution)/shard_map/ppermute | solution.py:118

commit v3 on v2

--- a/solution.py
+++ b/solution.py
@@ -38,17 +38,18 @@
         columns = [near[own] / high, far[own] / flow, low * far[own] / norm, fhigh * near[own] / norm]
         vectors.append(np.stack([np.broadcast_to(c[:, None], (rows, 128)) for c in columns]))
         for k in range(1, parts):
-            if d >= k:
-                scalars[d, k] = math.cosh(theta * (d - k + 1) * rows) / low
+            other = d ^ k
+            if other < d:
+                scalars[d, k] = math.cosh(theta * (other + 1) * rows) / low
             else:
-                scalars[d, 4 + k] = math.cosh(theta * (total - (d - k + parts) * rows)) / fhigh
+                scalars[d, 4 + k] = math.cosh(theta * (total - other * rows)) / fhigh
     return np.stack(blocks), np.stack(vectors).astype(np.float32), scalars.astype(np.float32)
 
 
-def call(body, outs, ins, scratch=(), dtype=F32, out_space=VMEM):
+def call(body, outs, ins, scratch=(), out_space=VMEM):
     return pl.pallas_call(
         body,
-        out_shape=[jax.ShapeDtypeStruct(s, dtype) for s in outs],
+        out_shape=[s if hasattr(s, "dtype") else jax.ShapeDtypeStruct(s, F32) for s in outs],
         in_specs=ins,
         out_specs=[out_space] * len(outs),
         scratch_shapes=list(scratch),
@@ -114,13 +115,30 @@
     def pick(z, first, second):
         return first.at[outer.index(z)] if z in outer else second.at[middle.index(z)]
 
-    def ring(value, axis, size, step):
-        return lax.ppermute(value, axis, [(i, (i + step) % size) for i in range(size)])
-
-    def borders(labels, below_o, above_o, first_o, last_o, first, last, sems):
+    def swap(value, axis, size, partner):
+        return lax.ppermute(value, axis, [(i, partner(i) % size) for i in range(size)])
+
+    def inside(value):
+        return swap(value, "gz", layers, lambda i: i ^ 1)
+
+    def across(value):
+        def partner(i, j):
+            k = i + 1 if i % 2 else i - 1
+            return (k, j) if 0 <= k < layers else (i, j ^ 1)
+        pairs = [(i, j, *partner(i, j)) for i in range(layers) for j in range(parts)]
+        return lax.ppermute(value, ALL, [(i * parts + j, k * parts + m) for i, j, k, m in pairs])
+
+    def crosswise(value, step):
+        return swap(value, "gy", parts, lambda i: i ^ step)
+
+    def even(axis):
+        return lax.axis_index(axis) % 2 == 0
+
+    def borders(labels, in_o, out_o, one_o, three_o, first, last, sems):
+        top, bottom = jnp.int32(nz - 1), jnp.int32(0)
         copies = [
-            pltpu.make_async_copy(labels.at[pl.ds(0, 1)], below_o, sems.at[0]),
-            pltpu.make_async_copy(labels.at[pl.ds(nz - 1, 1)], above_o, sems.at[1]),
+            pltpu.make_async_copy(labels.at[pl.ds(jnp.where(even("gz"), top, bottom), 1)], in_o, sems.at[0]),
+            pltpu.make_async_copy(labels.at[pl.ds(jnp.where(even("gz"), bottom, top), 1)], out_o, sems.at[1]),
             pltpu.make_async_copy(labels.at[:, pl.ds(0, 8)], first, sems.at[2]),
             pltpu.make_async_copy(labels.at[:, pl.ds(ny - 8, 8)], last, sems.at[3]),
         ]
@@ -129,24 +147,34 @@
         for copy in copies:
             copy.wait()
         for z in range(nz):
-            first_o[z : z + 1, :] = first[z, 0:1, :]
-            last_o[z : z + 1, :] = last[z, 7:8, :]
-
-    below, above, first, last = call(
-        borders,
-        [plane, plane, (nz, nx), (nz, nx)],
-        [HBM],
-        [pltpu.VMEM(edge, jnp.int32)] * 2 + [pltpu.SemaphoreType.DMA((4,))],
-        jnp.int32,
+            low, high = first[z, 0:1, :], last[z, 7:8, :]
+            one_o[z : z + 1, :] = jnp.where(even("gy"), high, low)
+            three_o[z : z + 1, :] = jnp.where(even("gy"), low, high)
+
+    sent = [jax.ShapeDtypeStruct(shape, jnp.int32) for shape in (plane, plane, (nz, nx), (nz, nx))]
+    in_o, out_o, one, three = call(
+        borders, sent, [HBM], [pltpu.VMEM(edge, jnp.int32)] * 2 + [pltpu.SemaphoreType.DMA((4,))]
     )(labels)
-    table = 0.5 / phase_table
-    ylo, yhi = ring(last, "gy", parts, 1), ring(first, "gy", parts, -1)
-    zlo, zhi = ring(above, "gz", layers, 1), ring(below, "gz", layers, -1)
-    masks = collector_mask.astype(F32)[..., None]
-
-    def faces(labels, table, values, masks, source, k_o, fx_o, fy_o, fz_o, d_o, e_o, b_o, held, framed_k, sem):
+    out_o, in_o = across(out_o), inside(in_o)
+    one, three = crosswise(one, 1), crosswise(three, 3)
+
+    head = jnp.concatenate([phase_table, collector_value])
+    packed = jnp.concatenate(
+        [jnp.pad(head, (0, ny - head.shape[0]))[None], collector_mask.reshape(2 * nz, ny).astype(F32)]
+    )
+
+    def halves(settings):
+        return [wide(settings[n : n + 1, :], nx) for n in range(4)]
+
+    def faces(labels, packed, source, k_o, fx_o, fy_o, fz_o, d_o, e_o, b_o, settings, held, framed_k, sem):
         copy = pltpu.make_async_copy(source, held, sem)
         copy.start()
+        for n in range(6):
+            value = jnp.broadcast_to(packed[0:1, n : n + 1], (1, 128))
+            settings[n : n + 1, :] = 0.5 / value if n < 4 else value
+        columns = jnp.transpose(packed[1 : 2 * nz + 1, :])
+        table = halves(settings)
+        values = [settings[4 + n : 5 + n, :] for n in range(2)]
         for z in range(nz):
             for r in starts:
                 k = lookup(labels[z, rows_at(r), :], table)
@@ -172,19 +200,19 @@
                     fz = recip(k + k_o[z + 1, at, :])
                     fz_o[z, at, :] = fz
                     d = d + fz
-                low = jnp.where(side == 0, recip(k[:, :128]) * masks[0, z, at, :], 0.0)
-                high = jnp.where(side == 127, recip(k[:, -128:]) * masks[1, z, at, :], 0.0)
+                low = jnp.where(side == 0, recip(k[:, :128]) * columns[at, z : z + 1], 0.0)
+                high = jnp.where(side == 127, recip(k[:, -128:]) * columns[at, nz + z : nz + z + 1], 0.0)
                 e_o[z, at, :] = jnp.concatenate([low, high], axis=1)
                 d_o[z, at, :] = ends(d, low, high)
                 b_o[z, at, :] = ends(held[z, at, :], low * values[0], high * values[1])
                 fx_o[z, at, :] = fx
 
-    k, fx, fy, fz, d, e, b = call(
+    k, fx, fy, fz, d, e, b, settings = call(
         faces,
-        [block, block, (nz, ny + 8, nx), (nz - 1, ny, nx), block, (nz, ny, 256), block],
-        [VMEM, SMEM, SMEM, VMEM, HBM],
+        [block, block, (nz, ny + 8, nx), (nz - 1, ny, nx), block, (nz, ny, 256), block, (8, 128)],
+        [VMEM, VMEM, HBM],
         [pltpu.VMEM(block, F32), pltpu.VMEM(framed, F32), pltpu.SemaphoreType.DMA],
-    )(labels, table, collector_value, masks, source)
+    )(labels, packed, source)
 
     def weighted(x, my, vectors, r, carry):
         return (
@@ -195,19 +223,22 @@
     def sums_out(my, sums, z, outs):
         right, left = (jnp.sum(v, 0, keepdims=True) for v in sums)
         for step, out in enumerate(outs, 1):
-            out[z : z + 1, :] = jnp.where(my + step < parts, right, left)
+            out[z : z + 1, :] = jnp.where((my ^ step) > my, right, left)
 
     zero = lambda: jnp.zeros((8, nx), F32)
     none = lambda: jnp.zeros((8, 128), F32)
 
-    def scaled(table, k, ylo, yhi, zlo, zhi, d, b, vectors, s_o, xo_o, xm_o, fye_o, fze_o, one, two, three):
+    def scaled(settings, k, y_one, y_three, z_in, z_out, d, b, vectors, s_o, xo_o, xm_o, fye_o, fze_o, one, two, three):
         my, level = lax.axis_index("gy"), lax.axis_index("gz")
         has_low, has_high = (my > 0).astype(F32), (my < parts - 1).astype(F32)
         has_below, has_above = (level > 0).astype(F32), (level < layers - 1).astype(F32)
         sub = sublane((STEP, nx))
-        for z in range(nz):
-            first = has_low * recip(lookup(ylo[z : z + 1, :], table) + k[z, 0:1, :])
-            last = has_high * recip(lookup(yhi[z : z + 1, :], table) + k[z, ny - 1 : ny, :])
+        table = halves(settings)
+        for z in range(nz):
+            ones, threes = y_one[z : z + 1, :], y_three[z : z + 1, :]
+            ylo, yhi = jnp.where(even("gy"), threes, ones), jnp.where(even("gy"), ones, threes)
+            first = has_low * recip(lookup(ylo, table) + k[z, 0:1, :])
+            last = has_high * recip(lookup(yhi, table) + k[z, ny - 1 : ny, :])
             fye_o[z, 0:1, :] = first
             fye_o[z, 1:2, :] = last
             carry = (zero(), zero())
@@ -219,11 +250,11 @@
                 if r + STEP == ny:
                     diagonal = diagonal + jnp.where(sub == STEP - 1, last, 0.0)
                 if z == 0:
-                    face = has_below * recip(lookup(zlo[0, at, :], table) + k[z, at, :])
+                    face = has_below * recip(lookup(jnp.where(even("gz"), z_out[0, at, :], z_in[0, at, :]), table) + k[z, at, :])
                     fze_o[0, at, :] = face
                     diagonal = diagonal + face
                 if z == nz - 1:
-                    face = has_above * recip(lookup(zhi[0, at, :], table) + k[z, at, :])
+                    face = has_above * recip(lookup(jnp.where(even("gz"), z_in[0, at, :], z_out[0, at, :]), table) + k[z, at, :])
                     fze_o[1, at, :] = face
                     diagonal = diagonal + face
                 s = lax.rsqrt(diagonal)
@@ -232,14 +263,15 @@
                 pick(z, xo_o, xm_o)[at, :] = x
                 carry = weighted(x, my, vectors, r, carry)
             sums_out(my, carry, z, (one, two, three))
-            one[nz + z : nz + z + 1, :] = s_o[z, ny - 1 : ny, :]
-            three[nz + z : nz + z + 1, :] = s_o[z, 0:1, :]
+            low, high = s_o[z, 0:1, :], s_o[z, ny - 1 : ny, :]
+            one[nz + z : nz + z + 1, :] = jnp.where(even("gy"), high, low)
+            three[nz + z : nz + z + 1, :] = jnp.where(even("gy"), low, high)
 
     s, xo, xm, fye, fze, one, two, three = call(
         scaled,
         [block, ends_shape, middle_shape, edge, (2, ny, nx), (2 * nz, nx), (nz, nx), (2 * nz, nx)],
-        [SMEM] + [VMEM] * 8,
-    )(table, k, ylo, yhi, zlo, zhi, d, b, vectors)
+        [VMEM] * 9,
+    )(settings, k, one, three, in_o, out_o, d, b, vectors)
 
     def lines(xo, xm, green, out):
         my = lax.axis_index("gy")
@@ -250,31 +282,32 @@
             stack = jnp.concatenate([head, head, tail], axis=0)
             out[z] = jnp.dot(green[my], stack, preferred_element_type=F32)
 
-    def solve(z, part, s, xo, xm, vectors, scalars, one, two, three, below, above, put):
+    def solve(z, part, s, xo, xm, vectors, scalars, one, two, three, s_one, s_three, put):
         my = lax.axis_index("gy")
         got = [r[z : z + 1, :] for r in (one, two, three)]
         left = sum(scalars[my, n + 1] * got[n] for n in range(3))
         right = sum(scalars[my, 5 + n] * got[n] for n in range(3))
+        ones, threes = s_one[nz + z : nz + z + 1, :], s_three[nz + z : nz + z + 1, :]
         for r in starts:
             at = rows_at(r)
             g = part[z, at, :] + (wide(vectors[my, 2, at, :], nx) * left + wide(vectors[my, 3, at, :], nx) * right)
             put(r + 8, s[z, at, :] * g)
             if r == 0:
                 beside = (2.0 + SHIFT) * g[0:1] - g[1:2] - pick(z, xo, xm)[0:1, :]
-                put(7, below[nz + z : nz + z + 1, :] * beside)
+                put(7, jnp.where(even("gy"), threes, ones) * beside)
             if r + STEP == ny:
                 beside = (2.0 + SHIFT) * g[-1:] - g[-2:-1] - pick(z, xo, xm)[ny - 1 : ny, :]
-                put(ny + 8, above[nz + z : nz + z + 1, :] * beside)
-
-    def solve_outer(part, s, xo, xm, vectors, scalars, one, two, three, below, above, p_o, low_o, high_o):
+                put(ny + 8, jnp.where(even("gy"), ones, threes) * beside)
+
+    def solve_outer(part, s, xo, xm, vectors, scalars, one, two, three, s_one, s_three, p_o, in_o, out_o):
         for n, z in enumerate(outer):
             def put(r, value):
                 p_o[n, r : r + value.shape[0], :] = value
-                if z == 0 and value.shape[0] == STEP:
-                    low_o[0, rows_at(r - 8), :] = value
-                if z == nz - 1 and value.shape[0] == STEP:
-                    high_o[0, rows_at(r - 8), :] = value
-            solve(z, part, s, xo, xm, vectors, scalars, one, two, three, below, above, put)
+            solve(z, part, s, xo, xm, vectors, scalars, one, two, three, s_one, s_three, put)
+        top = jnp.where(even("gz"), 1, 0)
+        for r in starts:
+            in_o[0, rows_at(r), :] = p_o[top, rows_at(r + 8), :]
+            out_o[0, rows_at(r), :] = p_o[1 - top, rows_at(r + 8), :]
 
     def total(value):
         return jnp.sum(jnp.sum(value, 0, keepdims=True), 1, keepdims=True)
@@ -304,13 +337,13 @@
         edges = e[z, at, :]
         return v, ends(q, edges[:, :128] * v[:, :128], edges[:, 128:] * v[:, -128:])
 
-    def fill(part, s, xo, xm, vectors, scalars, one, two, three, below, above, p_outer, p_o, field):
+    def fill(part, s, xo, xm, vectors, scalars, one, two, three, s_one, s_three, p_outer, p_o, field):
         for z in middle:
             def put(r, value):
                 field[z, r : r + value.shape[0], :] = value
                 if value.shape[0] == STEP:
                     p_o[z, rows_at(r - 8), :] = value
-            solve(z, part, s, xo, xm, vectors, scalars, one, two, three, below, above, put)
+            solve(z, part, s, xo, xm, vectors, scalars, one, two, three, s_one, s_three, put)
         for n, z in enumerate(outer):
             for r in starts:
                 p_o[z, rows_at(r), :] = p_outer[n, rows_at(r + 8), :]
@@ -319,10 +352,10 @@
             return p_outer[outer.index(z), rows_at(r), :] if z in outer else field[z, rows_at(r), :]
         return read
 
-    def inner_first(part, s, xo, xm, vectors, scalars, one, two, three, below, above, p_outer, fx, fy, fz, fye, e, b,
+    def inner_first(part, s, xo, xm, vectors, scalars, one, two, three, s_one, s_three, p_outer, fx, fy, fz, fye, e, b,
                     p_o, q_o, xm_o, one_o, two_o, three_o, dots, field):
         my = lax.axis_index("gy")
-        read = fill(part, s, xo, xm, vectors, scalars, one, two, three, below, above, p_outer, p_o, field)
+        read = fill(part, s, xo, xm, vectors, scalars, one, two, three, s_one, s_three, p_outer, p_o, field)
         bp, pq = none(), none()
         for z in outer + middle:
             carry = (zero(), zero())
@@ -343,15 +376,15 @@
     def image_of(z, ends, whole, at):
         return ends[outer.index(z), at, :] if z in outer else whole[z, at, :]
 
-    def outside(z, r, v, image, zlo, zhi, fze):
+    def outside(z, r, v, image, z_in, z_out, fze):
         at = rows_at(r)
         if z == 0:
-            image = image + fze[0, at, :] * (v - zlo[0, at, :])
+            image = image + fze[0, at, :] * (v - jnp.where(even("gz"), z_out[0, at, :], z_in[0, at, :]))
         if z == nz - 1:
-            image = image + fze[1, at, :] * (v - zhi[0, at, :])
+            image = image + fze[1, at, :] * (v - jnp.where(even("gz"), z_in[0, at, :], z_out[0, at, :]))
         return image
 
-    def outer_first(p, q, one, two, three, zlo, zhi, fze, s, vectors, dots, qo_o, xo_o, one_o, two_o, three_o, dots_o):
+    def outer_first(p, q, one, two, three, z_in, z_out, fze, s, vectors, dots, qo_o, xo_o, one_o, two_o, three_o, dots_o):
         my = lax.axis_index("gy")
         pq = none()
         for z in outer:
@@ -359,7 +392,7 @@
             for r in starts:
                 at = rows_at(r)
                 v = p[z, at, :]
-                image = outside(z, r, v, q[z, at, :], zlo, zhi, fze)
+                image = outside(z, r, v, q[z, at, :], z_in, z_out, fze)
                 scaled_image = s[z, at, :] * image
                 qo_o[outer.index(z), at, :] = image
                 xo_o[outer.index(z), at, :] = scaled_image
@@ -372,9 +405,9 @@
         dots_out(dots_o, (none(), pq), 0)
         dots_o[...] = dots_o[...] + dots[...]
 
-    def inner_last(part, s, xo, xm, vectors, scalars, one, two, three, below, above, p_outer, fx, fy, fz, fye, e, b, q, qo,
+    def inner_last(part, s, xo, xm, vectors, scalars, one, two, three, s_one, s_three, p_outer, fx, fy, fz, fye, e, b, q, qo,
                    w_o, v_o, dots, field):
-        read = fill(part, s, xo, xm, vectors, scalars, one, two, three, below, above, p_outer, w_o, field)
+        read = fill(part, s, xo, xm, vectors, scalars, one, two, three, s_one, s_three, p_outer, w_o, field)
         bw, qw, wv = none(), none(), none()
         for z in range(nz):
             for r in starts:
@@ -386,13 +419,13 @@
                 v_o[z, at, :] = image
         dots_out(dots, (bw, qw, wv), 2)
 
-    def outer_last(w, v, zlo, zhi, fze, dots_first, dots, v_o, dots_o):
+    def outer_last(w, v, z_in, z_out, fze, dots_first, dots, v_o, dots_o):
         wv = none()
         for n, z in enumerate(outer):
             for r in starts:
                 at = rows_at(r)
                 field, image = w[z, at, :], v[z, at, :]
-                full = outside(z, r, field, image, zlo, zhi, fze)
+                full = outside(z, r, field, image, z_in, z_out, fze)
                 v_o[n, at, :] = full
                 wv = wv + folded((full - image) * field)
         dots_out(dots_o, (wv,), 4)
@@ -422,7 +455,7 @@
             copy.wait()
 
     def gather(sums):
-        return [ring(v, "gy", parts, n) for n, v in enumerate(sums, 1)]
+        return [crosswise(v, n) for n, v in enumerate(sums, 1)]
 
     field = [pltpu.VMEM(framed, F32)]
     rows = [(nz, nx)] * 3
@@ -433,22 +466,23 @@
         beside = beside or (got[0], got[2])
         part = call(lines, [block], [VMEM] * 3)(xo, xm, green)[0]
         known = (part, s, xo, xm, vectors, scalars, *got, *beside)
-        pair, low, high = call(solve_outer, [framed_pair, plane, plane], places)(*known)
-        return (*known, pair), ring(high, "gz", layers, 1), ring(low, "gz", layers, -1), beside
+        pair, in_o, out_o = call(solve_outer, [framed_pair, plane, plane], places)(*known)
+        out_o = across(out_o)
+        return (*known, pair), inside(in_o), out_o, beside
 
     places = [VMEM] * 5 + [SMEM] + [VMEM] * 5
-    known, zlo, zhi, beside = start(xo, xm, (one, two, three), None)
+    known, z_in, z_out, beside = start(xo, xm, (one, two, three), None)
     p, q, xm, *sums, dots = call(
         inner_first, [block, block, middle_shape, *rows, (1, 128)], places + [VMEM] * 7, field
     )(*known, fx, fy, fz, fye, e, b)
     qo, xo, *sums, dots = call(outer_first, [ends_shape, ends_shape, *rows, (1, 128)], [VMEM] * 11)(
-        p, q, *sums, zlo, zhi, fze, s, vectors, dots
+        p, q, *sums, z_in, z_out, fze, s, vectors, dots
     )
-    known, zlo, zhi, _ = start(xo, xm, sums, beside)
+    known, z_in, z_out, _ = start(xo, xm, sums, beside)
     w, v, last_dots = call(inner_last, [block, block, (1, 128)], places + [VMEM] * 9, field)(
         *known, fx, fy, fz, fye, e, b, q, qo
     )
-    vo, dots = call(outer_last, [ends_shape, (1, 128)], [VMEM] * 7)(w, v, zlo, zhi, fze, last_dots, dots)
+    vo, dots = call(outer_last, [ends_shape, (1, 128)], [VMEM] * 7)(w, v, z_in, z_out, fze, last_dots, dots)
     count = parts * layers
     gathered = lax.all_to_all(jnp.broadcast_to(dots, (count, 128)), ALL, 0, 0, tiled=True)
     return tuple(

time: 78.8 us -> 72.3 us (0.918)
  starting transfers between devices: 27.7 us -> 19.4 us
  waiting for transfers between devices: 5.02 us -> 10.1 us
  local copies, waits for them, and re-layouts: 2.75 us -> 1.31 us
  blocking collectives: 28.3 us -> 27.2 us
  Pallas kernels: 12.6 us -> 11.7 us
    ppermute x14, starting transfers between devices: 27.7 us -> 19.4 us  [the longest x11 18.2 us: swap(): lax.ppermute(value, axis, [(i, partner(i) % size) for i in range(size)])]
    ppermute x14, waiting for transfers between devices: 5.02 us -> 10.1 us  [the longest x3 6.44 us: across(): lax.ppermute(value, ALL, [(i * parts + j, k * parts + m) for i, j, k, m i...]
    unnamed x14 -> x10, local copies, waits for them, and re-layouts: 2.46 us -> 1.24 us
    all_to_all x1, blocking collectives: 28.3 us -> 27.2 us  [local(): lax.all_to_all(jnp.broadcast_to(dots, (count, 128)), ALL, 0, 0, tiled=True)]
where the time goes in v3:
time: 72.3 us; the launch traced here: 72.1 us
  blocking collectives  27.2 us (38%)
  starting transfers between devices  19.4 us (27%)
  Pallas kernels  11.7 us (16%)
  waiting for transfers between devices  10.1 us (14%)
  other arithmetic  1.44 us (2%)
  local copies, waits for them, and re-layouts  1.31 us (2%)
  between operations  0.93 us (1%)
    all_to_all x1, blocking collectives, local(): lax.all_to_all(jnp.broadcast_to(dots, (count, 128)), ALL, 0, 0, tiled=True)  27.2 us
    ppermute x11, starting transfers between devices, swap(): lax.ppermute(value, axis, [(i, partner(i) % size) for i in range(size)])  18.2 us
    ppermute x3, waiting for transfers between devices, across(): lax.ppermute(value, ALL, [(i * parts + j, k * parts + m) for i, j, k, m i...  6.44 us
    ppermute x11, waiting for transfers between devices, swap(): lax.ppermute(value, axis, [(i, partner(i) % size) for i in range(size)])  3.62 us
    pallas_call x1, Pallas kernels, local(): call(inner_last, [block, block, (1, 128)], places + [VMEM] * 9, field)  2.29 us
    pallas_call x1, Pallas kernels, local(): call(inner_first, [block, block, middle_shape, *rows, (1, 128)], places +...  2.22 us
    pallas_call x1, Pallas kernels, local(): call(faces, [block, block, (nz, ny + 8, nx), (nz - 1, ny, nx), block, (nz...  1.78 us
    pallas_call x1, Pallas kernels, local(): call(combine, [block, block], [VMEM] * 8, [pltpu.VMEM(block, F32)] * 2 +...  1.59 us
  transfers between devices with their start and end apart: 14, of which 5 were waited for; matrix products, arithmetic and copies ran while one was open for 2% of the time, Pallas kernels for 10%

profile of v3, /device:TPU:1, one launch (start us, length us, event | category | flops | bytes accessed | tf_op | source)
XLA Modules:
  0.0 72.1 jit_solution(2274537158552851003)
XLA Ops:
  0.6 1.2 %copy-done.1 = s32[4,128,512]{2,1,0:T(8,128)S(1)} copy-done((s32[4,128,512]{2,1,0:T(8,128)S(1)}, s32[4,128,512]{2,1,0:T(8,128)}, u32[]{:S(2)}) %copy-start.1) | copy-done | bytes 1048600
  2.0 3.3 %collective-permute-start.2 = (s32[1,128,512]{2,1,0:T(8,128)S(1)}, s32[1,128,512]{2,1,0:T(8,128)S(1)}, u32[]{:S(2)}, u32[]{:S(2)}) collective-permute-start(s32[1,128,512]{2,1,0:T(8,128)S(1)} %get-tuple-element.50), channel_id=1, source_target_pairs={{0,4},{4,0},{8,12},{12,8},{16,20},{20,16},{24,28},{28,24},{32,36},... | collective-permute-start | bytes 786440 | tf_op jit(solution)/shard_map/ppermute | solution.py:119
  5.3 1.2 %collective-permute-start = (s32[4,512]{1,0:T(4,128)S(1)}, s32[4,512]{1,0:T(4,128)S(1)}, u32[]{:S(2)}, u32[]{:S(2)}) collective-permute-start(s32[4,512]{1,0:T(4,128)S(1)} %get-tuple-element.48), channel_id=1, source_target_pairs={{0,1},{1,0},{2,3},{3,2},{4,5},{5,4},{6,7},{7,6},{8,9},{9,8},{10,11... | collective-permute-start | bytes 24584 | tf_op jit(solution)/shard_map/ppermute | solution.py:119
  6.5 1.9 %collective-permute-start.1 = (s32[4,512]{1,0:T(4,128)S(1)}, s32[4,512]{1,0:T(4,128)S(1)}, u32[]{:S(2)}, u32[]{:S(2)}) collective-permute-start(s32[4,512]{1,0:T(4,128)S(1)} %get-tuple-element.49), channel_id=1, source_target_pairs={{0,3},{1,2},{2,1},{3,0},{4,7},{5,6},{6,5},{7,4},{8,11},{9,10},{10,... | collective-permute-start | bytes 24584 | tf_op jit(solution)/shard_map/ppermute | solution.py:119
  8.4 0.7 convert_element_type.8
  9.1 0.7 %fusion.1 = f32[1,128]{1,0:T(1,128)S(1)} fusion(f32[2]{0:T(128)} %param.11, f32[4]{0:T(128)} %param.9), kind=kLoop, calls=%fused_computation.4 | loop fusion | flops 512 | bytes 536 | tf_op jit(solution)/shard_map/broadcast_in_dim | solution.py:163
  9.9 1.8 %shard_map.95 = (f32[4,128,512]{2,1,0:T(8,128)S(1)}, f32[4,128,512]{2,1,0:T(8,128)S(1)}, f32[4,136,512]{2,1,0:T(8,128)S(1)}, f32[3,128,512]{2,1,0:T(8,128)S(1)},...) custom-call(s32[4,128,512]{2,1,0:T(8,128)S(1)} %copy-done.1, ...), custom_call_target="tpu_custom_call" | custom-call | tf_op jit(solution)/shard_map/pallas_call | solution.py:210
  11.7 0.6 shard_map.97
  12.3 0.5 collective-permute-start.4
  12.8 0.8 %collective-permute-start.6 = (f32[8,512]{1,0:T(8,128)S(1)}, f32[8,512]{1,0:T(8,128)S(1)}, u32[]{:S(2)}, u32[]{:S(2)}) collective-permute-start(f32[8,512]{1,0:T(8,128)S(1)} %get-tuple-element.59), channel_id=1, source_target_pairs={{0,3},{1,2},{2,1},{3,0},{4,7},{5,6},{6,5},{7,4},{8,11},{9,10},{10,... | collective-permute-start | bytes 49160 | tf_op jit(solution)/shard_map/ppermute | solution.py:119
  13.6 2.1 %collective-permute-start.5 = (f32[4,512]{1,0:T(4,128)S(1)}, f32[4,512]{1,0:T(4,128)S(1)}, u32[]{:S(2)}, u32[]{:S(2)}) collective-permute-start(f32[4,512]{1,0:T(4,128)S(1)} %get-tuple-element.58), channel_id=1, source_target_pairs={{0,2},{1,3},{2,0},{3,1},{4,6},{5,7},{6,4},{7,5},{8,10},{9,11},{10,... | collective-permute-start | bytes 24584 | tf_op jit(solution)/shard_map/ppermute | solution.py:119
  15.7 0.5 shard_map.98.part
  16.1 1.5 %collective-permute-done.5.two = f32[4,512]{1,0:T(4,128)S(1)} collective-permute-done((f32[4,512]{1,0:T(4,128)S(1)}, f32[4,512]{1,0:T(4,128)S(1)}, u32[]{:S(2)}, u32[]{:S(2)}) %collective-permute-start.5) | collective-permute-done | bytes 8224 | tf_op jit(solution)/shard_map/ppermute | solution.py:119
  17.6 0.7 %shard_map.99 = (f32[2,144,512]{2,1,0:T(8,128)S(1)}, f32[1,128,512]{2,1,0:T(8,128)S(1)}, f32[1,128,512]{2,1,0:T(8,128)S(1)}) custom-call(f32[4,128,512]{2,1,0:T(8,128)S(1)} %shard_map.98.part, f32[4,128,512]{2,1,0:T(8,128)S(1)} %get-tuple-element.56.s, f32[2,128,512]{2,1,0:T(8,128)S(1)} %get-tuple-element.54.xo, f32[2,128,512]{2,1,0:T(8,128)S(1)} %get-tuple-element.55.xm, ...), custom_call_target="tpu_custom_call" | custom-call | tf_op jit(solution)/shard_map/pallas_call | solution.py:469
  18.3 2.4 %collective-permute-start.7 = (f32[1,128,512]{2,1,0:T(8,128)S(1)}, f32[1,128,512]{2,1,0:T(8,128)S(1)}, u32[]{:S(2)}, u32[]{:S(2)}) collective-permute-start(f32[1,128,512]{2,1,0:T(8,128)S(1)} %get-tuple-element.71), channel_id=1, source_target_pairs={{0,4},{4,0},{8,12},{12,8},{16,20},{20,16},{24,28},{28,24},{32,36},... | collective-permute-start | bytes 786440 | tf_op jit(solution)/shard_map/ppermute | solution.py:119
  20.8 1.0 %collective-permute-start.8 = (f32[1,128,512]{2,1,0:T(8,128)S(1)}, f32[1,128,512]{2,1,0:T(8,128)S(1)}, u32[]{:S(2)}, u32[]{:S(2)}) collective-permute-start(f32[1,128,512]{2,1,0:T(8,128)S(1)} %get-tuple-element.72), channel_id=1, source_target_pairs={{0,1},{1,0},{2,3},{3,2},{4,8},{5,9},{6,10},{7,11},{8,4},{9,5},{10,... | collective-permute-start | bytes 786440 | tf_op jit(solution)/shard_map/ppermute | solution.py:129
  21.8 2.2 %shard_map.100 = (f32[4,128,512]{2,1,0:T(8,128)S(1)}, f32[4,128,512]{2,1,0:T(8,128)S(1)}, f32[2,128,512]{2,1,0:T(8,128)S(1)}, f32[4,512]{1,0:T(4,128)S(1)}, f32[...) custom-call(f32[4,128,512]{2,1,0:T(8,128)S(1)} %shard_map.98.part, ...), custom_call_target="tpu_custom_call" | custom-call | tf_op jit(solution)/shard_map/pallas_call | solution.py:475
  24.0 2.8 %collective-permute-done.8.z_out = f32[1,128,512]{2,1,0:T(8,128)S(1)} collective-permute-done((f32[1,128,512]{2,1,0:T(8,128)S(1)}, f32[1,128,512]{2,1,0:T(8,128)S(1)}, u32[]{:S(2)}, u32[]{:S(2)}) %collective-permute-start.8) | collective-permute-done | bytes 262176 | tf_op jit(solution)/shard_map/ppermute | solution.py:129
  26.9 0.3 shard_map.101
  27.2 1.1 %collective-permute-start.9 = (f32[4,512]{1,0:T(4,128)S(1)}, f32[4,512]{1,0:T(4,128)S(1)}, u32[]{:S(2)}, u32[]{:S(2)}) collective-permute-start(f32[4,512]{1,0:T(4,128)S(1)} %get-tuple-element.77), channel_id=1, source_target_pairs={{0,1},{1,0},{2,3},{3,2},{4,5},{5,4},{6,7},{7,6},{8,9},{9,8},{10,11... | collective-permute-start | bytes 24584 | tf_op jit(solution)/shard_map/ppermute | solution.py:119
  28.3 1.5 %collective-permute-start.10 = (f32[4,512]{1,0:T(4,128)S(1)}, f32[4,512]{1,0:T(4,128)S(1)}, u32[]{:S(2)}, u32[]{:S(2)}) collective-permute-start(f32[4,512]{1,0:T(4,128)S(1)} %get-tuple-element.78), channel_id=1, source_target_pairs={{0,2},{1,3},{2,0},{3,1},{4,6},{5,7},{6,4},{7,5},{8,10},{9,11},{10,... | collective-permute-start | bytes 24584 | tf_op jit(solution)/shard_map/ppermute | solution.py:119
  29.8 1.4 %collective-permute-start.11 = (f32[4,512]{1,0:T(4,128)S(1)}, f32[4,512]{1,0:T(4,128)S(1)}, u32[]{:S(2)}, u32[]{:S(2)}) collective-permute-start(f32[4,512]{1,0:T(4,128)S(1)} %get-tuple-element.79), channel_id=1, source_target_pairs={{0,3},{1,2},{2,1},{3,0},{4,7},{5,6},{6,5},{7,4},{8,11},{9,10},{10,... | collective-permute-start | bytes 24584 | tf_op jit(solution)/shard_map/ppermute | solution.py:119
  31.2 0.5 shard_map.102.part
  31.6 0.7 collective-permute-done.10.two
  32.3 1.4 %collective-permute-done.11.three = f32[4,512]{1,0:T(4,128)S(1)} collective-permute-done((f32[4,512]{1,0:T(4,128)S(1)}, f32[4,512]{1,0:T(4,128)S(1)}, u32[]{:S(2)}, u32[]{:S(2)}) %collective-permute-start.11) | collective-permute-done | bytes 8224 | tf_op jit(solution)/shard_map/ppermute | solution.py:119
  33.8 0.7 %shard_map.103 = (f32[2,144,512]{2,1,0:T(8,128)S(1)}, f32[1,128,512]{2,1,0:T(8,128)S(1)}, f32[1,128,512]{2,1,0:T(8,128)S(1)}) custom-call(f32[4,128,512]{2,1,0:T(8,128)S(1)} %shard_map.102.part, f32[4,128,512]{2,1,0:T(8,128)S(1)} %get-tuple-element.56.s, f32[2,128,512]{2,1,0:T(8,128)S(1)} %get-tuple-element.75.xo, f32[2,128,512]{2,1,0:T(8,128)S(1)} %get-tuple-element.76.xm, ...), custom_call_target="tpu_custom_call" | custom-call | tf_op jit(solution)/shard_map/pallas_call | solution.py:469
  34.5 2.1 %collective-permute-start.12 = (f32[1,128,512]{2,1,0:T(8,128)S(1)}, f32[1,128,512]{2,1,0:T(8,128)S(1)}, u32[]{:S(2)}, u32[]{:S(2)}) collective-permute-start(f32[1,128,512]{2,1,0:T(8,128)S(1)} %get-tuple-element.84), channel_id=1, source_target_pairs={{0,4},{4,0},{8,12},{12,8},{16,20},{20,16},{24,28},{28,24},{32,36},... | collective-permute-start | bytes 786440 | tf_op jit(solution)/shard_map/ppermute | solution.py:119
  36.8 2.3 %shard_map.104 = (f32[4,128,512]{2,1,0:T(8,128)S(1)}, f32[4,128,512]{2,1,0:T(8,128)S(1)}, f32[1,128]{1,0:T(1,128)S(1)}) custom-call(f32[4,128,512]{2,1,0:T(8,128)S(1)} %shard_map.102.part, f32[4,128,512]{2,1,0:T(8,128)S(1)} %get-tuple-element.56.s, f32[2,128,512]{2,1,0:T(8,128)S(1)} %get-tuple-element.75.xo, f32[2,128,512]{2,1,0:T(8,128)S(1)} %get-tuple-element.76.xm, ...), custom_call_target="tpu_custom_call" | custom-call | tf_op jit(solution)/shard_map/pallas_call | solution.py:482
  39.1 3.6 %collective-permute-done.13.z_out = f32[1,128,512]{2,1,0:T(8,128)S(1)} collective-permute-done((f32[1,128,512]{2,1,0:T(8,128)S(1)}, f32[1,128,512]{2,1,0:T(8,128)S(1)}, u32[]{:S(2)}, u32[]{:S(2)}) %collective-permute-start.13) | collective-permute-done | bytes 262176 | tf_op jit(solution)/shard_map/ppermute | solution.py:129
  42.7 0.3 shard_map.105
  43.1 27.2 %all_to_all.8 = f32[256,1,128]{2,1,0:T(1,128)S(1)} all-to-all(f32[256,1,128]{2,1,0:T(1,128)S(1)} %broadcast_in_dim.9), channel_id=1, replica_groups=mesh['gz'=64,'gy'=4] {'gz','gy'}, dimensions={0} | all-to-all | bytes 262144 | tf_op jit(solution)/shard_map/all_to_all | solution.py:487
  70.3 1.6 %shard_map.106 = (f32[4,128,512]{2,1,0:T(8,128)}, f32[4,128,512]{2,1,0:T(8,128)}) custom-call(f32[256,128]{1,0:T(8,128)S(1)} %bitcast.5, f32[4,128,512]{2,1,0:T(8,128)S(1)} %get-tuple-element.66.p, f32[4,128,512]{2,1,0:T(8,128)S(1)} %get-tuple-element.82.w, f32[4,128,512]{2,1,0:T(8,128)S(1)} %get-tuple-element.67.q, ...), custom_call_target="tpu_custom_call" | custom-call | tf_op jit(solution)/shard_map/pallas_call | solution.py:489
  (23 shorter events, 0.4 us)
Async XLA Ops:
  0.6 1.2 %copy-start.1 = (s32[4,128,512]{2,1,0:T(8,128)S(1)}, s32[4,128,512]{2,1,0:T(8,128)}, u32[]{:S(2)}) copy-start(s32[4,128,512]{2,1,0:T(8,128)} %labels.3) | copy-start | bytes 3145732
  1.9 8.0 %copy-start.3 = (f32[4,128,512]{2,1,0:T(8,128)S(1)}, f32[4,128,512]{2,1,0:T(8,128)}, u32[]{:S(2)}) copy-start(f32[4,128,512]{2,1,0:T(8,128)} %source.1) | copy-start | bytes 3145732
  2.0 9.7 %copy-start = (f32[4,4,128,128]{3,2,1,0:T(8,128)S(1)}, f32[4,4,128,128]{3,2,1,0:T(8,128)}, u32[]{:S(2)}) copy-start(f32[4,4,128,128]{3,2,1,0:T(8,128)} %constant.10.clone.vectors) | copy-start | bytes 3145732
  2.0 9.7 %collective-permute-start.2 = (s32[1,128,512]{2,1,0:T(8,128)S(1)}, s32[1,128,512]{2,1,0:T(8,128)S(1)}, u32[]{:S(2)}, u32[]{:S(2)}) collective-permute-start(s32[1,128,512]{2,1,0:T(8,128)S(1)} %get-tuple-element.50), channel_id=1, source_target_pairs={{0,4},{4,0},{8,12},{12,8},{16,20},{20,16},{24,28},{28,24},{32,36},... | collective-permute-start | bytes 786440 | tf_op jit(solution)/shard_map/ppermute | solution.py:119
  5.3 6.4 %collective-permute-start.3 = (s32[1,128,512]{2,1,0:T(8,128)S(1)}, s32[1,128,512]{2,1,0:T(8,128)S(1)}, u32[]{:S(2)}, u32[]{:S(2)}) collective-permute-start(s32[1,128,512]{2,1,0:T(8,128)S(1)} %get-tuple-element.51), channel_id=1, source_target_pairs={{0,1},{1,0},{2,3},{3,2},{4,8},{5,9},{6,10},{7,11},{8,4},{9,5},{10,... | collective-permute-start | bytes 786440 | tf_op jit(solution)/shard_map/ppermute | solution.py:129
  5.3 6.3 %collective-permute-start = (s32[4,512]{1,0:T(4,128)S(1)}, s32[4,512]{1,0:T(4,128)S(1)}, u32[]{:S(2)}, u32[]{:S(2)}) collective-permute-start(s32[4,512]{1,0:T(4,128)S(1)} %get-tuple-element.48), channel_id=1, source_target_pairs={{0,1},{1,0},{2,3},{3,2},{4,5},{5,4},{6,7},{7,6},{8,9},{9,8},{10,11... | collective-permute-start | bytes 24584 | tf_op jit(solution)/shard_map/ppermute | solution.py:119
  6.5 5.1 %collective-permute-start.1 = (s32[4,512]{1,0:T(4,128)S(1)}, s32[4,512]{1,0:T(4,128)S(1)}, u32[]{:S(2)}, u32[]{:S(2)}) collective-permute-start(s32[4,512]{1,0:T(4,128)S(1)} %get-tuple-element.49), channel_id=1, source_target_pairs={{0,3},{1,2},{2,1},{3,0},{4,7},{5,6},{6,5},{7,4},{8,11},{9,10},{10,... | collective-permute-start | bytes 24584 | tf_op jit(solution)/shard_map/ppermute | solution.py:119
  11.7 3.9 %copy-start.2 = (bf16[4,128,384]{2,1,0:T(8,128)(2,1)S(1)}, bf16[4,128,384]{2,1,0:T(8,128)(2,1)}, u32[]{:S(2)}) copy-start(bf16[4,128,384]{2,1,0:T(8,128)(2,1)} %constant.9.clone.green) | copy-start | bytes 1179652
  12.3 5.3 %collective-permute-start.4 = (f32[8,512]{1,0:T(8,128)S(1)}, f32[8,512]{1,0:T(8,128)S(1)}, u32[]{:S(2)}, u32[]{:S(2)}) collective-permute-start(f32[8,512]{1,0:T(8,128)S(1)} %get-tuple-element.57), channel_id=1, source_target_pairs={{0,1},{1,0},{2,3},{3,2},{4,5},{5,4},{6,7},{7,6},{8,9},{9,8},{10,11... | collective-permute-start | bytes 49160 | tf_op jit(solution)/shard_map/ppermute | solution.py:119
  12.8 4.8 %collective-permute-start.6 = (f32[8,512]{1,0:T(8,128)S(1)}, f32[8,512]{1,0:T(8,128)S(1)}, u32[]{:S(2)}, u32[]{:S(2)}) collective-permute-start(f32[8,512]{1,0:T(8,128)S(1)} %get-tuple-element.59), channel_id=1, source_target_pairs={{0,3},{1,2},{2,1},{3,0},{4,7},{5,6},{6,5},{7,4},{8,11},{9,10},{10,... | collective-permute-start | bytes 49160 | tf_op jit(solution)/shard_map/ppermute | solution.py:119
  13.6 4.0 %collective-permute-start.5 = (f32[4,512]{1,0:T(4,128)S(1)}, f32[4,512]{1,0:T(4,128)S(1)}, u32[]{:S(2)}, u32[]{:S(2)}) collective-permute-start(f32[4,512]{1,0:T(4,128)S(1)} %get-tuple-element.58), channel_id=1, source_target_pairs={{0,2},{1,3},{2,0},{3,1},{4,6},{5,7},{6,4},{7,5},{8,10},{9,11},{10,... | collective-permute-start | bytes 24584 | tf_op jit(solution)/shard_map/ppermute | solution.py:119
  15.7 1.9 %copy-start.4 = (f32[4,8]{1,0:T(4,128)S(1)}, f32[4,8]{1,0:T(4,128)}, u32[]{:S(2)}) copy-start(f32[4,8]{1,0:T(4,128)} %constant.11.clone.scalars) | copy-start | bytes 388
  18.3 5.7 %collective-permute-start.7 = (f32[1,128,512]{2,1,0:T(8,128)S(1)}, f32[1,128,512]{2,1,0:T(8,128)S(1)}, u32[]{:S(2)}, u32[]{:S(2)}) collective-permute-start(f32[1,128,512]{2,1,0:T(8,128)S(1)} %get-tuple-element.71), channel_id=1, source_target_pairs={{0,4},{4,0},{8,12},{12,8},{16,20},{20,16},{24,28},{28,24},{32,36},... | collective-permute-start | bytes 786440 | tf_op jit(solution)/shard_map/ppermute | solution.py:119
  20.8 6.1 %collective-permute-start.8 = (f32[1,128,512]{2,1,0:T(8,128)S(1)}, f32[1,128,512]{2,1,0:T(8,128)S(1)}, u32[]{:S(2)}, u32[]{:S(2)}) collective-permute-start(f32[1,128,512]{2,1,0:T(8,128)S(1)} %get-tuple-element.72), channel_id=1, source_target_pairs={{0,1},{1,0},{2,3},{3,2},{4,8},{5,9},{6,10},{7,11},{8,4},{9,5},{10,... | collective-permute-start | bytes 786440 | tf_op jit(solution)/shard_map/ppermute | solution.py:129
  27.2 4.4 %collective-permute-start.9 = (f32[4,512]{1,0:T(4,128)S(1)}, f32[4,512]{1,0:T(4,128)S(1)}, u32[]{:S(2)}, u32[]{:S(2)}) collective-permute-start(f32[4,512]{1,0:T(4,128)S(1)} %get-tuple-element.77), channel_id=1, source_target_pairs={{0,1},{1,0},{2,3},{3,2},{4,5},{5,4},{6,7},{7,6},{8,9},{9,8},{10,11... | collective-permute-start | bytes 24584 | tf_op jit(solution)/shard_map/ppermute | solution.py:119
  28.3 4.0 %collective-permute-start.10 = (f32[4,512]{1,0:T(4,128)S(1)}, f32[4,512]{1,0:T(4,128)S(1)}, u32[]{:S(2)}, u32[]{:S(2)}) collective-permute-start(f32[4,512]{1,0:T(4,128)S(1)} %get-tuple-element.78), channel_id=1, source_target_pairs={{0,2},{1,3},{2,0},{3,1},{4,6},{5,7},{6,4},{7,5},{8,10},{9,11},{10,... | collective-permute-start | bytes 24584 | tf_op jit(solution)/shard_map/ppermute | solution.py:119
  29.8 4.0 %collective-permute-start.11 = (f32[4,512]{1,0:T(4,128)S(1)}, f32[4,512]{1,0:T(4,128)S(1)}, u32[]{:S(2)}, u32[]{:S(2)}) collective-permute-start(f32[4,512]{1,0:T(4,128)S(1)} %get-tuple-element.79), channel_id=1, source_target_pairs={{0,3},{1,2},{2,1},{3,0},{4,7},{5,6},{6,5},{7,4},{8,11},{9,10},{10,... | collective-permute-start | bytes 24584 | tf_op jit(solution)/shard_map/ppermute | solution.py:119
  34.5 4.5 %collective-permute-start.12 = (f32[1,128,512]{2,1,0:T(8,128)S(1)}, f32[1,128,512]{2,1,0:T(8,128)S(1)}, u32[]{:S(2)}, u32[]{:S(2)}) collective-permute-start(f32[1,128,512]{2,1,0:T(8,128)S(1)} %get-tuple-element.84), channel_id=1, source_target_pairs={{0,4},{4,0},{8,12},{12,8},{16,20},{20,16},{24,28},{28,24},{32,36},... | collective-permute-start | bytes 786440 | tf_op jit(solution)/shard_map/ppermute | solution.py:119
  36.6 6.1 %collective-permute-start.13 = (f32[1,128,512]{2,1,0:T(8,128)S(1)}, f32[1,128,512]{2,1,0:T(8,128)S(1)}, u32[]{:S(2)}, u32[]{:S(2)}) collective-permute-start(f32[1,128,512]{2,1,0:T(8,128)S(1)} %get-tuple-element.85), channel_id=1, source_target_pairs={{0,1},{1,0},{2,3},{3,2},{4,8},{5,9},{6,10},{7,11},{8,4},{9,5},{10,... | collective-permute-start | bytes 786440 | tf_op jit(solution)/shard_map/ppermute | solution.py:129

commit v4 on v3

--- a/solution.py
+++ b/solution.py
@@ -13,7 +13,6 @@
 SHIFT = 0.0016
 VMEM = pl.BlockSpec(memory_space=pltpu.VMEM)
 HBM = pl.BlockSpec(memory_space=pltpu.HBM)
-SMEM = pl.BlockSpec(memory_space=pltpu.SMEM)
 ALL = ("gz", "gy")
 STEP = 64
 
@@ -43,7 +42,7 @@
                 scalars[d, k] = math.cosh(theta * (other + 1) * rows) / low
             else:
                 scalars[d, 4 + k] = math.cosh(theta * (total - other * rows)) / fhigh
-    return np.stack(blocks), np.stack(vectors).astype(np.float32), scalars.astype(np.float32)
+    return np.stack(blocks), np.stack(vectors).astype(np.float32), np.repeat(scalars[..., None], 128, 2).astype(np.float32)
 
 
 def call(body, outs, ins, scratch=(), out_space=VMEM):
@@ -134,13 +133,19 @@
     def even(axis):
         return lax.axis_index(axis) % 2 == 0
 
-    def borders(labels, in_o, out_o, one_o, three_o, first, last, sems):
-        top, bottom = jnp.int32(nz - 1), jnp.int32(0)
+    def side(inner):
+        return jnp.where(even("gz") == inner, jnp.int32(nz - 1), jnp.int32(0))
+
+    def border(labels, out_o, sem):
+        copy = pltpu.make_async_copy(labels.at[pl.ds(side(False), 1)], out_o, sem)
+        copy.start()
+        copy.wait()
+
+    def borders(labels, in_o, one_o, three_o, first, last, sems):
         copies = [
-            pltpu.make_async_copy(labels.at[pl.ds(jnp.where(even("gz"), top, bottom), 1)], in_o, sems.at[0]),
-            pltpu.make_async_copy(labels.at[pl.ds(jnp.where(even("gz"), bottom, top), 1)], out_o, sems.at[1]),
-            pltpu.make_async_copy(labels.at[:, pl.ds(0, 8)], first, sems.at[2]),
-            pltpu.make_async_copy(labels.at[:, pl.ds(ny - 8, 8)], last, sems.at[3]),
+            pltpu.make_async_copy(labels.at[pl.ds(side(True), 1)], in_o, sems.at[0]),
+            pltpu.make_async_copy(labels.at[:, pl.ds(0, 8)], first, sems.at[1]),
+            pltpu.make_async_copy(labels.at[:, pl.ds(ny - 8, 8)], last, sems.at[2]),
         ]
         for copy in copies:
             copy.start()
@@ -151,9 +156,10 @@
             one_o[z : z + 1, :] = jnp.where(even("gy"), high, low)
             three_o[z : z + 1, :] = jnp.where(even("gy"), low, high)
 
-    sent = [jax.ShapeDtypeStruct(shape, jnp.int32) for shape in (plane, plane, (nz, nx), (nz, nx))]
-    in_o, out_o, one, three = call(
-        borders, sent, [HBM], [pltpu.VMEM(edge, jnp.int32)] * 2 + [pltpu.SemaphoreType.DMA((4,))]
+    sent = [jax.ShapeDtypeStruct(shape, jnp.int32) for shape in (plane, (nz, nx), (nz, nx))]
+    out_o = call(border, sent[:1], [HBM], [pltpu.SemaphoreType.DMA])(labels)[0]
+    in_o, one, three = call(
+        borders, sent, [HBM], [pltpu.VMEM(edge, jnp.int32)] * 2 + [pltpu.SemaphoreType.DMA((3,))]
     )(labels)
     out_o, in_o = across(out_o), inside(in_o)
     one, three = crosswise(one, 1), crosswise(three, 3)
@@ -282,32 +288,43 @@
             stack = jnp.concatenate([head, head, tail], axis=0)
             out[z] = jnp.dot(green[my], stack, preferred_element_type=F32)
 
-    def solve(z, part, s, xo, xm, vectors, scalars, one, two, three, s_one, s_three, put):
+    def solve(z, x, part, s, vectors, scalars, one, two, three, s_one, s_three, put):
         my = lax.axis_index("gy")
-        got = [r[z : z + 1, :] for r in (one, two, three)]
-        left = sum(scalars[my, n + 1] * got[n] for n in range(3))
-        right = sum(scalars[my, 5 + n] * got[n] for n in range(3))
-        ones, threes = s_one[nz + z : nz + z + 1, :], s_three[nz + z : nz + z + 1, :]
+        got = [r[pl.ds(z, 1), :] for r in (one, two, three)]
+        left = sum(wide(scalars[my, n + 1 : n + 2, :], nx) * got[n] for n in range(3))
+        right = sum(wide(scalars[my, n + 5 : n + 6, :], nx) * got[n] for n in range(3))
+        ones, threes = s_one[pl.ds(nz + z, 1), :], s_three[pl.ds(nz + z, 1), :]
         for r in starts:
             at = rows_at(r)
             g = part[z, at, :] + (wide(vectors[my, 2, at, :], nx) * left + wide(vectors[my, 3, at, :], nx) * right)
             put(r + 8, s[z, at, :] * g)
             if r == 0:
-                beside = (2.0 + SHIFT) * g[0:1] - g[1:2] - pick(z, xo, xm)[0:1, :]
+                beside = (2.0 + SHIFT) * g[0:1] - g[1:2] - x[0:1, :]
                 put(7, jnp.where(even("gy"), threes, ones) * beside)
             if r + STEP == ny:
-                beside = (2.0 + SHIFT) * g[-1:] - g[-2:-1] - pick(z, xo, xm)[ny - 1 : ny, :]
+                beside = (2.0 + SHIFT) * g[-1:] - g[-2:-1] - x[ny - 1 : ny, :]
                 put(ny + 8, jnp.where(even("gy"), ones, threes) * beside)
 
-    def solve_outer(part, s, xo, xm, vectors, scalars, one, two, three, s_one, s_three, p_o, in_o, out_o):
-        for n, z in enumerate(outer):
-            def put(r, value):
-                p_o[n, r : r + value.shape[0], :] = value
-            solve(z, part, s, xo, xm, vectors, scalars, one, two, three, s_one, s_three, put)
-        top = jnp.where(even("gz"), 1, 0)
-        for r in starts:
-            in_o[0, rows_at(r), :] = p_o[top, rows_at(r + 8), :]
-            out_o[0, rows_at(r), :] = p_o[1 - top, rows_at(r + 8), :]
+    def solve_out(part, s, xo, xm, vectors, scalars, one, two, three, s_one, s_three, held_o, out_o):
+        def put(r, value):
+            held_o[r : r + value.shape[0], :] = value
+            if value.shape[0] == STEP:
+                out_o[0, rows_at(r - 8), :] = value
+        z = side(False)
+        place = xo.at[jnp.where(z == 0, 0, 1)]
+        solve(z, place, part, s, vectors, scalars, one, two, three, s_one, s_three, put)
+
+    def solve_in(part, s, xo, xm, vectors, scalars, one, two, three, s_one, s_three, held, p_o, in_o):
+        z = side(True)
+        n = jnp.where(z == 0, 0, 1)
+
+        def put(r, value):
+            p_o[n, r : r + value.shape[0], :] = value
+            if value.shape[0] == STEP:
+                in_o[0, rows_at(r - 8), :] = value
+        solve(z, xo.at[n], part, s, vectors, scalars, one, two, three, s_one, s_three, put)
+        for r in range(0, ny + 16, 16):
+            p_o[1 - n, r : r + 16, :] = held[r : r + 16, :]
 
     def total(value):
         return jnp.sum(jnp.sum(value, 0, keepdims=True), 1, keepdims=True)
@@ -343,7 +360,7 @@
                 field[z, r : r + value.shape[0], :] = value
                 if value.shape[0] == STEP:
                     p_o[z, rows_at(r - 8), :] = value
-            solve(z, part, s, xo, xm, vectors, scalars, one, two, three, s_one, s_three, put)
+            solve(z, pick(z, xo, xm), part, s, vectors, scalars, one, two, three, s_one, s_three, put)
         for n, z in enumerate(outer):
             for r in starts:
                 p_o[z, rows_at(r), :] = p_outer[n, rows_at(r + 8), :]
@@ -461,25 +478,27 @@
     rows = [(nz, nx)] * 3
     framed_pair = (len(outer), ny + 16, nx)
 
+    places = [VMEM] * 12
+
     def start(xo, xm, sums, beside):
         got = gather(sums)
         beside = beside or (got[0], got[2])
         part = call(lines, [block], [VMEM] * 3)(xo, xm, green)[0]
         known = (part, s, xo, xm, vectors, scalars, *got, *beside)
-        pair, in_o, out_o = call(solve_outer, [framed_pair, plane, plane], places)(*known)
+        held, out_o = call(solve_out, [(ny + 16, nx), plane], places[:-1])(*known)
         out_o = across(out_o)
+        pair, in_o = call(solve_in, [framed_pair, plane], places)(*known, held)
         return (*known, pair), inside(in_o), out_o, beside
 
-    places = [VMEM] * 5 + [SMEM] + [VMEM] * 5
     known, z_in, z_out, beside = start(xo, xm, (one, two, three), None)
     p, q, xm, *sums, dots = call(
-        inner_first, [block, block, middle_shape, *rows, (1, 128)], places + [VMEM] * 7, field
+        inner_first, [block, block, middle_shape, *rows, (1, 128)], places + [VMEM] * 6, field
     )(*known, fx, fy, fz, fye, e, b)
     qo, xo, *sums, dots = call(outer_first, [ends_shape, ends_shape, *rows, (1, 128)], [VMEM] * 11)(
         p, q, *sums, z_in, z_out, fze, s, vectors, dots
     )
     known, z_in, z_out, _ = start(xo, xm, sums, beside)
-    w, v, last_dots = call(inner_last, [block, block, (1, 128)], places + [VMEM] * 9, field)(
+    w, v, last_dots = call(inner_last, [block, block, (1, 128)], places + [VMEM] * 8, field)(
         *known, fx, fy, fz, fye, e, b, q, qo
     )
     vo, dots = call(outer_last, [ends_shape, (1, 128)], [VMEM] * 7)(w, v, z_in, z_out, fze, last_dots, dots)

time: 72.3 us -> 70.6 us (0.976)
  starting transfers between devices: 19.4 us -> 22 us
  Pallas kernels: 11.7 us -> 9.77 us
  waiting for transfers between devices: 10.1 us -> 8.41 us
  other arithmetic: 1.44 us -> 0.09 us
    ppermute x3, starting transfers between devices: 1.2 us -> 11.2 us  [across(): lax.ppermute(value, ALL, [(i * parts + j, k * parts + m) for i, j, k, m i...]
    ppermute x11, starting transfers between devices: 18.2 us -> 10.8 us  [swap(): lax.ppermute(value, axis, [(i, partner(i) % size) for i in range(size)])]
    ppermute x3, waiting for transfers between devices: 6.44 us -> 4.67 us  [across(): lax.ppermute(value, ALL, [(i * parts + j, k * parts + m) for i, j, k, m i...]
    pallas_call x3 -> x6, Pallas kernels: 3.78 us -> 2.28 us  [the longest x1 1.85 us: local(): call(inner_last, [block, block, (1, 128)], places + [VMEM] * 8, field)]
  transfers between devices with their start and end apart: 14 -> 14, of which waited for: 5 -> 6; matrix products, arithmetic and copies ran while one was open for 2% -> 0% of each run, Pallas kernels for 10% -> 9%
where the time goes in v4:
time: 70.6 us; the launch traced here: 70.5 us
  blocking collectives  27.9 us (40%)
  starting transfers between devices  22 us (31%)
  Pallas kernels  9.77 us (14%)
  waiting for transfers between devices  8.41 us (12%)
  local copies, waits for them, and re-layouts  1.32 us (2%)
  between operations  0.94 us (1%)
    all_to_all x1, blocking collectives, local(): lax.all_to_all(jnp.broadcast_to(dots, (count, 128)), ALL, 0, 0, tiled=True)  27.9 us
    ppermute x3, starting transfers between devices, across(): lax.ppermute(value, ALL, [(i * parts + j, k * parts + m) for i, j, k, m i...  11.2 us
    ppermute x11, starting transfers between devices, swap(): lax.ppermute(value, axis, [(i, partner(i) % size) for i in range(size)])  10.8 us
    ppermute x3, waiting for transfers between devices, across(): lax.ppermute(value, ALL, [(i * parts + j, k * parts + m) for i, j, k, m i...  4.67 us
    ppermute x11, waiting for transfers between devices, swap(): lax.ppermute(value, axis, [(i, partner(i) % size) for i in range(size)])  3.74 us
    pallas_call x1, Pallas kernels, local(): call(inner_last, [block, block, (1, 128)], places + [VMEM] * 8, field)  1.85 us
    pallas_call x1, Pallas kernels, local(): call(faces, [block, block, (nz, ny + 8, nx), (nz - 1, ny, nx), block, (nz...  1.82 us
    pallas_call x1, Pallas kernels, local(): call(inner_first, [block, block, middle_shape, *rows, (1, 128)], places +...  1.78 us
  transfers between devices with their start and end apart: 14, of which 6 were waited for; matrix products, arithmetic and copies ran while one was open for 0% of the time, Pallas kernels for 9%

profile of v4, /device:TPU:1, one launch (start us, length us, event | category | flops | bytes accessed | tf_op | source)
XLA Modules:
  0.0 70.5 jit_solution(5523856563371252917)
XLA Ops:
  0.6 1.2 %copy-done.1 = s32[4,128,512]{2,1,0:T(8,128)S(1)} copy-done((s32[4,128,512]{2,1,0:T(8,128)S(1)}, s32[4,128,512]{2,1,0:T(8,128)}, u32[]{:S(2)}) %copy-start.1) | copy-done | bytes 1048600
  1.9 3.1 %collective-permute-start.3 = (s32[1,128,512]{2,1,0:T(8,128)S(1)}, s32[1,128,512]{2,1,0:T(8,128)S(1)}, u32[]{:S(2)}, u32[]{:S(2)}) collective-permute-start(s32[1,128,512]{2,1,0:T(8,128)S(1)} %shard_map.97), channel_id=1, source_target_pairs={{0,1},{1,0},{2,3},{3,2},{4,8},{5,9},{6,10},{7,11},{8,4},{9,5},{10,... | collective-permute-start | bytes 786440 | tf_op jit(solution)/shard_map/ppermute | solution.py:128
  5.0 0.1 shard_map.96
  5.2 0.3 collective-permute-start.2
  5.5 1.7 %collective-permute-start = (s32[4,512]{1,0:T(4,128)S(1)}, s32[4,512]{1,0:T(4,128)S(1)}, u32[]{:S(2)}, u32[]{:S(2)}) collective-permute-start(s32[4,512]{1,0:T(4,128)S(1)} %get-tuple-element.49), channel_id=1, source_target_pairs={{0,1},{1,0},{2,3},{3,2},{4,5},{5,4},{6,7},{7,6},{8,9},{9,8},{10,11... | collective-permute-start | bytes 24584 | tf_op jit(solution)/shard_map/ppermute | solution.py:118
  7.2 1.3 %collective-permute-start.1 = (s32[4,512]{1,0:T(4,128)S(1)}, s32[4,512]{1,0:T(4,128)S(1)}, u32[]{:S(2)}, u32[]{:S(2)}) collective-permute-start(s32[4,512]{1,0:T(4,128)S(1)} %get-tuple-element.50), channel_id=1, source_target_pairs={{0,3},{1,2},{2,1},{3,0},{4,7},{5,6},{6,5},{7,4},{8,11},{9,10},{10,... | collective-permute-start | bytes 24584 | tf_op jit(solution)/shard_map/ppermute | solution.py:118
  8.6 1.8 %shard_map.95 = (f32[4,128,512]{2,1,0:T(8,128)S(1)}, f32[4,128,512]{2,1,0:T(8,128)S(1)}, f32[4,136,512]{2,1,0:T(8,128)S(1)}, f32[3,128,512]{2,1,0:T(8,128)S(1)},...) custom-call(s32[4,128,512]{2,1,0:T(8,128)S(1)} %copy-done.1, ...), custom_call_target="tpu_custom_call" | custom-call | tf_op jit(solution)/shard_map/pallas_call | solution.py:216
  10.5 0.5 collective-permute-done.1.y_three
  11.0 0.6 shard_map.98
  11.6 1.6 %collective-permute-start.6 = (f32[8,512]{1,0:T(8,128)S(1)}, f32[8,512]{1,0:T(8,128)S(1)}, u32[]{:S(2)}, u32[]{:S(2)}) collective-permute-start(f32[8,512]{1,0:T(8,128)S(1)} %get-tuple-element.59), channel_id=1, source_target_pairs={{0,3},{1,2},{2,1},{3,0},{4,7},{5,6},{6,5},{7,4},{8,11},{9,10},{10,... | collective-permute-start | bytes 49160 | tf_op jit(solution)/shard_map/ppermute | solution.py:118
  13.3 1.6 %collective-permute-start.5 = (f32[4,512]{1,0:T(4,128)S(1)}, f32[4,512]{1,0:T(4,128)S(1)}, u32[]{:S(2)}, u32[]{:S(2)}) collective-permute-start(f32[4,512]{1,0:T(4,128)S(1)} %get-tuple-element.58), channel_id=1, source_target_pairs={{0,2},{1,3},{2,0},{3,1},{4,6},{5,7},{6,4},{7,5},{8,10},{9,11},{10,... | collective-permute-start | bytes 24584 | tf_op jit(solution)/shard_map/ppermute | solution.py:118
  14.9 0.4 shard_map.99.part
  15.3 1.9 %collective-permute-done.5.two = f32[4,512]{1,0:T(4,128)S(1)} collective-permute-done((f32[4,512]{1,0:T(4,128)S(1)}, f32[4,512]{1,0:T(4,128)S(1)}, u32[]{:S(2)}, u32[]{:S(2)}) %collective-permute-start.5) | collective-permute-done | bytes 8224 | tf_op jit(solution)/shard_map/ppermute | solution.py:118
  17.3 0.1 shard_map.100
  17.4 4.7 %collective-permute-start.8 = (f32[1,128,512]{2,1,0:T(8,128)S(1)}, f32[1,128,512]{2,1,0:T(8,128)S(1)}, u32[]{:S(2)}, u32[]{:S(2)}) collective-permute-start(f32[1,128,512]{2,1,0:T(8,128)S(1)} %get-tuple-element.73), channel_id=1, source_target_pairs={{0,1},{1,0},{2,3},{3,2},{4,8},{5,9},{6,10},{7,11},{8,4},{9,5},{10,... | collective-permute-start | bytes 786440 | tf_op jit(solution)/shard_map/ppermute | solution.py:128
  22.1 0.1 shard_map.101
  22.3 1.8 %shard_map.102 = (f32[4,128,512]{2,1,0:T(8,128)S(1)}, f32[4,128,512]{2,1,0:T(8,128)S(1)}, f32[2,128,512]{2,1,0:T(8,128)S(1)}, f32[4,512]{1,0:T(4,128)S(1)}, f32[...) custom-call(f32[4,128,512]{2,1,0:T(8,128)S(1)} %shard_map.99.part, ...), custom_call_target="tpu_custom_call" | custom-call | tf_op jit(solution)/shard_map/pallas_call | solution.py:494
  24.0 2.4 %collective-permute-done.8.z_out = f32[1,128,512]{2,1,0:T(8,128)S(1)} collective-permute-done((f32[1,128,512]{2,1,0:T(8,128)S(1)}, f32[1,128,512]{2,1,0:T(8,128)S(1)}, u32[]{:S(2)}, u32[]{:S(2)}) %collective-permute-start.8) | collective-permute-done | bytes 262176 | tf_op jit(solution)/shard_map/ppermute | solution.py:128
  26.4 0.4 shard_map.103
  26.8 1.1 %collective-permute-start.9 = (f32[4,512]{1,0:T(4,128)S(1)}, f32[4,512]{1,0:T(4,128)S(1)}, u32[]{:S(2)}, u32[]{:S(2)}) collective-permute-start(f32[4,512]{1,0:T(4,128)S(1)} %get-tuple-element.78), channel_id=1, source_target_pairs={{0,1},{1,0},{2,3},{3,2},{4,5},{5,4},{6,7},{7,6},{8,9},{9,8},{10,11... | collective-permute-start | bytes 24584 | tf_op jit(solution)/shard_map/ppermute | solution.py:118
  27.9 0.9 %collective-permute-start.10 = (f32[4,512]{1,0:T(4,128)S(1)}, f32[4,512]{1,0:T(4,128)S(1)}, u32[]{:S(2)}, u32[]{:S(2)}) collective-permute-start(f32[4,512]{1,0:T(4,128)S(1)} %get-tuple-element.79), channel_id=1, source_target_pairs={{0,2},{1,3},{2,0},{3,1},{4,6},{5,7},{6,4},{7,5},{8,10},{9,11},{10,... | collective-permute-start | bytes 24584 | tf_op jit(solution)/shard_map/ppermute | solution.py:118
  28.9 1.9 %collective-permute-start.11 = (f32[4,512]{1,0:T(4,128)S(1)}, f32[4,512]{1,0:T(4,128)S(1)}, u32[]{:S(2)}, u32[]{:S(2)}) collective-permute-start(f32[4,512]{1,0:T(4,128)S(1)} %get-tuple-element.80), channel_id=1, source_target_pairs={{0,3},{1,2},{2,1},{3,0},{4,7},{5,6},{6,5},{7,4},{8,11},{9,10},{10,... | collective-permute-start | bytes 24584 | tf_op jit(solution)/shard_map/ppermute | solution.py:118
  30.8 0.5 shard_map.104.part
  31.2 0.7 %collective-permute-done.10.two = f32[4,512]{1,0:T(4,128)S(1)} collective-permute-done((f32[4,512]{1,0:T(4,128)S(1)}, f32[4,512]{1,0:T(4,128)S(1)}, u32[]{:S(2)}, u32[]{:S(2)}) %collective-permute-start.10) | collective-permute-done | bytes 8224 | tf_op jit(solution)/shard_map/ppermute | solution.py:118
  31.9 0.6 collective-permute-done.11.three
  32.7 3.4 %collective-permute-start.13 = (f32[1,128,512]{2,1,0:T(8,128)S(1)}, f32[1,128,512]{2,1,0:T(8,128)S(1)}, u32[]{:S(2)}, u32[]{:S(2)}) collective-permute-start(f32[1,128,512]{2,1,0:T(8,128)S(1)} %get-tuple-element.87), channel_id=1, source_target_pairs={{0,1},{1,0},{2,3},{3,2},{4,8},{5,9},{6,10},{7,11},{8,4},{9,5},{10,... | collective-permute-start | bytes 786440 | tf_op jit(solution)/shard_map/ppermute | solution.py:128
  36.1 0.1 shard_map.106
  36.3 1.9 %shard_map.107 = (f32[4,128,512]{2,1,0:T(8,128)S(1)}, f32[4,128,512]{2,1,0:T(8,128)S(1)}, f32[1,128]{1,0:T(1,128)S(1)}) custom-call(f32[4,128,512]{2,1,0:T(8,128)S(1)} %shard_map.104.part, f32[4,128,512]{2,1,0:T(8,128)S(1)} %get-tuple-element.56.s, f32[2,128,512]{2,1,0:T(8,128)S(1)} %get-tuple-element.76.xo, f32[2,128,512]{2,1,0:T(8,128)S(1)} %get-tuple-element.77.xm, ...), custom_call_target="tpu_custom_call" | custom-call | tf_op jit(solution)/shard_map/pallas_call | solution.py:501
  38.1 2.3 %collective-permute-done.13.z_out = f32[1,128,512]{2,1,0:T(8,128)S(1)} collective-permute-done((f32[1,128,512]{2,1,0:T(8,128)S(1)}, f32[1,128,512]{2,1,0:T(8,128)S(1)}, u32[]{:S(2)}, u32[]{:S(2)}) %collective-permute-start.13) | collective-permute-done | bytes 262176 | tf_op jit(solution)/shard_map/ppermute | solution.py:128
  40.4 0.3 shard_map.108
  40.8 27.9 %all_to_all.8 = f32[256,1,128]{2,1,0:T(1,128)S(1)} all-to-all(f32[256,1,128]{2,1,0:T(1,128)S(1)} %broadcast_in_dim.9), channel_id=1, replica_groups=mesh['gz'=64,'gy'=4] {'gz','gy'}, dimensions={0} | all-to-all | bytes 262144 | tf_op jit(solution)/shard_map/all_to_all | solution.py:506
  68.7 1.6 %shard_map.109 = (f32[4,128,512]{2,1,0:T(8,128)}, f32[4,128,512]{2,1,0:T(8,128)}) custom-call(f32[256,128]{1,0:T(8,128)S(1)} %bitcast.5, f32[4,128,512]{2,1,0:T(8,128)S(1)} %get-tuple-element.67.p, f32[4,128,512]{2,1,0:T(8,128)S(1)} %get-tuple-element.84.w, f32[4,128,512]{2,1,0:T(8,128)S(1)} %get-tuple-element.68.q, ...), custom_call_target="tpu_custom_call" | custom-call | tf_op jit(solution)/shard_map/pallas_call | solution.py:508
  (32 shorter events, 0.6 us)
Async XLA Ops:
  0.6 1.2 %copy-start.1 = (s32[4,128,512]{2,1,0:T(8,128)S(1)}, s32[4,128,512]{2,1,0:T(8,128)}, u32[]{:S(2)}) copy-start(s32[4,128,512]{2,1,0:T(8,128)} %labels.5) | copy-start | bytes 3145732
  1.9 6.7 %copy-start.5 = (s32[2,4,128]{2,1,0:T(4,128)S(1)}, s32[2,4,128]{2,1,0:T(4,128)}, u32[]{:S(2)}) copy-start(s32[2,4,128]{2,1,0:T(4,128)} %param.10) | copy-start | bytes 12292
  1.9 6.7 %copy-start.6 = (f32[2]{0:T(128)S(1)}, f32[2]{0:T(128)}, u32[]{:S(2)}) copy-start(f32[2]{0:T(128)} %param.11) | copy-start | bytes 28
  1.9 6.7 %copy-start.7 = (f32[4]{0:T(128)S(1)}, f32[4]{0:T(128)}, u32[]{:S(2)}) copy-start(f32[4]{0:T(128)} %param.9) | copy-start | bytes 52
  1.9 6.8 %copy-start.3 = (f32[4,128,512]{2,1,0:T(8,128)S(1)}, f32[4,128,512]{2,1,0:T(8,128)}, u32[]{:S(2)}) copy-start(f32[4,128,512]{2,1,0:T(8,128)} %source.1) | copy-start | bytes 3145732
  1.9 9.0 %collective-permute-start.3 = (s32[1,128,512]{2,1,0:T(8,128)S(1)}, s32[1,128,512]{2,1,0:T(8,128)S(1)}, u32[]{:S(2)}, u32[]{:S(2)}) collective-permute-start(s32[1,128,512]{2,1,0:T(8,128)S(1)} %shard_map.97), channel_id=1, source_target_pairs={{0,1},{1,0},{2,3},{3,2},{4,8},{5,9},{6,10},{7,11},{8,4},{9,5},{10,... | collective-permute-start | bytes 786440 | tf_op jit(solution)/shard_map/ppermute | solution.py:128
  5.1 5.8 %copy-start = (f32[4,4,128,128]{3,2,1,0:T(8,128)S(1)}, f32[4,4,128,128]{3,2,1,0:T(8,128)}, u32[]{:S(2)}) copy-start(f32[4,4,128,128]{3,2,1,0:T(8,128)} %constant.10.clone.vectors) | copy-start | bytes 3145732
  5.2 5.8 %collective-permute-start.2 = (s32[1,128,512]{2,1,0:T(8,128)S(1)}, s32[1,128,512]{2,1,0:T(8,128)S(1)}, u32[]{:S(2)}, u32[]{:S(2)}) collective-permute-start(s32[1,128,512]{2,1,0:T(8,128)S(1)} %get-tuple-element.51), channel_id=1, source_target_pairs={{0,4},{4,0},{8,12},{12,8},{16,20},{20,16},{24,28},{28,24},{32,36},... | collective-permute-start | bytes 786440 | tf_op jit(solution)/shard_map/ppermute | solution.py:118
  5.5 5.0 %collective-permute-start = (s32[4,512]{1,0:T(4,128)S(1)}, s32[4,512]{1,0:T(4,128)S(1)}, u32[]{:S(2)}, u32[]{:S(2)}) collective-permute-start(s32[4,512]{1,0:T(4,128)S(1)} %get-tuple-element.49), channel_id=1, source_target_pairs={{0,1},{1,0},{2,3},{3,2},{4,5},{5,4},{6,7},{7,6},{8,9},{9,8},{10,11... | collective-permute-start | bytes 24584 | tf_op jit(solution)/shard_map/ppermute | solution.py:118
  7.2 3.7 %collective-permute-start.1 = (s32[4,512]{1,0:T(4,128)S(1)}, s32[4,512]{1,0:T(4,128)S(1)}, u32[]{:S(2)}, u32[]{:S(2)}) collective-permute-start(s32[4,512]{1,0:T(4,128)S(1)} %get-tuple-element.50), channel_id=1, source_target_pairs={{0,3},{1,2},{2,1},{3,0},{4,7},{5,6},{6,5},{7,4},{8,11},{9,10},{10,... | collective-permute-start | bytes 24584 | tf_op jit(solution)/shard_map/ppermute | solution.py:118
  10.9 3.9 %copy-start.2 = (bf16[4,128,384]{2,1,0:T(8,128)(2,1)S(1)}, bf16[4,128,384]{2,1,0:T(8,128)(2,1)}, u32[]{:S(2)}) copy-start(bf16[4,128,384]{2,1,0:T(8,128)(2,1)} %constant.9.clone.green) | copy-start | bytes 1179652
  11.5 5.7 %collective-permute-start.4 = (f32[8,512]{1,0:T(8,128)S(1)}, f32[8,512]{1,0:T(8,128)S(1)}, u32[]{:S(2)}, u32[]{:S(2)}) collective-permute-start(f32[8,512]{1,0:T(8,128)S(1)} %get-tuple-element.57), channel_id=1, source_target_pairs={{0,1},{1,0},{2,3},{3,2},{4,5},{5,4},{6,7},{7,6},{8,9},{9,8},{10,11... | collective-permute-start | bytes 49160 | tf_op jit(solution)/shard_map/ppermute | solution.py:118
  11.6 5.6 %collective-permute-start.6 = (f32[8,512]{1,0:T(8,128)S(1)}, f32[8,512]{1,0:T(8,128)S(1)}, u32[]{:S(2)}, u32[]{:S(2)}) collective-permute-start(f32[8,512]{1,0:T(8,128)S(1)} %get-tuple-element.59), channel_id=1, source_target_pairs={{0,3},{1,2},{2,1},{3,0},{4,7},{5,6},{6,5},{7,4},{8,11},{9,10},{10,... | collective-permute-start | bytes 49160 | tf_op jit(solution)/shard_map/ppermute | solution.py:118
  13.3 4.0 %collective-permute-start.5 = (f32[4,512]{1,0:T(4,128)S(1)}, f32[4,512]{1,0:T(4,128)S(1)}, u32[]{:S(2)}, u32[]{:S(2)}) collective-permute-start(f32[4,512]{1,0:T(4,128)S(1)} %get-tuple-element.58), channel_id=1, source_target_pairs={{0,2},{1,3},{2,0},{3,1},{4,6},{5,7},{6,4},{7,5},{8,10},{9,11},{10,... | collective-permute-start | bytes 24584 | tf_op jit(solution)/shard_map/ppermute | solution.py:118
  14.9 2.4 %copy-start.4 = (f32[4,8,128]{2,1,0:T(8,128)S(1)}, f32[4,8,128]{2,1,0:T(8,128)}, u32[]{:S(2)}) copy-start(f32[4,8,128]{2,1,0:T(8,128)} %constant.11.clone.scalars) | copy-start | bytes 49156
  17.4 9.0 %collective-permute-start.8 = (f32[1,128,512]{2,1,0:T(8,128)S(1)}, f32[1,128,512]{2,1,0:T(8,128)S(1)}, u32[]{:S(2)}, u32[]{:S(2)}) collective-permute-start(f32[1,128,512]{2,1,0:T(8,128)S(1)} %get-tuple-element.73), channel_id=1, source_target_pairs={{0,1},{1,0},{2,3},{3,2},{4,8},{5,9},{6,10},{7,11},{8,4},{9,5},{10,... | collective-permute-start | bytes 786440 | tf_op jit(solution)/shard_map/ppermute | solution.py:128
  22.2 4.3 %collective-permute-start.7 = (f32[1,128,512]{2,1,0:T(8,128)S(1)}, f32[1,128,512]{2,1,0:T(8,128)S(1)}, u32[]{:S(2)}, u32[]{:S(2)}) collective-permute-start(f32[1,128,512]{2,1,0:T(8,128)S(1)} %get-tuple-element.72), channel_id=1, source_target_pairs={{0,4},{4,0},{8,12},{12,8},{16,20},{20,16},{24,28},{28,24},{32,36},... | collective-permute-start | bytes 786440 | tf_op jit(solution)/shard_map/ppermute | solution.py:118
  26.8 4.4 %collective-permute-start.9 = (f32[4,512]{1,0:T(4,128)S(1)}, f32[4,512]{1,0:T(4,128)S(1)}, u32[]{:S(2)}, u32[]{:S(2)}) collective-permute-start(f32[4,512]{1,0:T(4,128)S(1)} %get-tuple-element.78), channel_id=1, source_target_pairs={{0,1},{1,0},{2,3},{3,2},{4,5},{5,4},{6,7},{7,6},{8,9},{9,8},{10,11... | collective-permute-start | bytes 24584 | tf_op jit(solution)/shard_map/ppermute | solution.py:118
  27.9 4.0 %collective-permute-start.10 = (f32[4,512]{1,0:T(4,128)S(1)}, f32[4,512]{1,0:T(4,128)S(1)}, u32[]{:S(2)}, u32[]{:S(2)}) collective-permute-start(f32[4,512]{1,0:T(4,128)S(1)} %get-tuple-element.79), channel_id=1, source_target_pairs={{0,2},{1,3},{2,0},{3,1},{4,6},{5,7},{6,4},{7,5},{8,10},{9,11},{10,... | collective-permute-start | bytes 24584 | tf_op jit(solution)/shard_map/ppermute | solution.py:118
  28.9 3.7 %collective-permute-start.11 = (f32[4,512]{1,0:T(4,128)S(1)}, f32[4,512]{1,0:T(4,128)S(1)}, u32[]{:S(2)}, u32[]{:S(2)}) collective-permute-start(f32[4,512]{1,0:T(4,128)S(1)} %get-tuple-element.80), channel_id=1, source_target_pairs={{0,3},{1,2},{2,1},{3,0},{4,7},{5,6},{6,5},{7,4},{8,11},{9,10},{10,... | collective-permute-start | bytes 24584 | tf_op jit(solution)/shard_map/ppermute | solution.py:118
  32.7 7.8 %collective-permute-start.13 = (f32[1,128,512]{2,1,0:T(8,128)S(1)}, f32[1,128,512]{2,1,0:T(8,128)S(1)}, u32[]{:S(2)}, u32[]{:S(2)}) collective-permute-start(f32[1,128,512]{2,1,0:T(8,128)S(1)} %get-tuple-element.87), channel_id=1, source_target_pairs={{0,1},{1,0},{2,3},{3,2},{4,8},{5,9},{6,10},{7,11},{8,4},{9,5},{10,... | collective-permute-start | bytes 786440 | tf_op jit(solution)/shard_map/ppermute | solution.py:128
  36.2 4.3 %collective-permute-start.12 = (f32[1,128,512]{2,1,0:T(8,128)S(1)}, f32[1,128,512]{2,1,0:T(8,128)S(1)}, u32[]{:S(2)}, u32[]{:S(2)}) collective-permute-start(f32[1,128,512]{2,1,0:T(8,128)S(1)} %get-tuple-element.86), channel_id=1, source_target_pairs={{0,4},{4,0},{8,12},{12,8},{16,20},{20,16},{24,28},{28,24},{32,36},... | collective-permute-start | bytes 786440 | tf_op jit(solution)/shard_map/ppermute | solution.py:118

commit v5 on v4

--- a/solution.py
+++ b/solution.py
@@ -465,14 +465,22 @@
                 at = rows_at(r)
                 x_held[z, at, :] = along * p[z, at, :] - across * w[z, at, :]
                 r_held[z, at, :] = b[z, at, :] - along * image_of(z, qo, q, at) + across * image_of(z, vo, v, at)
-            for n, (held, out) in enumerate(((x_held, x_o), (r_held, r_o))):
-                copies.append(pltpu.make_async_copy(held.at[z], out.at[z], sems.at[n, z]))
-                copies[-1].start()
+                for n, (held, out) in enumerate(((x_held, x_o), (r_held, r_o))):
+                    some = pl.ds(r, STEP)
+                    copies.append(pltpu.make_async_copy(held.at[z, some], out.at[z, some], sems.at[n, z, r // STEP]))
+                    copies[-1].start()
         for copy in copies:
             copy.wait()
 
+    def pass_on(one, three, one_o, three_o):
+        one_o[...] = one[...]
+        three_o[...] = three[...]
+
     def gather(sums):
-        return [crosswise(v, n) for n, v in enumerate(sums, 1)]
+        one, two, three = sums
+        two = crosswise(two, 2)
+        one, three = call(pass_on, [one.shape, three.shape], [VMEM] * 2)(one, three)
+        return [crosswise(one, 1), two, crosswise(three, 3)]
 
     field = [pltpu.VMEM(framed, F32)]
     rows = [(nz, nx)] * 3
@@ -509,7 +517,7 @@
             combine,
             [block, block],
             [VMEM] * 8,
-            [pltpu.VMEM(block, F32)] * 2 + [pltpu.SemaphoreType.DMA((2, nz))],
+            [pltpu.VMEM(block, F32)] * 2 + [pltpu.SemaphoreType.DMA((2, nz, len(starts)))],
             out_space=HBM,
         )(gathered, p, w, q, qo, v, vo, b)
     )

time: 70.6 us -> 70.3 us (level)
  waiting for transfers between devices: 8.41 us -> 9.16 us
    ppermute x11, waiting for transfers between devices: 3.74 us -> 4.49 us  [swap(): lax.ppermute(value, axis, [(i, partner(i) % size) for i in range(size)])]
where the time goes in v5:
time: 70.3 us; the launch traced here: 70.2 us
  blocking collectives  27.4 us (39%)
  starting transfers between devices  21.4 us (30%)
  Pallas kernels  9.79 us (14%)
  waiting for transfers between devices  9.16 us (13%)
  local copies, waits for them, and re-layouts  1.32 us (2%)
  between operations  0.96 us (1%)
    all_to_all x1, blocking collectives, local(): lax.all_to_all(jnp.broadcast_to(dots, (count, 128)), ALL, 0, 0, tiled=True)  27.4 us
    ppermute x3, starting transfers between devices, across(): lax.ppermute(value, ALL, [(i * parts + j, k * parts + m) for i, j, k, m i...  11.2 us
    ppermute x11, starting transfers between devices, swap(): lax.ppermute(value, axis, [(i, partner(i) % size) for i in range(size)])  10.2 us
    ppermute x3, waiting for transfers between devices, across(): lax.ppermute(value, ALL, [(i * parts + j, k * parts + m) for i, j, k, m i...  4.68 us
    ppermute x11, waiting for transfers between devices, swap(): lax.ppermute(value, axis, [(i, partner(i) % size) for i in range(size)])  4.49 us
    pallas_call x1, Pallas kernels, local(): call(inner_last, [block, block, (1, 128)], places + [VMEM] * 8, field)  1.85 us
    pallas_call x1, Pallas kernels, local(): call(faces, [block, block, (nz, ny + 8, nx), (nz - 1, ny, nx), block, (nz...  1.82 us
    pallas_call x1, Pallas kernels, local(): call(inner_first, [block, block, middle_shape, *rows, (1, 128)], places +...  1.78 us
  transfers between devices with their start and end apart: 14, of which 6 were waited for; matrix products, arithmetic and copies ran while one was open for 0% of the time, Pallas kernels for 9%

profile of v5, /device:TPU:1, one launch (start us, length us, event | category | flops | bytes accessed | tf_op | source)
XLA Modules:
  0.0 70.2 jit_solution(8157905541817919842)
XLA Ops:
  0.6 1.2 %copy-done.1 = s32[4,128,512]{2,1,0:T(8,128)S(1)} copy-done((s32[4,128,512]{2,1,0:T(8,128)S(1)}, s32[4,128,512]{2,1,0:T(8,128)}, u32[]{:S(2)}) %copy-start.1) | copy-done | bytes 1048600
  1.9 3.1 %collective-permute-start.3 = (s32[1,128,512]{2,1,0:T(8,128)S(1)}, s32[1,128,512]{2,1,0:T(8,128)S(1)}, u32[]{:S(2)}, u32[]{:S(2)}) collective-permute-start(s32[1,128,512]{2,1,0:T(8,128)S(1)} %shard_map.97), channel_id=1, source_target_pairs={{0,1},{1,0},{2,3},{3,2},{4,8},{5,9},{6,10},{7,11},{8,4},{9,5},{10,... | collective-permute-start | bytes 786440 | tf_op jit(solution)/shard_map/ppermute | solution.py:128
  5.0 0.1 shard_map.96
  5.2 0.3 collective-permute-start.2
  5.5 1.7 %collective-permute-start = (s32[4,512]{1,0:T(4,128)S(1)}, s32[4,512]{1,0:T(4,128)S(1)}, u32[]{:S(2)}, u32[]{:S(2)}) collective-permute-start(s32[4,512]{1,0:T(4,128)S(1)} %get-tuple-element.53), channel_id=1, source_target_pairs={{0,1},{1,0},{2,3},{3,2},{4,5},{5,4},{6,7},{7,6},{8,9},{9,8},{10,11... | collective-permute-start | bytes 24584 | tf_op jit(solution)/shard_map/ppermute | solution.py:118
  7.2 1.3 %collective-permute-start.1 = (s32[4,512]{1,0:T(4,128)S(1)}, s32[4,512]{1,0:T(4,128)S(1)}, u32[]{:S(2)}, u32[]{:S(2)}) collective-permute-start(s32[4,512]{1,0:T(4,128)S(1)} %get-tuple-element.54), channel_id=1, source_target_pairs={{0,3},{1,2},{2,1},{3,0},{4,7},{5,6},{6,5},{7,4},{8,11},{9,10},{10,... | collective-permute-start | bytes 24584 | tf_op jit(solution)/shard_map/ppermute | solution.py:118
  8.6 1.8 %shard_map.95 = (f32[4,128,512]{2,1,0:T(8,128)S(1)}, f32[4,128,512]{2,1,0:T(8,128)S(1)}, f32[4,136,512]{2,1,0:T(8,128)S(1)}, f32[3,128,512]{2,1,0:T(8,128)S(1)},...) custom-call(s32[4,128,512]{2,1,0:T(8,128)S(1)} %copy-done.1, ...), custom_call_target="tpu_custom_call" | custom-call | tf_op jit(solution)/shard_map/pallas_call | solution.py:216
  10.5 0.5 collective-permute-done.1.y_three
  11.0 0.6 shard_map.98
  11.7 1.6 %collective-permute-start.6 = (f32[8,512]{1,0:T(8,128)S(1)}, f32[8,512]{1,0:T(8,128)S(1)}, u32[]{:S(2)}, u32[]{:S(2)}) collective-permute-start(f32[8,512]{1,0:T(8,128)S(1)} %get-tuple-element.65), channel_id=1, source_target_pairs={{0,3},{1,2},{2,1},{3,0},{4,7},{5,6},{6,5},{7,4},{8,11},{9,10},{10,... | collective-permute-start | bytes 49160 | tf_op jit(solution)/shard_map/ppermute | solution.py:118
  13.3 1.6 %collective-permute-start.5 = (f32[4,512]{1,0:T(4,128)S(1)}, f32[4,512]{1,0:T(4,128)S(1)}, u32[]{:S(2)}, u32[]{:S(2)}) collective-permute-start(f32[4,512]{1,0:T(4,128)S(1)} %get-tuple-element.64), channel_id=1, source_target_pairs={{0,2},{1,3},{2,0},{3,1},{4,6},{5,7},{6,4},{7,5},{8,10},{9,11},{10,... | collective-permute-start | bytes 24584 | tf_op jit(solution)/shard_map/ppermute | solution.py:118
  14.9 0.5 shard_map.99.part
  15.4 1.9 %collective-permute-done.5.two = f32[4,512]{1,0:T(4,128)S(1)} collective-permute-done((f32[4,512]{1,0:T(4,128)S(1)}, f32[4,512]{1,0:T(4,128)S(1)}, u32[]{:S(2)}, u32[]{:S(2)}) %collective-permute-start.5) | collective-permute-done | bytes 8224 | tf_op jit(solution)/shard_map/ppermute | solution.py:118
  17.3 0.1 shard_map.101
  17.4 4.7 %collective-permute-start.8 = (f32[1,128,512]{2,1,0:T(8,128)S(1)}, f32[1,128,512]{2,1,0:T(8,128)S(1)}, u32[]{:S(2)}, u32[]{:S(2)}) collective-permute-start(f32[1,128,512]{2,1,0:T(8,128)S(1)} %get-tuple-element.79), channel_id=1, source_target_pairs={{0,1},{1,0},{2,3},{3,2},{4,8},{5,9},{6,10},{7,11},{8,4},{9,5},{10,... | collective-permute-start | bytes 786440 | tf_op jit(solution)/shard_map/ppermute | solution.py:128
  22.1 0.1 shard_map.102
  22.3 1.8 %shard_map.103 = (f32[4,128,512]{2,1,0:T(8,128)S(1)}, f32[4,128,512]{2,1,0:T(8,128)S(1)}, f32[2,128,512]{2,1,0:T(8,128)S(1)}, f32[4,512]{1,0:T(4,128)S(1)}, f32[...) custom-call(f32[4,128,512]{2,1,0:T(8,128)S(1)} %shard_map.99.part, ...), custom_call_target="tpu_custom_call" | custom-call | tf_op jit(solution)/shard_map/pallas_call | solution.py:502
  24.0 2.4 %collective-permute-done.8.z_out = f32[1,128,512]{2,1,0:T(8,128)S(1)} collective-permute-done((f32[1,128,512]{2,1,0:T(8,128)S(1)}, f32[1,128,512]{2,1,0:T(8,128)S(1)}, u32[]{:S(2)}, u32[]{:S(2)}) %collective-permute-start.8) | collective-permute-done | bytes 262176 | tf_op jit(solution)/shard_map/ppermute | solution.py:128
  26.4 0.4 shard_map.104
  26.8 1.1 %collective-permute-start.9 = (f32[4,512]{1,0:T(4,128)S(1)}, f32[4,512]{1,0:T(4,128)S(1)}, u32[]{:S(2)}, u32[]{:S(2)}) collective-permute-start(f32[4,512]{1,0:T(4,128)S(1)} %get-tuple-element.86), channel_id=1, source_target_pairs={{0,1},{1,0},{2,3},{3,2},{4,5},{5,4},{6,7},{7,6},{8,9},{9,8},{10,11... | collective-permute-start | bytes 24584 | tf_op jit(solution)/shard_map/ppermute | solution.py:118
  28.0 0.8 %collective-permute-start.11 = (f32[4,512]{1,0:T(4,128)S(1)}, f32[4,512]{1,0:T(4,128)S(1)}, u32[]{:S(2)}, u32[]{:S(2)}) collective-permute-start(f32[4,512]{1,0:T(4,128)S(1)} %get-tuple-element.88), channel_id=1, source_target_pairs={{0,3},{1,2},{2,1},{3,0},{4,7},{5,6},{6,5},{7,4},{8,11},{9,10},{10,... | collective-permute-start | bytes 24584 | tf_op jit(solution)/shard_map/ppermute | solution.py:118
  28.7 1.4 %collective-permute-start.10 = (f32[4,512]{1,0:T(4,128)S(1)}, f32[4,512]{1,0:T(4,128)S(1)}, u32[]{:S(2)}, u32[]{:S(2)}) collective-permute-start(f32[4,512]{1,0:T(4,128)S(1)} %get-tuple-element.87), channel_id=1, source_target_pairs={{0,2},{1,3},{2,0},{3,1},{4,6},{5,7},{6,4},{7,5},{8,10},{9,11},{10,... | collective-permute-start | bytes 24584 | tf_op jit(solution)/shard_map/ppermute | solution.py:118
  30.2 0.5 shard_map.105.part
  30.6 1.0 %collective-permute-done.11.three = f32[4,512]{1,0:T(4,128)S(1)} collective-permute-done((f32[4,512]{1,0:T(4,128)S(1)}, f32[4,512]{1,0:T(4,128)S(1)}, u32[]{:S(2)}, u32[]{:S(2)}) %collective-permute-start.11) | collective-permute-done | bytes 8224 | tf_op jit(solution)/shard_map/ppermute | solution.py:118
  31.7 1.1 %collective-permute-done.10.two = f32[4,512]{1,0:T(4,128)S(1)} collective-permute-done((f32[4,512]{1,0:T(4,128)S(1)}, f32[4,512]{1,0:T(4,128)S(1)}, u32[]{:S(2)}, u32[]{:S(2)}) %collective-permute-start.10) | collective-permute-done | bytes 8224 | tf_op jit(solution)/shard_map/ppermute | solution.py:118
  32.8 3.4 %collective-permute-start.13 = (f32[1,128,512]{2,1,0:T(8,128)S(1)}, f32[1,128,512]{2,1,0:T(8,128)S(1)}, u32[]{:S(2)}, u32[]{:S(2)}) collective-permute-start(f32[1,128,512]{2,1,0:T(8,128)S(1)} %get-tuple-element.95), channel_id=1, source_target_pairs={{0,1},{1,0},{2,3},{3,2},{4,8},{5,9},{6,10},{7,11},{8,4},{9,5},{10,... | collective-permute-start | bytes 786440 | tf_op jit(solution)/shard_map/ppermute | solution.py:128
  36.2 0.1 shard_map.108
  36.4 1.9 %shard_map.109 = (f32[4,128,512]{2,1,0:T(8,128)S(1)}, f32[4,128,512]{2,1,0:T(8,128)S(1)}, f32[1,128]{1,0:T(1,128)S(1)}) custom-call(f32[4,128,512]{2,1,0:T(8,128)S(1)} %shard_map.105.part, f32[4,128,512]{2,1,0:T(8,128)S(1)} %get-tuple-element.60.s, f32[2,128,512]{2,1,0:T(8,128)S(1)} %get-tuple-element.82.xo, f32[2,128,512]{2,1,0:T(8,128)S(1)} %get-tuple-element.83.xm, ...), custom_call_target="tpu_custom_call" | custom-call | tf_op jit(solution)/shard_map/pallas_call | solution.py:509
  38.3 2.3 %collective-permute-done.13.z_out = f32[1,128,512]{2,1,0:T(8,128)S(1)} collective-permute-done((f32[1,128,512]{2,1,0:T(8,128)S(1)}, f32[1,128,512]{2,1,0:T(8,128)S(1)}, u32[]{:S(2)}, u32[]{:S(2)}) %collective-permute-start.13) | collective-permute-done | bytes 262176 | tf_op jit(solution)/shard_map/ppermute | solution.py:128
  40.6 0.3 shard_map.110
  41.0 27.4 %all_to_all.8 = f32[256,1,128]{2,1,0:T(1,128)S(1)} all-to-all(f32[256,1,128]{2,1,0:T(1,128)S(1)} %broadcast_in_dim.9), channel_id=1, replica_groups=mesh['gz'=64,'gy'=4] {'gz','gy'}, dimensions={0} | all-to-all | bytes 262144 | tf_op jit(solution)/shard_map/all_to_all | solution.py:514
  68.4 1.6 %shard_map.111 = (f32[4,128,512]{2,1,0:T(8,128)}, f32[4,128,512]{2,1,0:T(8,128)}) custom-call(f32[256,128]{1,0:T(8,128)S(1)} %bitcast.5, f32[4,128,512]{2,1,0:T(8,128)S(1)} %get-tuple-element.73.p, f32[4,128,512]{2,1,0:T(8,128)S(1)} %get-tuple-element.92.w, f32[4,128,512]{2,1,0:T(8,128)S(1)} %get-tuple-element.74.q, ...), custom_call_target="tpu_custom_call" | custom-call | tf_op jit(solution)/shard_map/pallas_call | solution.py:516
  (34 shorter events, 0.6 us)
Async XLA Ops:
  0.6 1.2 %copy-start.1 = (s32[4,128,512]{2,1,0:T(8,128)S(1)}, s32[4,128,512]{2,1,0:T(8,128)}, u32[]{:S(2)}) copy-start(s32[4,128,512]{2,1,0:T(8,128)} %labels.5) | copy-start | bytes 3145732
  1.9 6.7 %copy-start.5 = (s32[2,4,128]{2,1,0:T(4,128)S(1)}, s32[2,4,128]{2,1,0:T(4,128)}, u32[]{:S(2)}) copy-start(s32[2,4,128]{2,1,0:T(4,128)} %param.10) | copy-start | bytes 12292
  1.9 6.7 %copy-start.6 = (f32[2]{0:T(128)S(1)}, f32[2]{0:T(128)}, u32[]{:S(2)}) copy-start(f32[2]{0:T(128)} %param.11) | copy-start | bytes 28
  1.9 6.7 %copy-start.7 = (f32[4]{0:T(128)S(1)}, f32[4]{0:T(128)}, u32[]{:S(2)}) copy-start(f32[4]{0:T(128)} %param.9) | copy-start | bytes 52
  1.9 6.8 %copy-start.3 = (f32[4,128,512]{2,1,0:T(8,128)S(1)}, f32[4,128,512]{2,1,0:T(8,128)}, u32[]{:S(2)}) copy-start(f32[4,128,512]{2,1,0:T(8,128)} %source.1) | copy-start | bytes 3145732
  1.9 9.0 %collective-permute-start.3 = (s32[1,128,512]{2,1,0:T(8,128)S(1)}, s32[1,128,512]{2,1,0:T(8,128)S(1)}, u32[]{:S(2)}, u32[]{:S(2)}) collective-permute-start(s32[1,128,512]{2,1,0:T(8,128)S(1)} %shard_map.97), channel_id=1, source_target_pairs={{0,1},{1,0},{2,3},{3,2},{4,8},{5,9},{6,10},{7,11},{8,4},{9,5},{10,... | collective-permute-start | bytes 786440 | tf_op jit(solution)/shard_map/ppermute | solution.py:128
  5.1 5.8 %copy-start = (f32[4,4,128,128]{3,2,1,0:T(8,128)S(1)}, f32[4,4,128,128]{3,2,1,0:T(8,128)}, u32[]{:S(2)}) copy-start(f32[4,4,128,128]{3,2,1,0:T(8,128)} %constant.10.clone.vectors) | copy-start | bytes 3145732
  5.2 5.8 %collective-permute-start.2 = (s32[1,128,512]{2,1,0:T(8,128)S(1)}, s32[1,128,512]{2,1,0:T(8,128)S(1)}, u32[]{:S(2)}, u32[]{:S(2)}) collective-permute-start(s32[1,128,512]{2,1,0:T(8,128)S(1)} %get-tuple-element.55), channel_id=1, source_target_pairs={{0,4},{4,0},{8,12},{12,8},{16,20},{20,16},{24,28},{28,24},{32,36},... | collective-permute-start | bytes 786440 | tf_op jit(solution)/shard_map/ppermute | solution.py:118
  5.5 5.0 %collective-permute-start = (s32[4,512]{1,0:T(4,128)S(1)}, s32[4,512]{1,0:T(4,128)S(1)}, u32[]{:S(2)}, u32[]{:S(2)}) collective-permute-start(s32[4,512]{1,0:T(4,128)S(1)} %get-tuple-element.53), channel_id=1, source_target_pairs={{0,1},{1,0},{2,3},{3,2},{4,5},{5,4},{6,7},{7,6},{8,9},{9,8},{10,11... | collective-permute-start | bytes 24584 | tf_op jit(solution)/shard_map/ppermute | solution.py:118
  7.2 3.7 %collective-permute-start.1 = (s32[4,512]{1,0:T(4,128)S(1)}, s32[4,512]{1,0:T(4,128)S(1)}, u32[]{:S(2)}, u32[]{:S(2)}) collective-permute-start(s32[4,512]{1,0:T(4,128)S(1)} %get-tuple-element.54), channel_id=1, source_target_pairs={{0,3},{1,2},{2,1},{3,0},{4,7},{5,6},{6,5},{7,4},{8,11},{9,10},{10,... | collective-permute-start | bytes 24584 | tf_op jit(solution)/shard_map/ppermute | solution.py:118
  10.9 4.0 %copy-start.2 = (bf16[4,128,384]{2,1,0:T(8,128)(2,1)S(1)}, bf16[4,128,384]{2,1,0:T(8,128)(2,1)}, u32[]{:S(2)}) copy-start(bf16[4,128,384]{2,1,0:T(8,128)(2,1)} %constant.9.clone.green) | copy-start | bytes 1179652
  11.6 5.7 %collective-permute-start.4 = (f32[8,512]{1,0:T(8,128)S(1)}, f32[8,512]{1,0:T(8,128)S(1)}, u32[]{:S(2)}, u32[]{:S(2)}) collective-permute-start(f32[8,512]{1,0:T(8,128)S(1)} %get-tuple-element.63), channel_id=1, source_target_pairs={{0,1},{1,0},{2,3},{3,2},{4,5},{5,4},{6,7},{7,6},{8,9},{9,8},{10,11... | collective-permute-start | bytes 49160 | tf_op jit(solution)/shard_map/ppermute | solution.py:118
  11.7 5.6 %collective-permute-start.6 = (f32[8,512]{1,0:T(8,128)S(1)}, f32[8,512]{1,0:T(8,128)S(1)}, u32[]{:S(2)}, u32[]{:S(2)}) collective-permute-start(f32[8,512]{1,0:T(8,128)S(1)} %get-tuple-element.65), channel_id=1, source_target_pairs={{0,3},{1,2},{2,1},{3,0},{4,7},{5,6},{6,5},{7,4},{8,11},{9,10},{10,... | collective-permute-start | bytes 49160 | tf_op jit(solution)/shard_map/ppermute | solution.py:118
  13.3 4.0 %collective-permute-start.5 = (f32[4,512]{1,0:T(4,128)S(1)}, f32[4,512]{1,0:T(4,128)S(1)}, u32[]{:S(2)}, u32[]{:S(2)}) collective-permute-start(f32[4,512]{1,0:T(4,128)S(1)} %get-tuple-element.64), channel_id=1, source_target_pairs={{0,2},{1,3},{2,0},{3,1},{4,6},{5,7},{6,4},{7,5},{8,10},{9,11},{10,... | collective-permute-start | bytes 24584 | tf_op jit(solution)/shard_map/ppermute | solution.py:118
  14.9 2.4 %copy-start.4 = (f32[4,8,128]{2,1,0:T(8,128)S(1)}, f32[4,8,128]{2,1,0:T(8,128)}, u32[]{:S(2)}) copy-start(f32[4,8,128]{2,1,0:T(8,128)} %constant.11.clone.scalars) | copy-start | bytes 49156
  17.4 9.0 %collective-permute-start.8 = (f32[1,128,512]{2,1,0:T(8,128)S(1)}, f32[1,128,512]{2,1,0:T(8,128)S(1)}, u32[]{:S(2)}, u32[]{:S(2)}) collective-permute-start(f32[1,128,512]{2,1,0:T(8,128)S(1)} %get-tuple-element.79), channel_id=1, source_target_pairs={{0,1},{1,0},{2,3},{3,2},{4,8},{5,9},{6,10},{7,11},{8,4},{9,5},{10,... | collective-permute-start | bytes 786440 | tf_op jit(solution)/shard_map/ppermute | solution.py:128
  22.2 4.3 %collective-permute-start.7 = (f32[1,128,512]{2,1,0:T(8,128)S(1)}, f32[1,128,512]{2,1,0:T(8,128)S(1)}, u32[]{:S(2)}, u32[]{:S(2)}) collective-permute-start(f32[1,128,512]{2,1,0:T(8,128)S(1)} %get-tuple-element.78), channel_id=1, source_target_pairs={{0,4},{4,0},{8,12},{12,8},{16,20},{20,16},{24,28},{28,24},{32,36},... | collective-permute-start | bytes 786440 | tf_op jit(solution)/shard_map/ppermute | solution.py:118
  26.8 3.8 %collective-permute-start.9 = (f32[4,512]{1,0:T(4,128)S(1)}, f32[4,512]{1,0:T(4,128)S(1)}, u32[]{:S(2)}, u32[]{:S(2)}) collective-permute-start(f32[4,512]{1,0:T(4,128)S(1)} %get-tuple-element.86), channel_id=1, source_target_pairs={{0,1},{1,0},{2,3},{3,2},{4,5},{5,4},{6,7},{7,6},{8,9},{9,8},{10,11... | collective-permute-start | bytes 24584 | tf_op jit(solution)/shard_map/ppermute | solution.py:118
  28.0 3.7 %collective-permute-start.11 = (f32[4,512]{1,0:T(4,128)S(1)}, f32[4,512]{1,0:T(4,128)S(1)}, u32[]{:S(2)}, u32[]{:S(2)}) collective-permute-start(f32[4,512]{1,0:T(4,128)S(1)} %get-tuple-element.88), channel_id=1, source_target_pairs={{0,3},{1,2},{2,1},{3,0},{4,7},{5,6},{6,5},{7,4},{8,11},{9,10},{10,... | collective-permute-start | bytes 24584 | tf_op jit(solution)/shard_map/ppermute | solution.py:118
  28.7 4.0 %collective-permute-start.10 = (f32[4,512]{1,0:T(4,128)S(1)}, f32[4,512]{1,0:T(4,128)S(1)}, u32[]{:S(2)}, u32[]{:S(2)}) collective-permute-start(f32[4,512]{1,0:T(4,128)S(1)} %get-tuple-element.87), channel_id=1, source_target_pairs={{0,2},{1,3},{2,0},{3,1},{4,6},{5,7},{6,4},{7,5},{8,10},{9,11},{10,... | collective-permute-start | bytes 24584 | tf_op jit(solution)/shard_map/ppermute | solution.py:118
  32.8 7.8 %collective-permute-start.13 = (f32[1,128,512]{2,1,0:T(8,128)S(1)}, f32[1,128,512]{2,1,0:T(8,128)S(1)}, u32[]{:S(2)}, u32[]{:S(2)}) collective-permute-start(f32[1,128,512]{2,1,0:T(8,128)S(1)} %get-tuple-element.95), channel_id=1, source_target_pairs={{0,1},{1,0},{2,3},{3,2},{4,8},{5,9},{6,10},{7,11},{8,4},{9,5},{10,... | collective-permute-start | bytes 786440 | tf_op jit(solution)/shard_map/ppermute | solution.py:128
  36.3 4.3 %collective-permute-start.12 = (f32[1,128,512]{2,1,0:T(8,128)S(1)}, f32[1,128,512]{2,1,0:T(8,128)S(1)}, u32[]{:S(2)}, u32[]{:S(2)}) collective-permute-start(f32[1,128,512]{2,1,0:T(8,128)S(1)} %get-tuple-element.94), channel_id=1, source_target_pairs={{0,4},{4,0},{8,12},{12,8},{16,20},{20,16},{24,28},{28,24},{32,36},... | collective-permute-start | bytes 786440 | tf_op jit(solution)/shard_map/ppermute | solution.py:118
